TPU v7x, 256 devices: a whole 4x4x8 slice. The times are simulated.
256 devices in a mesh: band: 64 (over x, z, core), wp: 4 (over y).
Axes of the slice: x: 4, y: 4, z: 8, core: 2. Of those that a mesh axis runs over, the one named last changes fastest.
Arguments:
- uv_tiles: bfloat16 [4, 4096, 2, 128, 128], P('wp', 'band'), may hold values from -6 to 6
- target_bands: int32 [4, 4096, 1], P('wp', 'band'), may hold values from 0 to 63; in each aligned block of 64 rows (0 to 63, 64 to 127, ..., all dimensions but the last counted through in order) at most 2 rows name the same one
- uv_offsets: int32 [4, 4096, 2], P('wp', 'band'), may hold values from 0 to 8064, as said below
- tile_counts: int32 [4, 64], P('wp', 'band'), may hold values from 48 to 64, as said below
- plane_w: float32 [4], P('wp'), may hold values from -8 to 8
Outputs:
- stacked_image: float32 [8192, 8192], P('wp', 'band')
Inputs may be any that keep to these rules, and one draw needn't show every extreme that they name: `target_bands`: among the 64 slots of one device no band is named more than 2 times. `uv_offsets`: the first entry is at most 0, the second at most 8064; both bounds are reached. `tile_counts`: some device uses all 64 slots.
All inputs are finite; a program needn't handle non-finite values.
Results may differ from a plain program's by a relative error of at most 0.0029.
Values may be sent and summed in bfloat16 or wider, within the bound.
No kernel may reach another device: no remote copies, remote signals or barrier semaphores. Data moves between devices by JAX's collectives and lax.ppermute only.
A program may use at most 128 MiB of HBM per device.

v0:
```python
import math

import jax
import jax.numpy as jnp
from jax import lax
from jax.sharding import PartitionSpec as P

N = 8192
F2 = 128


def dft_table(length):
    counter = jnp.arange(length, dtype=jnp.int32)
    turns = counter[:, None] * counter[None, :] % length
    angles = 2.0 * math.pi / length * turns.astype(jnp.float32)
    cosine = jnp.cos(angles)
    sine_part = jnp.sin(angles)
    return jnp.stack(
        [jnp.stack([cosine, -sine_part], axis=1), jnp.stack([sine_part, cosine], axis=1)], axis=0
    )


def twiddles(outer, inner, length):
    turns = (
        jnp.arange(outer, dtype=jnp.int32)[:, None]
        * jnp.arange(inner, dtype=jnp.int32)[None, :]
        % length
    )
    angles = 2.0 * math.pi / length * turns.astype(jnp.float32)
    return (jnp.cos(angles), jnp.sin(angles))


def rotate(section, cosine, sine_part):
    real_part = section[:, 0]
    imag_part = section[:, 1]
    return jnp.stack(
        [real_part * cosine - imag_part * sine_part, real_part * sine_part + imag_part * cosine],
        axis=1,
    )


def along_last(spectrum, table_low, table_high, cosine, sine_part):
    outer = table_low.shape[1]
    inner = table_high.shape[1]
    shaped = spectrum.reshape(spectrum.shape[:3] + (outer, inner))
    section_one = jnp.einsum(
        "pkqn,aqrnm->aprkm", table_low, shaped, precision=lax.Precision.HIGHEST
    )
    section_one = rotate(section_one, cosine, sine_part)
    section_two = jnp.einsum(
        "pjqm,aqrkm->aprjk", table_high, section_one, precision=lax.Precision.HIGHEST
    )
    return section_two.reshape(spectrum.shape)


def along_first(spectrum, table_low, table_high, cosine, sine_part):
    outer = table_low.shape[1]
    inner = table_high.shape[1]
    shaped = spectrum.reshape(spectrum.shape[:2] + (outer, inner, spectrum.shape[3]))
    section_one = jnp.einsum(
        "pkqn,aqnmc->apkmc", table_low, shaped, precision=lax.Precision.HIGHEST
    )
    section_one = rotate(section_one, cosine[:, :, None], sine_part[:, :, None])
    section_two = jnp.einsum(
        "pjqm,aqkmc->apjkc", table_high, section_one, precision=lax.Precision.HIGHEST
    )
    return section_two.reshape(spectrum.shape)


def local(uv_tiles, target_bands, uv_offsets, tile_counts, plane_w):
    band_count = lax.axis_size("band")
    tile_slots = uv_tiles.shape[1]
    tile_edge = uv_tiles.shape[3]
    capacity = max(2, 2 * tile_slots // band_count)
    slot_total = band_count * capacity
    band_rows = N // band_count
    plane_count = plane_w.shape[0]
    in_use = jnp.arange(tile_slots, dtype=jnp.int32) < tile_counts[0, 0]
    target = target_bands[0, :, 0]
    onehot = (
        (target[:, None] == jnp.arange(band_count, dtype=jnp.int32)[None, :]) & in_use[:, None]
    ).astype(jnp.int32)
    before = jnp.cumsum(onehot, axis=0) - onehot
    arrival = jnp.sum(before * onehot, axis=1)
    slot_index = target * capacity + arrival
    matches = (
        (slot_index[None, :] == jnp.arange(slot_total, dtype=jnp.int32)[:, None]) & in_use[None, :]
    ).astype(jnp.int32)
    source = jnp.sum(matches * jnp.arange(tile_slots, dtype=jnp.int32)[None, :], axis=1)
    filled = jnp.sum(matches, axis=1)
    packed = jnp.take(uv_tiles[0], source, axis=0) * filled[:, None, None, None].astype(
        jnp.bfloat16
    )
    places = jnp.stack([uv_offsets[0, :, 0], uv_offsets[0, :, 1]], axis=1)
    packed_places = jnp.take(places, source, axis=0) * filled[:, None]
    arrived = lax.all_to_all(packed, "band", split_axis=0, concat_axis=0, tiled=True)
    arrived_places = lax.all_to_all(packed_places, "band", split_axis=0, concat_axis=0, tiled=True)

    def add_tile(number, uv_grid):
        addend = arrived[number].astype(jnp.float32)[None]
        corner = (jnp.int32(0), jnp.int32(0), arrived_places[number, 0], arrived_places[number, 1])
        current = lax.dynamic_slice(uv_grid, corner, (1, 2, tile_edge, tile_edge))
        return lax.dynamic_update_slice(uv_grid, current + addend, corner)

    uv_grid = lax.fori_loop(
        0, slot_total, add_tile, jnp.zeros((plane_count, 2, band_rows, N), jnp.float32)
    )
    outer = N // F2
    table_low = dft_table(outer)
    table_high = dft_table(F2)
    cosine, sine_part = twiddles(outer, F2, N)
    spectrum = along_last(uv_grid, table_low, table_high, cosine, sine_part).astype(jnp.bfloat16)
    blocked = spectrum.reshape((plane_count, 2, band_rows, band_count, band_rows))
    columns = lax.all_to_all(blocked, "band", split_axis=3, concat_axis=2, tiled=True)
    flat = columns.reshape((plane_count, 2, N, columns.shape[4])).astype(jnp.float32)
    sky_blocks = along_first(flat, table_low, table_high, cosine, sine_part)[:, :, :, None, :]
    sky_image = sky_blocks.reshape((plane_count, 2, N, band_rows))
    column_start = lax.axis_index("band") * band_rows
    rows_axis = (jnp.arange(N, dtype=jnp.float32) - N // 2) / N
    cols_axis = (
        (column_start + jnp.arange(band_rows, dtype=jnp.int32)).astype(jnp.float32) - N // 2
    ) / N
    radius = rows_axis[:, None] ** 2 + cols_axis[None, :] ** 2
    w_term = -radius / (1.0 + jnp.sqrt(1.0 - radius))
    phase_angle = 2.0 * math.pi * plane_w[0] * w_term
    stacked = sky_image[0, 0] * jnp.cos(phase_angle) - sky_image[0, 1] * jnp.sin(phase_angle)
    stacked = stacked / N
    return lax.psum_scatter(stacked, "wp", scatter_dimension=0, tiled=True)


def solution(mesh):
    placed = (
        P("wp", "band", None, None, None),
        P("wp", "band", None),
        P("wp", "band", None),
        P("wp", "band"),
        P("wp"),
    )
    return jax.shard_map(
        local, mesh=mesh, in_specs=placed, out_specs=P("wp", "band"), check_vma=False
    )
```

profile of v0, /device:TPU:33, one launch (start us, length us, event | category | flops | bytes accessed | tf_op | source)
XLA Modules:
  0.0 1208.5 jit_solution(6153174239312586864)
XLA Ops:
  12.7 11.9 all-to-all-start
  24.6 8.6 gather_fusion.1
  33.2 7.5 select_multiply_fusion
  40.7 10.5 all-to-all-start.1
  52.4 183.5 %all-to-all-done.1 = bf16[128,2,128,128]{3,2,1,0:T(8,128)(2,1)} async-done(((bf16[128,2,128,128]{3,2,1,0:T(8,128)(2,1)}), bf16[128,2,128,128]{3,2,1,0:T(8,128)(2,1)}, u32[]{:S(2)}, u32[]{:S(2)}) %all-to-all-start.1) | async-done | bytes 8388640 | tf_op jit(solution)/shard_map/all_to_all | solution.py:96
  235.9 4.2 broadcast_in_dim.25
  240.1 682.0 %while.13 = (s32[]{:T(128)}, f32[1,2,128,8192]{3,2,1,0:T(8,128)}, s32[128,2]{0,1:T(2,128)S(1)}, bf16[128,2,128,128]{3,2,1,0:T(8,128)(2,1)}, s32[]{:T(128)}, /*index=5*/s32[]{:T(128)}, s32[]{:T(128)}) while((s32[]{:T(128)}, f32[1,2,128,8192]{3,2,1,0:T(8,128)}, s32[128,2]{0,1:T(2,128)S(1)}, bf16[128,2,128,128]{3,2,1,0:T(8,128)(2,1)}, s32[]{:T(128)}, ...), condition=%wide.region_5.6_spmd, body=%wide.region_4.5_spmd.sunk | while | flops 65541 | bytes 589959 | solution.py:105
  286.0 2.1 dynamic_update_slice.9
  296.8 2.1 dynamic_update_slice.9
  307.6 2.1 dynamic_update_slice.9
  318.4 2.0 dynamic_update_slice.9
  329.1 2.0 dynamic_update_slice.9
  339.9 2.1 dynamic_update_slice.9
  382.4 2.1 dynamic_update_slice.9
  393.1 2.1 dynamic_update_slice.9
  414.4 2.1 dynamic_update_slice.9
  435.6 2.1 dynamic_update_slice.9
  456.9 2.1 dynamic_update_slice.9
  478.1 2.1 dynamic_update_slice.9
  552.2 2.1 dynamic_update_slice.9
  573.5 2.1 dynamic_update_slice.9
  616.2 2.0 dynamic_update_slice.9
  627.0 2.1 dynamic_update_slice.9
  637.8 2.0 dynamic_update_slice.9
  659.0 2.1 dynamic_update_slice.9
  680.6 2.1 dynamic_update_slice.9
  691.3 2.1 dynamic_update_slice.9
  754.7 2.1 dynamic_update_slice.9
  765.5 2.0 dynamic_update_slice.9
  797.2 2.1 dynamic_update_slice.9
  850.7 2.1 dynamic_update_slice.9
  871.9 2.0 dynamic_update_slice.9
  893.5 2.1 dynamic_update_slice.9
  922.2 5.0 copy.63
  927.2 8.8 fusion.24
  936.0 3.5 multiply_subtract_fusion.1
  939.5 3.4 maximum_bitcast_fusion
  942.9 15.1 %fusion.10 = bf16[1,2,128,128,64]{2,3,1,4,0:T(8,128)(2,1)S(1)} fusion(f32[2,128,64,128,1]{3,2,0,1,4:T(8,128)S(1)} %maximum_bitcast_fusion, f32[1,128,2,128]{3,1,2,0:T(8,128)S(1)} %get-tuple-element.100, f32[1,128,2,128]{3,1,2,0:T(8,128)S(1)} %get-tuple-element.99), kind=kOutput, calls=%fused_computation.21 | convolution fusion | flops 6444613632 | bytes 12845056 | tf_op jit(solution)/shard_map/pjqm,aqrkm->aprjk/dot_general | solution.py:50
  958.0 4.7 copy.42
  962.7 11.1 copy.43
  973.8 31.0 %all-to-all-start.2 = ((bf16[1,2,128,64,128]{4,1,2,0,3:T(2,128)(2,1)}), bf16[1,2,128,64,128]{4,1,2,0,3:T(2,128)(2,1)}, u32[]{:S(2)}, u32[]{:S(2)}) async-start(bf16[1,2,128,64,128]{4,1,2,0,3:T(2,128)(2,1)} %copy.43), calls=%async_computation.2 | async-start | bytes 8388608 | tf_op jit(solution)/shard_map/all_to_all | solution.py:114
  1005.8 93.8 %all-to-all-done.2 = bf16[1,2,128,64,128]{4,1,2,0,3:T(2,128)(2,1)} async-done(((bf16[1,2,128,64,128]{4,1,2,0,3:T(2,128)(2,1)}), bf16[1,2,128,64,128]{4,1,2,0,3:T(2,128)(2,1)}, u32[]{:S(2)}, u32[]{:S(2)}) %all-to-all-start.2) | async-done | bytes 4194336 | tf_op jit(solution)/shard_map/all_to_all | solution.py:114
  1099.6 10.3 fusion.21
  1109.9 2.9 multiply_subtract_fusion
  1114.5 13.7 %fusion.18 = f32[1,2,128,64,128]{4,2,1,3,0:T(8,128)S(1)} fusion(f32[2,64,128,128,1]{3,1,0,2,4:T(8,128)S(1)} %maximum_bitcast_fusion.1, f32[1,128,2,128]{3,1,2,0:T(8,128)S(1)} %get-tuple-element.100, f32[1,128,2,128]{3,1,2,0:T(8,128)S(1)} %get-tuple-element.99), kind=kOutput, calls=%fused_computation.35 | convolution fusion | flops 6442516480 | bytes 17039360 | tf_op jit(solution)/shard_map/pjqm,aqkmc->apjkc/dot_general | solution.py:64
  1128.2 4.9 copy.48
  1133.1 20.5 %fusion.13 = f32[8192,128]{1,0:T(8,128)} fusion(f32[1,2,8192,128]{3,2,1,0:T(8,128)S(1)} %bitcast.116, f32[128]{0:T(128)S(1)} %multiply_multiply_fusion.1, f32[8192]{0:T(1024)S(1)} %multiply_multiply_fusion, f32[]{:T(128)} %bitcast.46), kind=kLoop, calls=%fused_computation.25 | loop fusion | flops 10485760 | bytes 12616196 | tf_op jit(solution)/shard_map/div | solution.py:127
  1153.7 47.7 %reduce-scatter.2.cloned.1.call-done = f32[2048,128]{1,0:T(8,128)} async-done(((f32[8192,128]{1,0:T(8,128)}), f32[2048,128]{1,0:T(8,128)}) %reduce-scatter.2.cloned.1.call-update) | async-done | bytes 1048592 | tf_op jit(solution)/shard_map/reduce_scatter | solution.py:128
  (394 shorter events, 402.4 us)
Async XLA Ops:
  12.7 28.0 %all-to-all-start = ((s32[64,2,2]{1,2,0:T(2,128)}), s32[64,2,2]{1,2,0:T(2,128)S(1)}, u32[]{:S(2)}, u32[]{:S(2)}) async-start(s32[64,2,2]{1,2,0:T(2,128)} %select_multiply_fusion.1), calls=%async_computation | async-start | bytes 131072 | tf_op jit(solution)/shard_map/all_to_all | solution.py:97
  40.7 195.2 %all-to-all-start.1 = ((bf16[128,2,128,128]{3,2,1,0:T(8,128)(2,1)}), bf16[128,2,128,128]{3,2,1,0:T(8,128)(2,1)}, u32[]{:S(2)}, u32[]{:S(2)}) async-start(bf16[128,2,128,128]{3,2,1,0:T(8,128)(2,1)} %select_multiply_fusion), calls=%async_computation.1 | async-start | bytes 16777216 | tf_op jit(solution)/shard_map/all_to_all | solution.py:96
  973.8 125.8 %all-to-all-start.2 = ((bf16[1,2,128,64,128]{4,1,2,0,3:T(2,128)(2,1)}), bf16[1,2,128,64,128]{4,1,2,0,3:T(2,128)(2,1)}, u32[]{:S(2)}, u32[]{:S(2)}) async-start(bf16[1,2,128,64,128]{4,1,2,0,3:T(2,128)(2,1)} %copy.43), calls=%async_computation.2 | async-start | bytes 8388608 | tf_op jit(solution)/shard_map/all_to_all | solution.py:114
  1004.8 196.6 %reduce-scatter.2.cloned.1.call-start = ((), (), s32[]{:S(2)}) async-start(), calls=%async_computation.4 | async-start | bytes 5242880 | tf_op jit(solution)/shard_map/reduce_scatter | solution.py:128
Sparse Core Ops, SparseCore 0:
  1153.8 47.5 reduce-scatter.1
where the time goes:
time: 1220 us; the launch traced here: 1210 us
  local copies, waits for them, and re-layouts  353 us (29%)
  waiting for transfers between devices  325 us (27%)
  loops' own time  235 us (19%)
  other arithmetic  179 us (15%)
  starting transfers between devices  53.5 us (4%)
  matrix products  48 us (4%)
  between operations  15.2 us (1%)
    another operation x1, loops' own time, local(): lax.fori_loop(0, slot_total, add_tile, jnp.zeros((plane_count, 2, band_ro...  235 us
    dynamic_update_slice x128, local copies, waits for them, and re-layouts, add_tile(): return lax.dynamic_update_slice(uv_grid, current + addend, corner)  234 us
    all_to_all x1, waiting for transfers between devices, local(): lax.all_to_all(packed, 'band', split_axis=0, concat_axis=0, tiled=True)  183 us
    add x128, other arithmetic, add_tile(): return lax.dynamic_update_slice(uv_grid, current + addend, corner)  136 us
    all_to_all x1, waiting for transfers between devices, local(): lax.all_to_all(blocked, 'band', split_axis=3, concat_axis=2, tiled=True)  93.8 us
    dynamic_slice x128, local copies, waits for them, and re-layouts, add_tile(): arrived_places[number, 1]  77.9 us
    reduce_scatter x1, waiting for transfers between devices, local(): return lax.psum_scatter(stacked, 'wp', scatter_dimension=0, tiled=True)  47.7 us
    all_to_all x1, starting transfers between devices, local(): lax.all_to_all(blocked, 'band', split_axis=3, concat_axis=2, tiled=True)  31 us
  transfers between devices with their start and end apart: 4, of which 3 were waited for; matrix products, arithmetic and copies ran while one was open for 1% of the time, Pallas kernels for 0%

commit v1 on v0

v1 whole, which is shorter than its diff:
```python
import functools
import math

import jax
import jax.numpy as jnp
import ml_dtypes
import numpy as np
from jax import lax
from jax.experimental import pallas as pl
from jax.experimental.pallas import tpu as pltpu
from jax.sharding import PartitionSpec as P

N = 8192
BANDS = 64
EDGE = 128
SLOTS = 64
HALF = 64
ROWS = 8192
F32 = jnp.float32
BF16 = jnp.bfloat16
VMEM_LIMIT = 56 * 1024 * 1024


def circle(numerator, length):
    angle = 2.0 * np.pi * (np.asarray(numerator) % length) / length
    return np.cos(angle), np.sin(angle)


def split(table):
    high = table.astype(ml_dtypes.bfloat16)
    low = (table - high.astype(np.float64)).astype(ml_dtypes.bfloat16)
    return high, low


def row_first_table():
    cosine, sine = circle(np.arange(64)[:, None] * np.arange(64)[None, :], 64)
    table = np.zeros((2, 64, 64, 2))
    table[0, :, :, 0] = cosine
    table[0, :, :, 1] = -sine
    table[1, :, :, 0] = sine
    table[1, :, :, 1] = cosine
    high, low = split(table.reshape(128, 128))
    return np.concatenate([high, high, low], axis=1)


def row_twiddles():
    cosine, sine = circle(np.arange(128)[:, None] * np.arange(128)[None, :], N)
    return np.stack([cosine, sine]).astype(np.float32)


def row_second_table():
    cosine, sine = circle(np.arange(64)[:, None] * np.arange(128)[None, :], 64)
    table = np.block([[cosine, -sine], [sine, cosine]])
    high, low = split(table)
    return np.concatenate([high, low], axis=0)


def column_first_table():
    rows = np.arange(128)[:, None, None]
    k = np.arange(64)[None, :, None]
    band = np.arange(64)[None, None, :]
    cosine, sine = circle(k * (128 * band + rows), N)
    table = np.concatenate(
        [np.concatenate([cosine, -sine], axis=2), np.concatenate([sine, cosine], axis=2)], axis=1
    )
    high, low = split(table)
    return np.concatenate([high, low], axis=2)


def column_second_table():
    cosine, sine = circle(np.arange(128)[:, None] * np.arange(128)[None, :], 128)
    table = np.zeros((2, 128, 2, 2, 64))
    cosine = cosine.reshape(128, 2, 64) / N
    sine = sine.reshape(128, 2, 64) / N
    table[0, :, :, 0] = cosine
    table[0, :, :, 1] = -sine
    table[1, :, :, 0] = sine
    table[1, :, :, 1] = cosine
    high, low = split(table.reshape(256, 256))
    return np.concatenate([high, high, low], axis=1)


def pack_kernel(shift_ref, used_ref, tiles_ref, out_ref, rows_ref, *, per_step):
    step = pl.program_id(0)

    def one(index, carry):
        slot = step * per_step + index
        shift = shift_ref[slot]
        keep = used_ref[slot] > 0
        for part in range(2):
            block = tiles_ref[index, part].astype(F32)
            block = jnp.where(keep, pltpu.roll(block, shift, 1), 0.0)
            rows_ref[pl.ds(slot * 2 + part, HALF, stride=128), :] = block
        return carry

    lax.fori_loop(0, per_step, one, 0, unroll=2)

    @pl.when(step == pl.num_programs(0) - 1)
    def _():
        def cast(index, carry):
            where = pl.ds(pl.multiple_of(index * 128, 128), 128)
            out_ref[where, :] = rows_ref[where, :].astype(BF16)
            return carry

        lax.fori_loop(0, ROWS // 128, cast, 0)


def pack(shift, used, tiles, half):
    per_step = 8
    return pl.pallas_call(
        functools.partial(pack_kernel, per_step=per_step),
        grid=(SLOTS // per_step,),
        in_specs=[
            pl.BlockSpec(memory_space=pltpu.SMEM),
            pl.BlockSpec(memory_space=pltpu.SMEM),
            pl.BlockSpec((per_step, 2, HALF, 128), lambda i: (i, 0, half, 0)),
        ],
        out_specs=pl.BlockSpec((ROWS, 128), lambda i: (0, 0)),
        out_shape=jax.ShapeDtypeStruct((ROWS, 128), BF16),
        scratch_shapes=[pltpu.VMEM((ROWS, 128), F32)],
        compiler_params=pltpu.CompilerParams(vmem_limit_bytes=VMEM_LIMIT),
        cost_estimate=pl.CostEstimate(flops=8 * 1024 * 1024, bytes_accessed=4 << 20, transcendentals=0),
        name="pack_rows",
    )(shift, used, tiles)


def grid_kernel(
    place_ref, pieces_ref, first_ref, twiddle_ref, second_ref, out_ref, grid_a, grid_b, rows_ref
):
    def clear(index, carry):
        where = pl.ds(pl.multiple_of(index * 64, 64), 64)
        grid_a[where, :] = jnp.zeros((64, 128), F32)
        grid_b[where, :] = jnp.zeros((64, 128), F32)
        return carry

    lax.fori_loop(0, ROWS // 64, clear, 0)
    grid_a[pl.ds(ROWS, 8), :] = jnp.zeros((8, 128), F32)
    grid_b[pl.ds(ROWS, 8), :] = jnp.zeros((8, 128), F32)

    sublane = lax.broadcasted_iota(jnp.int32, (8, 128), 0)
    lane = lax.broadcasted_iota(jnp.int32, (8, 128), 1)
    position = lane + (sublane // 2) * 128
    upper = sublane < 2

    def place(index, carry):
        pieces = pieces_ref[pl.ds(pl.multiple_of(index * 16, 16), 16), :].astype(F32)
        for part in range(2):
            block = pieces[8 * part : 8 * part + 8]
            turned = [block] + [pltpu.roll(block, 8 - 2 * turn, 0) for turn in (1, 2, 3)]
            for piece in range(4):
                both = jnp.where(upper, turned[piece], turned[(piece + 3) % 4])
                packed = place_ref[index * 8 + part * 4 + piece]
                shift = packed & 127
                row = packed >> 7
                offset = position - shift
                inside = (offset >= 0) & (offset < 128)
                grid = grid_a if piece % 2 == 0 else grid_b
                window = pl.ds(row, 8)
                grid[window, :] = grid[window, :] + jnp.where(inside, both, 0.0)
        return carry

    lax.fori_loop(0, BANDS * SLOTS // 8, place, 0)

    first = first_ref[...]
    second = second_ref[...]
    cosine = twiddle_ref[0]
    sine = twiddle_ref[1]

    def band_step(band, carry):
        where = pl.ds(pl.multiple_of(band * 128, 128), 128)
        cells = grid_a[where, :] + grid_b[where, :]
        high = cells.astype(BF16)
        low = (cells - high.astype(F32)).astype(BF16)
        section = jnp.dot(
            first, jnp.concatenate([high, low, high], axis=0), preferred_element_type=F32
        )
        real = jnp.concatenate([section[:64], section[:64]], axis=0)
        imag = jnp.concatenate([section[64:], section[64:]], axis=0)
        turned = jnp.concatenate(
            [real * cosine - imag * sine, real * sine + imag * cosine], axis=1
        )
        high = turned.astype(BF16)
        low = (turned - high.astype(F32)).astype(BF16)
        contract = (((1,), (1,)), ((), ()))
        main = lax.dot_general(second, high, contract, preferred_element_type=F32)
        rest = lax.dot_general(second[:128], low, contract, preferred_element_type=F32)
        spectrum = main[:128] + main[128:] + rest
        rows_ref[pl.ds(band, 64, stride=128), :] = spectrum[:64]
        rows_ref[pl.ds(64 + band, 64, stride=128), :] = spectrum[64:]
        return carry

    lax.fori_loop(0, BANDS, band_step, 0, unroll=2)

    def cast(index, carry):
        where = pl.ds(pl.multiple_of(index * 128, 128), 128)
        out_ref[where, :] = rows_ref[where, :].astype(BF16)
        return carry

    lax.fori_loop(0, ROWS // 128, cast, 0)


def grid_and_rows(places, pieces, first, twiddle, second):
    vmem = pl.BlockSpec(memory_space=pltpu.VMEM)
    return pl.pallas_call(
        grid_kernel,
        in_specs=[pl.BlockSpec(memory_space=pltpu.SMEM), vmem, vmem, vmem, vmem],
        out_specs=vmem,
        out_shape=jax.ShapeDtypeStruct((ROWS, 128), BF16),
        scratch_shapes=[
            pltpu.VMEM((ROWS + 8, 128), F32),
            pltpu.VMEM((ROWS + 8, 128), F32),
            pltpu.VMEM((ROWS, 128), F32),
        ],
        compiler_params=pltpu.CompilerParams(vmem_limit_bytes=VMEM_LIMIT),
        cost_estimate=pl.CostEstimate(flops=20_000_000_000, bytes_accessed=4 << 20, transcendentals=0),
        name="place_and_row_transform",
    )(places, pieces, first, twiddle, second)


def column_first_kernel(rows_ref, table_ref, out_ref):
    for index in range(rows_ref.shape[0]):
        source = pl.program_id(0) * rows_ref.shape[0] + index
        rows = rows_ref[index]
        section = jnp.dot(
            table_ref[index], jnp.concatenate([rows, rows], axis=0), preferred_element_type=F32
        )
        out_ref[pl.ds(source, 64, stride=128), :] = section[:64]
        out_ref[pl.ds(64 + source, 64, stride=128), :] = section[64:]


def column_first(rows, table, half):
    per_step = 8
    steps = 64 // per_step
    return pl.pallas_call(
        column_first_kernel,
        grid=(steps,),
        in_specs=[
            pl.BlockSpec((per_step, 128, 128), lambda i: (i, 0, 0)),
            pl.BlockSpec((per_step, 128, 256), lambda i: (i + half * steps, 0, 0)),
        ],
        out_specs=pl.BlockSpec((ROWS, 128), lambda i: (0, 0)),
        out_shape=jax.ShapeDtypeStruct((ROWS, 128), F32),
        compiler_params=pltpu.CompilerParams(vmem_limit_bytes=VMEM_LIMIT),
        cost_estimate=pl.CostEstimate(flops=2_000_000_000, bytes_accessed=10 << 20, transcendentals=0),
        name="column_transform_over_bands",
    )(rows, table)


def column_second_kernel(first_ref, later_ref, table_ref, cosine_ref, sine_ref, out_ref):
    table = table_ref[...]
    for index in range(first_ref.shape[0]):
        cells = jnp.concatenate([first_ref[index], later_ref[index]], axis=0)
        high = cells.astype(BF16)
        low = (cells - high.astype(F32)).astype(BF16)
        sky = jnp.dot(
            table, jnp.concatenate([high, low, high], axis=0), preferred_element_type=F32
        )
        image = sky[:128] * cosine_ref[index] - sky[128:] * sine_ref[index]
        out_ref[:, index] = image.astype(BF16).reshape(4, 32, 128)


def column_second(first, later, table, cosine, sine, part, parts):
    per_step = 8
    count = 64 // parts
    steps = count // per_step
    block = pl.BlockSpec((per_step, 128, 128), lambda i: (i + part * steps, 0, 0))
    return pl.pallas_call(
        column_second_kernel,
        grid=(steps,),
        in_specs=[block, block, pl.BlockSpec((256, 768), lambda i: (0, 0)), block, block],
        out_specs=pl.BlockSpec((4, per_step, 32, 128), lambda i: (0, i, 0, 0)),
        out_shape=jax.ShapeDtypeStruct((4, count, 32, 128), BF16),
        compiler_params=pltpu.CompilerParams(vmem_limit_bytes=VMEM_LIMIT),
        cost_estimate=pl.CostEstimate(
            flops=6_000_000_000 // parts, bytes_accessed=(18 << 20) // parts, transcendentals=0
        ),
        name="column_transform_over_rows",
    )(first, later, table, cosine, sine)


def sum_kernel(*refs):
    out_ref = refs[-1]
    parts = len(refs) - 1
    count = 64 // parts
    for part in range(parts):

        def one(k, carry):
            total = refs[part][0, k].astype(F32)
            for plane in range(1, 4):
                total = total + refs[part][plane, k].astype(F32)
            out_ref[pl.ds(part * count + k, 32, stride=64), :] = total
            return carry

        lax.fori_loop(0, count, one, 0, unroll=2)


def window_sum(blocks):
    vmem = pl.BlockSpec(memory_space=pltpu.VMEM)
    return pl.pallas_call(
        sum_kernel,
        in_specs=[vmem] * len(blocks),
        out_specs=vmem,
        out_shape=jax.ShapeDtypeStruct((2048, 128), F32),
        compiler_params=pltpu.CompilerParams(vmem_limit_bytes=VMEM_LIMIT),
        cost_estimate=pl.CostEstimate(flops=1 << 20, bytes_accessed=3 << 20, transcendentals=0),
        name="window_sum",
    )(*blocks)


def w_phases(plane_w):
    k = jnp.arange(64, dtype=jnp.int32)[:, None, None]
    j = jnp.arange(128, dtype=jnp.int32)[None, :, None]
    column = lax.axis_index("band") * 128 + jnp.arange(128, dtype=jnp.int32)[None, None, :]
    x = ((64 * j + k).astype(F32) - N // 2) / N
    y = (column.astype(F32) - N // 2) / N
    radius = x**2 + y**2
    angle = 2.0 * math.pi * plane_w * (jnp.sqrt(1.0 - radius) - 1.0)
    return jnp.cos(angle), jnp.sin(angle)


def local(uv_tiles, target_bands, uv_offsets, tile_counts, plane_w):
    tiles = uv_tiles[0]
    used = (jnp.arange(SLOTS, dtype=jnp.int32) < tile_counts[0, 0]).astype(jnp.int32)
    column = uv_offsets[0, :, 1]
    shift = column % 128
    row = (target_bands[0, :, 0] * 64 + column // 128) * 2
    places = lax.all_gather(row * 128 + shift, "band", axis=0, tiled=True)

    first = jnp.asarray(row_first_table())
    twiddle = jnp.asarray(row_twiddles())
    second = jnp.asarray(row_second_table())
    column_table = jnp.asarray(column_first_table())
    last_table = jnp.asarray(column_second_table())

    sections = []
    for half in range(2):
        packed = pack(shift, used, tiles, half)
        arrived = lax.all_to_all(
            packed.reshape(64, 128, 128), "band", split_axis=0, concat_axis=0, tiled=True
        )
        spectrum = grid_and_rows(places, arrived.reshape(ROWS, 128), first, twiddle, second)
        columns = lax.all_to_all(
            spectrum.reshape(64, 128, 128), "band", split_axis=0, concat_axis=0, tiled=True
        )
        sections.append(column_first(columns, column_table, half).reshape(64, 128, 128))

    cosine, sine = w_phases(plane_w[0])
    parts = 2
    blocks = []
    for part in range(parts):
        image = column_second(sections[0], sections[1], last_table, cosine, sine, part, parts)
        blocks.append(lax.all_to_all(image, "wp", split_axis=0, concat_axis=0, tiled=True))
    return window_sum(blocks)


def solution(mesh):
    placed = (
        P("wp", "band", None, None, None),
        P("wp", "band", None),
        P("wp", "band", None),
        P("wp", "band"),
        P("wp"),
    )
    return jax.shard_map(
        local, mesh=mesh, in_specs=placed, out_specs=P("wp", "band"), check_vma=False
    )
```

time: 1220 us -> 589 us (0.48)
  local copies, waits for them, and re-layouts: 353 us -> 3.93 us
  blocking collectives: 0 us -> 295 us
  waiting for transfers between devices: 325 us -> 76.7 us
  loops' own time: 235 us -> 0 us
  other arithmetic: 179 us -> 20.2 us
  Pallas kernels: 0 us -> 141 us
  matrix products: 48 us -> 0 us
  between operations: 15.2 us -> 2.03 us
    unnamed x0 -> x1, blocking collectives: none -> 277 us
    another operation x1 -> x0, loops' own time: 235 us -> none  [local(): lax.fori_loop(0, slot_total, add_tile, jnp.zeros((plane_count, 2, band_ro...]
    dynamic_update_slice x128 -> x0, local copies, waits for them, and re-layouts: 234 us -> none  [add_tile(): return lax.dynamic_update_slice(uv_grid, current + addend, corner)]
    all_to_all x3 -> x5, waiting for transfers between devices: 277 us -> 76.7 us  [the longest x2 40.2 us: local(): lax.all_to_all(packed.reshape(64, 128, 128), 'band', split_axis=0, concat...]
    pallas_call x0 -> x9, Pallas kernels: none -> 141 us  [the longest x2 84.6 us: grid_and_rows(): pl.pallas_call(grid_kernel, in_specs=[pl.BlockSpec(memory_space=pltpu.SME...]
    add x129 -> x0, other arithmetic: 136 us -> none  [the longest x128 136 us: add_tile(): return lax.dynamic_update_slice(uv_grid, current + addend, corner)]
    dynamic_slice x128 -> x0, local copies, waits for them, and re-layouts: 77.9 us -> none  [add_tile(): arrived_places[number, 1]]
    dot_general x4 -> x0, matrix products: 48 us -> none  [the longest x1 15.1 us: along_last(): jnp.einsum('pjqm,aqrkm->aprjk', table_high, section_one, precision=lax.Pr...]
  transfers between devices with their start and end apart: 4 -> 5, of which waited for: 3 -> 4; matrix products, arithmetic and copies ran while one was open for 1% -> 3% of each run, Pallas kernels for 0% -> 19%
where the time goes in v1:
time: 589 us; the launch traced here: 584 us
  blocking collectives  295 us (50%)
  Pallas kernels  141 us (24%)
  waiting for transfers between devices  76.7 us (13%)
  starting transfers between devices  45.6 us (8%)
  other arithmetic  20.2 us (3%)
    unnamed x1, blocking collectives  277 us
    pallas_call x2, Pallas kernels, grid_and_rows(): pl.pallas_call(grid_kernel, in_specs=[pl.BlockSpec(memory_space=pltpu.SME...  84.6 us
    all_to_all x2, waiting for transfers between devices, local(): lax.all_to_all(packed.reshape(64, 128, 128), 'band', split_axis=0, concat...  40.2 us
    all_to_all x2, waiting for transfers between devices, local(): lax.all_to_all(spectrum.reshape(64, 128, 128), 'band', split_axis=0, conc...  29 us
    all_to_all x2, starting transfers between devices, local(): lax.all_to_all(spectrum.reshape(64, 128, 128), 'band', split_axis=0, conc...  22.4 us
    pallas_call x2, Pallas kernels, pack(): pl.pallas_call(functools.partial(pack_kernel, per_step=per_step), grid=(S...  19.3 us
    all_to_all x2, starting transfers between devices, local(): lax.all_to_all(packed.reshape(64, 128, 128), 'band', split_axis=0, concat...  19 us
    pallas_call x2, Pallas kernels, column_first(): pl.pallas_call(column_first_kernel, grid=(steps,), in_specs=[pl.BlockSpec...  18.8 us
  transfers between devices with their start and end apart: 5, of which 4 were waited for; matrix products, arithmetic and copies ran while one was open for 3% of the time, Pallas kernels for 19%

profile of v1, /device:TPU:33, one launch (start us, length us, event | category | flops | bytes accessed | tf_op | source)
XLA Modules:
  0.0 584.0 jit_solution(9702905281497460434)
XLA Ops:
  0.7 0.5 compare_convert_fusion.used_ref
  1.1 1.3 dynamic-slice
  3.1 1.3 and_select_fusion
  4.3 9.7 %pack_rows.3 = bf16[8192,128]{1,0:T(8,128)(2,1)} custom-call(s32[64]{0:T(128)} %get-tuple-element.7.shift_ref, s32[64]{0:T(128)} %compare_convert_fusion.used_ref, bf16[64,2,128,128]{3,2,1,0:T(8,128)(2,1)} %bitcast.42), custom_call_target="tpu_custom_call" | custom-call | flops 8388608 | bytes 4194304 | tf_op jit(solution)/shard_map/pack_rows/pallas_call | solution.py:110
  14.0 11.9 %all-to-all-start.2 = ((bf16[64,128,128]{2,1,0:T(8,128)(2,1)}), bf16[64,128,128]{2,1,0:T(8,128)(2,1)S(1)}, u32[]{:S(2)}, u32[]{:S(2)}) async-start(bf16[64,128,128]{2,1,0:T(8,128)(2,1)} %bitcast.45), calls=%async_computation.2 | async-start | bytes 4194304 | tf_op jit(solution)/shard_map/all_to_all | solution.py:338
  25.9 9.7 %pack_rows.2 = bf16[8192,128]{1,0:T(8,128)(2,1)} custom-call(s32[64]{0:T(128)} %get-tuple-element.7.shift_ref, s32[64]{0:T(128)} %compare_convert_fusion.used_ref, bf16[64,2,128,128]{3,2,1,0:T(8,128)(2,1)} %bitcast.43), custom_call_target="tpu_custom_call" | custom-call | flops 8388608 | bytes 4194304 | tf_op jit(solution)/shard_map/pack_rows/pallas_call | solution.py:110
  35.6 40.2 %all-to-all-done.2 = bf16[64,128,128]{2,1,0:T(8,128)(2,1)S(1)} async-done(((bf16[64,128,128]{2,1,0:T(8,128)(2,1)}), bf16[64,128,128]{2,1,0:T(8,128)(2,1)S(1)}, u32[]{:S(2)}, u32[]{:S(2)}) %all-to-all-start.2) | async-done | bytes 2097184 | tf_op jit(solution)/shard_map/all_to_all | solution.py:338
  75.8 0.0 copy-start.3
  75.8 1.3 copy-done.3
  77.2 7.1 %all-to-all-start = ((bf16[64,128,128]{2,1,0:T(8,128)(2,1)}), bf16[64,128,128]{2,1,0:T(8,128)(2,1)S(1)}, u32[]{:S(2)}, u32[]{:S(2)}) async-start(bf16[64,128,128]{2,1,0:T(8,128)(2,1)} %bitcast.44), calls=%async_computation | async-start | bytes 4194304 | tf_op jit(solution)/shard_map/all_to_all | solution.py:338
  84.3 276.7 %all-reduce.place_ref = s32[4096]{0:T(1024)} all-reduce(s32[4096]{0:T(1024)S(1)} %get-tuple-element.8), channel_id=1, replica_groups=mesh['band'=64,'wp'=4] {'band'}, use_global_device_ids=true, to_apply=%add | all-reduce | flops 4096 | bytes 32768
  361.0 42.3 %place_and_row_transform.3 = bf16[8192,128]{1,0:T(8,128)(2,1)} custom-call(s32[4096]{0:T(1024)} %all-reduce.place_ref, bf16[8192,128]{1,0:T(8,128)(2,1)} %bitcast.48, bf16[128,384]{1,0:T(8,128)(2,1)} %constant.68.clone.first_ref, f32[2,128,128]{2,1,0:T(8,128)} %constant.69.clone.twiddle_ref, bf16[256,256]{1,0:T(8,128)(2,1)} %constant.70.clone.second_ref), custom_call_target="tpu_custom_call" | custom-call | flops 20000000000 | bytes 4194304 | tf_op jit(solution)/shard_map/place_and_row_transform/pallas_call | solution.py:204
  403.3 0.0 all-to-all-done
  403.3 0.0 copy-start.2
  403.3 1.3 copy-done.2
  404.7 15.0 %all-to-all-start.3 = ((bf16[64,128,128]{2,1,0:T(8,128)(2,1)}), bf16[64,128,128]{2,1,0:T(8,128)(2,1)S(1)}, u32[]{:S(2)}, u32[]{:S(2)}) async-start(bf16[64,128,128]{2,1,0:T(8,128)(2,1)} %bitcast.49), calls=%async_computation.3 | async-start | bytes 4194304 | tf_op jit(solution)/shard_map/all_to_all | solution.py:342
  419.7 42.3 %place_and_row_transform.2 = bf16[8192,128]{1,0:T(8,128)(2,1)} custom-call(s32[4096]{0:T(1024)} %all-reduce.place_ref, bf16[8192,128]{1,0:T(8,128)(2,1)} %bitcast.47, bf16[128,384]{1,0:T(8,128)(2,1)} %constant.68.clone.first_ref, f32[2,128,128]{2,1,0:T(8,128)} %constant.69.clone.twiddle_ref, bf16[256,256]{1,0:T(8,128)(2,1)} %constant.70.clone.second_ref), custom_call_target="tpu_custom_call" | custom-call | flops 20000000000 | bytes 4194304 | tf_op jit(solution)/shard_map/place_and_row_transform/pallas_call | solution.py:204
  462.0 7.7 %all-to-all-done.3.rows_ref = bf16[64,128,128]{2,1,0:T(8,128)(2,1)S(1)} async-done(((bf16[64,128,128]{2,1,0:T(8,128)(2,1)}), bf16[64,128,128]{2,1,0:T(8,128)(2,1)S(1)}, u32[]{:S(2)}, u32[]{:S(2)}) %all-to-all-start.3) | async-done | bytes 2097184 | tf_op jit(solution)/shard_map/all_to_all | solution.py:342
  469.7 0.0 copy-start
  469.7 7.4 %all-to-all-start.1 = ((bf16[64,128,128]{2,1,0:T(8,128)(2,1)}), bf16[64,128,128]{2,1,0:T(8,128)(2,1)}, u32[]{:S(2)}, u32[]{:S(2)}) async-start(bf16[64,128,128]{2,1,0:T(8,128)(2,1)} %bitcast.46), calls=%async_computation.1 | async-start | bytes 4194304 | tf_op jit(solution)/shard_map/all_to_all | solution.py:342
  477.7 18.4 %fusion = (f32[64,128,128]{2,1,0:T(8,128)}, f32[64,128,128]{2,1,0:T(8,128)}) fusion(f32[128]{0:T(128)S(1)} %multiply_multiply_fusion.1, f32[64,128]{1,0:T(8,128)S(1)} %multiply_multiply_fusion, f32[]{:T(128)} %bitcast.13), kind=kLoop, calls=%fused_computation.1 | loop fusion | flops 4194304 | bytes 8421892 | tf_op jit(solution)/shard_map/sin | solution.py:318
  496.1 0.0 copy-done
  496.2 9.4 %column_transform_over_bands.3 = f32[8192,128]{1,0:T(8,128)} custom-call(bf16[64,128,128]{2,1,0:T(8,128)(2,1)} %copy-done, bf16[128,128,256]{2,1,0:T(8,128)(2,1)} %constant.71.clone.table_ref), custom_call_target="tpu_custom_call" | custom-call | flops 2000000000 | bytes 10485760 | tf_op jit(solution)/shard_map/column_transform_over_bands/pallas_call | solution.py:234
  505.6 21.3 %all-to-all-done.1.rows_ref = bf16[64,128,128]{2,1,0:T(8,128)(2,1)} async-done(((bf16[64,128,128]{2,1,0:T(8,128)(2,1)}), bf16[64,128,128]{2,1,0:T(8,128)(2,1)}, u32[]{:S(2)}, u32[]{:S(2)}) %all-to-all-start.1) | async-done | bytes 2097184 | tf_op jit(solution)/shard_map/all_to_all | solution.py:342
  526.9 9.4 %column_transform_over_bands.2 = f32[8192,128]{1,0:T(8,128)} custom-call(bf16[64,128,128]{2,1,0:T(8,128)(2,1)} %all-to-all-done.1.rows_ref, bf16[128,128,256]{2,1,0:T(8,128)(2,1)} %constant.71.clone.table_ref), custom_call_target="tpu_custom_call" | custom-call | flops 2000000000 | bytes 10485760 | tf_op jit(solution)/shard_map/column_transform_over_bands/pallas_call | solution.py:234
  536.3 7.4 %column_transform_over_rows.2 = bf16[4,32,32,128]{3,2,1,0:T(8,128)(2,1)} custom-call(f32[64,128,128]{2,1,0:T(8,128)} %bitcast.40, f32[64,128,128]{2,1,0:T(8,128)} %bitcast.38, bf16[256,768]{1,0:T(8,128)(2,1)} %constant.72.clone.table_ref, f32[64,128,128]{2,1,0:T(8,128)} %get-tuple-element.6.cosine_ref, f32[64,128,128]{2,1,0:T(8,128)} %get-tuple-element.5.sine_ref), custom_call_target="tpu_custom_call" | custom-call | flops 3000000000 | bytes 9437184 | tf_op jit(solution)/shard_map/column_transform_over_rows/pallas_call | solution.py:267
  543.7 4.2 all-to-all-start.4
  547.9 7.2 %column_transform_over_rows.3 = bf16[4,32,32,128]{3,2,1,0:T(8,128)(2,1)} custom-call(f32[64,128,128]{2,1,0:T(8,128)} %bitcast.41, f32[64,128,128]{2,1,0:T(8,128)} %bitcast.39, bf16[256,768]{1,0:T(8,128)(2,1)} %constant.72.clone.table_ref, f32[64,128,128]{2,1,0:T(8,128)} %get-tuple-element.6.cosine_ref, f32[64,128,128]{2,1,0:T(8,128)} %get-tuple-element.5.sine_ref), custom_call_target="tpu_custom_call" | custom-call | flops 3000000000 | bytes 9437184 | tf_op jit(solution)/shard_map/column_transform_over_rows/pallas_call | solution.py:267
  555.1 7.5 %all-to-all-done.4.refs_0_ = bf16[4,32,32,128]{3,2,1,0:T(8,128)(2,1)S(1)} async-done(((bf16[4,32,32,128]{3,2,1,0:T(8,128)(2,1)}), bf16[4,32,32,128]{3,2,1,0:T(8,128)(2,1)S(1)}, u32[]{:S(2)}, u32[]{:S(2)}) %all-to-all-start.4) | async-done | bytes 1048608 | tf_op jit(solution)/shard_map/all_to_all | solution.py:352
  562.5 0.0 copy-start.1
  562.5 17.8 %all_to_all.30.refs_1_ = bf16[4,32,32,128]{3,2,1,0:T(8,128)(2,1)} all-to-all(bf16[4,32,32,128]{3,2,1,0:T(8,128)(2,1)} %column_transform_over_rows.3), channel_id=1, replica_groups=mesh['band'=64,'wp'=4] {'wp'}, dimensions={0} | all-to-all | bytes 2097152 | tf_op jit(solution)/shard_map/all_to_all | solution.py:352
  580.3 0.0 copy-done.1
  580.3 3.6 window_sum.1
  (4 shorter events, 0.0 us)
Async XLA Ops:
  14.0 61.8 %all-to-all-start.2 = ((bf16[64,128,128]{2,1,0:T(8,128)(2,1)}), bf16[64,128,128]{2,1,0:T(8,128)(2,1)S(1)}, u32[]{:S(2)}, u32[]{:S(2)}) async-start(bf16[64,128,128]{2,1,0:T(8,128)(2,1)} %bitcast.45), calls=%async_computation.2 | async-start | bytes 4194304 | tf_op jit(solution)/shard_map/all_to_all | solution.py:338
  75.8 1.3 copy-start.3
  77.2 326.2 %all-to-all-start = ((bf16[64,128,128]{2,1,0:T(8,128)(2,1)}), bf16[64,128,128]{2,1,0:T(8,128)(2,1)S(1)}, u32[]{:S(2)}, u32[]{:S(2)}) async-start(bf16[64,128,128]{2,1,0:T(8,128)(2,1)} %bitcast.44), calls=%async_computation | async-start | bytes 4194304 | tf_op jit(solution)/shard_map/all_to_all | solution.py:338
  403.3 1.3 copy-start.2
  404.7 65.0 %all-to-all-start.3 = ((bf16[64,128,128]{2,1,0:T(8,128)(2,1)}), bf16[64,128,128]{2,1,0:T(8,128)(2,1)S(1)}, u32[]{:S(2)}, u32[]{:S(2)}) async-start(bf16[64,128,128]{2,1,0:T(8,128)(2,1)} %bitcast.49), calls=%async_computation.3 | async-start | bytes 4194304 | tf_op jit(solution)/shard_map/all_to_all | solution.py:342
  469.7 26.5 %copy-start = (bf16[64,128,128]{2,1,0:T(8,128)(2,1)}, bf16[64,128,128]{2,1,0:T(8,128)(2,1)S(1)}, u32[]{:S(2)}) copy-start(bf16[64,128,128]{2,1,0:T(8,128)(2,1)S(1)} %all-to-all-done.3.rows_ref) | copy-start | bytes 6291460
  469.7 57.2 %all-to-all-start.1 = ((bf16[64,128,128]{2,1,0:T(8,128)(2,1)}), bf16[64,128,128]{2,1,0:T(8,128)(2,1)}, u32[]{:S(2)}, u32[]{:S(2)}) async-start(bf16[64,128,128]{2,1,0:T(8,128)(2,1)} %bitcast.46), calls=%async_computation.1 | async-start | bytes 4194304 | tf_op jit(solution)/shard_map/all_to_all | solution.py:342
  543.7 18.9 %all-to-all-start.4 = ((bf16[4,32,32,128]{3,2,1,0:T(8,128)(2,1)}), bf16[4,32,32,128]{3,2,1,0:T(8,128)(2,1)S(1)}, u32[]{:S(2)}, u32[]{:S(2)}) async-start(bf16[4,32,32,128]{3,2,1,0:T(8,128)(2,1)} %column_transform_over_rows.2), calls=%async_computation.4 | async-start | bytes 2097152 | tf_op jit(solution)/shard_map/all_to_all | solution.py:352
  562.5 17.8 %copy-start.1 = (bf16[4,32,32,128]{3,2,1,0:T(8,128)(2,1)}, bf16[4,32,32,128]{3,2,1,0:T(8,128)(2,1)S(1)}, u32[]{:S(2)}) copy-start(bf16[4,32,32,128]{3,2,1,0:T(8,128)(2,1)S(1)} %all-to-all-done.4.refs_0_) | copy-start | bytes 3145732

commit v2 on v1

v2 whole, which is shorter than its diff:
```python
import functools
import math

import jax
import jax.numpy as jnp
import ml_dtypes
import numpy as np
from jax import lax
from jax.experimental import pallas as pl
from jax.experimental.pallas import tpu as pltpu
from jax.sharding import PartitionSpec as P

N = 8192
BANDS = 64
EDGE = 128
SLOTS = 64
ROWS = 8192
STRIDE = 129
F32 = jnp.float32
BF16 = jnp.bfloat16
VMEM_LIMIT = 56 * 1024 * 1024


def circle(numerator, length):
    angle = 2.0 * np.pi * (np.asarray(numerator) % length) / length
    return np.cos(angle), np.sin(angle)


def split(table):
    high = table.astype(ml_dtypes.bfloat16)
    low = (table - high.astype(np.float64)).astype(ml_dtypes.bfloat16)
    return high, low


def row_first_table():
    cosine, sine = circle(np.arange(64)[:, None] * np.arange(64)[None, :], 64)
    table = np.zeros((2, 64, 64, 2))
    table[0, :, :, 0] = cosine
    table[0, :, :, 1] = -sine
    table[1, :, :, 0] = sine
    table[1, :, :, 1] = cosine
    high, low = split(table.reshape(128, 128))
    return np.concatenate([high, high, low], axis=1)


def row_twiddles():
    cosine, sine = circle(np.arange(128)[:, None] * np.arange(128)[None, :], N)
    return np.stack([cosine, sine]).astype(np.float32)


def row_second_table():
    cosine, sine = circle(np.arange(64)[:, None] * np.arange(128)[None, :], 64)
    table = np.block([[cosine, -sine], [sine, cosine]])
    high, low = split(table)
    return np.concatenate([high, low], axis=0)


def column_second_table():
    cosine, sine = circle(np.arange(128)[:, None] * np.arange(128)[None, :], 128)
    table = np.zeros((2, 128, 2, 2, 64))
    cosine = cosine.reshape(128, 2, 64) / N
    sine = sine.reshape(128, 2, 64) / N
    table[0, :, :, 0] = cosine
    table[0, :, :, 1] = -sine
    table[1, :, :, 0] = sine
    table[1, :, :, 1] = cosine
    high, low = split(table.reshape(256, 256))
    return np.concatenate([high, low], axis=1)


def pack_kernel(count_ref, offset_ref, tiles_ref, out_ref, rows_ref, *, per_step):
    step = pl.program_id(0)

    def one(index, carry):
        slot = step * per_step + index
        shift = offset_ref[slot, 1] & 127
        keep = slot < count_ref[0, 0]
        for part in range(2):
            block = tiles_ref[index, part].astype(F32)
            block = jnp.where(keep, pltpu.roll(block, shift, 1), 0.0)
            rows_ref[pl.ds(slot * 2 + part, 64, stride=STRIDE), :] = block
        return carry

    lax.fori_loop(0, per_step, one, 0, unroll=4)

    @pl.when(step == pl.num_programs(0) - 1)
    def _():
        def cast(index, carry):
            rows = rows_ref[pl.ds(index * STRIDE, 128), :].astype(BF16)
            out_ref[pl.ds(pl.multiple_of(index * 128, 128), 128), :] = rows
            return carry

        lax.fori_loop(0, 64, cast, 0, unroll=2)


def pack(count, offsets, tiles, half):
    per_step = 8
    return pl.pallas_call(
        functools.partial(pack_kernel, per_step=per_step),
        grid=(SLOTS // per_step,),
        in_specs=[
            pl.BlockSpec(memory_space=pltpu.SMEM),
            pl.BlockSpec(memory_space=pltpu.SMEM),
            pl.BlockSpec((per_step, 2, 64, 128), lambda i: (i, 0, half, 0)),
        ],
        out_specs=pl.BlockSpec((ROWS, 128), lambda i: (0, 0)),
        out_shape=jax.ShapeDtypeStruct((ROWS, 128), BF16),
        scratch_shapes=[pltpu.VMEM((64 * STRIDE, 128), F32)],
        compiler_params=pltpu.CompilerParams(vmem_limit_bytes=VMEM_LIMIT),
        cost_estimate=pl.CostEstimate(flops=8 << 20, bytes_accessed=4 << 20, transcendentals=0),
        name="pack_rows",
    )(count, offsets, tiles)


def grid_kernel(
    place_ref, me_ref, pieces_ref, first_ref, twiddle_ref, second_ref, bands_ref, out_ref,
    grid_a, grid_b, rows_ref,
):
    def clear(index, carry):
        where = pl.ds(pl.multiple_of(index * 64, 64), 64)
        grid_a[where, :] = jnp.zeros((64, 128), F32)
        grid_b[where, :] = jnp.zeros((64, 128), F32)
        return carry

    lax.fori_loop(0, ROWS // 64, clear, 0)
    grid_a[pl.ds(ROWS, 8), :] = jnp.zeros((8, 128), F32)
    grid_b[pl.ds(ROWS, 8), :] = jnp.zeros((8, 128), F32)

    me = me_ref[0]
    sublane = lax.broadcasted_iota(jnp.int32, (8, 128), 0)
    lane = lax.broadcasted_iota(jnp.int32, (8, 128), 1)
    position = lane + (sublane // 2) * 128
    upper = sublane < 2

    def place(index, carry):
        pieces = pieces_ref[pl.ds(pl.multiple_of(index * 16, 16), 16), :].astype(F32)
        source = ((index // 8 - me) & 63) * 64 + (index & 7) * 8
        for part in range(2):
            block = pieces[8 * part : 8 * part + 8]
            turned = [block] + [pltpu.roll(block, 8 - 2 * turn, 0) for turn in (1, 2, 3)]
            for piece in range(4):
                both = jnp.where(upper, turned[piece], turned[(piece + 3) % 4])
                packed = place_ref[source + part * 4 + piece]
                shift = packed & 127
                row = packed >> 7
                offset = position - shift
                inside = (offset >= 0) & (offset < 128)
                grid = grid_a if piece % 2 == 0 else grid_b
                window = pl.ds(row, 8)
                grid[window, :] = grid[window, :] + jnp.where(inside, both, 0.0)
        return carry

    lax.fori_loop(0, BANDS * SLOTS // 8, place, 0)

    first = first_ref[...]
    second = second_ref[...]
    cosine = twiddle_ref[0]
    sine = twiddle_ref[1]

    def band_step(band, carry):
        where = pl.ds(pl.multiple_of(band * 128, 128), 128)
        cells = grid_a[where, :] + grid_b[where, :]
        high = cells.astype(BF16)
        low = (cells - high.astype(F32)).astype(BF16)
        section = jnp.dot(
            first, jnp.concatenate([high, low, high], axis=0), preferred_element_type=F32
        )
        real = jnp.concatenate([section[:64], section[:64]], axis=0)
        imag = jnp.concatenate([section[64:], section[64:]], axis=0)
        turned = jnp.concatenate(
            [real * cosine - imag * sine, real * sine + imag * cosine], axis=1
        )
        high = turned.astype(BF16)
        low = (turned - high.astype(F32)).astype(BF16)
        contract = (((1,), (1,)), ((), ()))
        main = lax.dot_general(second, high, contract, preferred_element_type=F32)
        rest = lax.dot_general(second[:128], low, contract, preferred_element_type=F32)
        spectrum = main[:128] + main[128:] + rest
        rows_ref[pl.ds(band, 64, stride=STRIDE), :] = spectrum[:64]
        rows_ref[pl.ds(64 + band, 64, stride=STRIDE), :] = spectrum[64:]
        return carry

    lax.fori_loop(0, BANDS, band_step, 0, unroll=2)

    table = bands_ref[...]

    def block_step(index, carry):
        rows = rows_ref[pl.ds(index * STRIDE, 128), :].astype(BF16)
        section = jnp.dot(table, jnp.concatenate([rows, rows], axis=0), preferred_element_type=F32)
        out_ref[pl.ds(pl.multiple_of(index * 128, 128), 128), :] = section.astype(BF16)
        return carry

    lax.fori_loop(0, 64, block_step, 0, unroll=2)


def grid_and_rows(places, me, pieces, first, twiddle, second, bands):
    vmem = pl.BlockSpec(memory_space=pltpu.VMEM)
    smem = pl.BlockSpec(memory_space=pltpu.SMEM)
    return pl.pallas_call(
        grid_kernel,
        in_specs=[smem, smem, vmem, vmem, vmem, vmem, vmem],
        out_specs=vmem,
        out_shape=jax.ShapeDtypeStruct((ROWS, 128), BF16),
        scratch_shapes=[
            pltpu.VMEM((ROWS + 8, 128), F32),
            pltpu.VMEM((ROWS + 8, 128), F32),
            pltpu.VMEM((64 * STRIDE, 128), F32),
        ],
        compiler_params=pltpu.CompilerParams(vmem_limit_bytes=VMEM_LIMIT),
        cost_estimate=pl.CostEstimate(flops=20_000_000_000, bytes_accessed=4 << 20, transcendentals=0),
        name="place_and_transform",
    )(places, me, pieces, first, twiddle, second, bands)


def column_kernel(early_ref, late_ref, table_ref, cosine_ref, sine_ref, own_ref, *sent):
    table = table_ref[...]
    count = early_ref.shape[0]
    late = jnp.swapaxes(late_ref[...], 0, 1).reshape(count, 128, 128)
    for index in range(count):
        cells = jnp.concatenate([early_ref[index], late[index]], axis=0)
        sky = jnp.dot(table, jnp.concatenate([cells, cells], axis=0), preferred_element_type=F32)
        image = sky[:128] * cosine_ref[index] - sky[128:] * sine_ref[index]
        own_ref[index] = image[:32]
        for step in range(3):
            sent[step][index] = image[32 * step + 32 : 32 * step + 64].astype(BF16)


def column_transform(early, late, table, cosine, sine, begin, count):
    per_step = 8
    skip = begin // per_step
    block = pl.BlockSpec((per_step, 128, 128), lambda i: (i + skip, 0, 0))
    result = pl.BlockSpec((per_step, 32, 128), lambda i: (i, 0, 0))
    return pl.pallas_call(
        column_kernel,
        grid=(count // per_step,),
        in_specs=[
            block,
            pl.BlockSpec((64, 2 * per_step, 128), lambda i: (0, i + skip, 0)),
            pl.BlockSpec((256, 512), lambda i: (0, 0)),
            block,
            block,
        ],
        out_specs=[result] * 4,
        out_shape=[jax.ShapeDtypeStruct((count, 32, 128), F32)]
        + [jax.ShapeDtypeStruct((count, 32, 128), BF16)] * 3,
        compiler_params=pltpu.CompilerParams(vmem_limit_bytes=VMEM_LIMIT),
        cost_estimate=pl.CostEstimate(
            flops=count * 70_000_000, bytes_accessed=count * (200 << 10), transcendentals=0
        ),
        name="column_transform",
    )(early, late, table, cosine, sine)


def sum_kernel(*refs, counts):
    out_ref = refs[-1]
    begin = 0
    for part, count in enumerate(counts):
        own, *others = refs[4 * part : 4 * part + 4]
        for group in range(0, count, 8):
            total = own[group : group + 8]
            for other in others:
                total = total + other[group : group + 8].astype(F32)
            out_ref[:, begin + group : begin + group + 8, :] = jnp.swapaxes(total, 0, 1)
        begin += count


def window_sum(parts, counts):
    vmem = pl.BlockSpec(memory_space=pltpu.VMEM)
    flat = [block for part in parts for block in part]
    return pl.pallas_call(
        functools.partial(sum_kernel, counts=counts),
        in_specs=[vmem] * len(flat),
        out_specs=vmem,
        out_shape=jax.ShapeDtypeStruct((32, 64, 128), F32),
        compiler_params=pltpu.CompilerParams(vmem_limit_bytes=VMEM_LIMIT),
        cost_estimate=pl.CostEstimate(flops=1 << 20, bytes_accessed=3 << 20, transcendentals=0),
        name="window_sum",
    )(*flat)


def w_phases(plane_w, turn):
    k = jnp.arange(64, dtype=jnp.int32)[:, None, None]
    j = (jnp.arange(128, dtype=jnp.int32)[None, :, None] + 32 * turn) % 128
    column = lax.axis_index("band") * 128 + jnp.arange(128, dtype=jnp.int32)[None, None, :]
    x = ((64 * j + k).astype(F32) - N // 2) / N
    y = (column.astype(F32) - N // 2) / N
    radius = x**2 + y**2
    angle = 2.0 * math.pi * plane_w * (jnp.sqrt(1.0 - radius) - 1.0)
    return jnp.cos(angle), jnp.sin(angle)


def band_table(row):
    k = jnp.arange(64, dtype=jnp.int32)[:, None]
    band = jnp.arange(64, dtype=jnp.int32)[None, :]
    angle = (2.0 * math.pi / N) * ((k * (128 * band + row)) % N).astype(F32)
    cosine = jnp.cos(angle)
    sine = jnp.sin(angle)
    real = jnp.concatenate([cosine, -sine], axis=1)
    imag = jnp.concatenate([sine, cosine], axis=1)
    table = jnp.stack([real, imag], axis=1).reshape(128, 128)
    high = table.astype(BF16)
    low = (table - high.astype(F32)).astype(BF16)
    return jnp.concatenate([high, low], axis=1)


def gather_places(place):
    held = place
    reach = 1
    while reach < BANDS:
        pairs = [(source, (source - reach) % BANDS) for source in range(BANDS)]
        held = jnp.concatenate([held, lax.ppermute(held, "band", pairs)])
        reach *= 2
    return held


def local(uv_tiles, target_bands, uv_offsets, tile_counts, plane_w):
    tiles = uv_tiles[0]
    offsets = uv_offsets[0]
    me = lax.axis_index("band")
    turn = lax.axis_index("wp")
    column = offsets[:, 1]
    place = (target_bands[0, :, 0] * 64 + column // 128) * 256 + column % 128
    places = gather_places(place)

    first = jnp.asarray(row_first_table())
    twiddle = jnp.asarray(row_twiddles())
    second = jnp.asarray(row_second_table())

    arrived = []
    for half in range(2):
        packed = pack(tile_counts, offsets, tiles, half)
        arrived.append(
            lax.all_to_all(
                packed.reshape(64, 128, 128), "band", split_axis=0, concat_axis=0, tiled=True
            ).reshape(ROWS, 128)
        )
    columns = []
    for half in range(2):
        spectrum = grid_and_rows(
            places, me[None], arrived[half], first, twiddle, second, band_table(me + 64 * half)
        )
        columns.append(
            lax.all_to_all(
                spectrum.reshape(64, 128, 128), "band", split_axis=0, concat_axis=0, tiled=True
            )
        )
    early = jnp.swapaxes(columns[0], 0, 1).reshape(64, 128, 128)

    cosine, sine = w_phases(plane_w[0], turn)
    table = jnp.roll(jnp.asarray(column_second_table()).reshape(2, 128, 512), -32 * turn, axis=1)
    table = table.reshape(256, 512)
    counts = (32, 32)
    parts = []
    begin = 0
    for count in counts:
        own, *sent = column_transform(early, columns[1], table, cosine, sine, begin, count)
        moved = [
            lax.ppermute(block, "wp", [(plane, (plane + step + 1) % 4) for plane in range(4)])
            for step, block in enumerate(sent)
        ]
        parts.append([own, *moved])
        begin += count
    return window_sum(parts, counts).reshape(2048, 128)


def solution(mesh):
    placed = (
        P("wp", "band", None, None, None),
        P("wp", "band", None),
        P("wp", "band", None),
        P("wp", "band"),
        P("wp"),
    )
    return jax.shard_map(
        local, mesh=mesh, in_specs=placed, out_specs=P("wp", "band"), check_vma=False
    )
```

time: 589 us -> 370 us (0.63)
  blocking collectives: 295 us -> 0 us
  waiting for transfers between devices: 76.7 us -> 134 us
  starting transfers between devices: 45.6 us -> 72.1 us
  Pallas kernels: 141 us -> 127 us
  local copies, waits for them, and re-layouts: 3.93 us -> 11.9 us
    unnamed x1 -> x0, blocking collectives: 277 us -> none
    ppermute x0 -> x12, waiting for transfers between devices: none -> 63.5 us  [the longest x6 50.6 us: gather_places(): held = jnp.concatenate([held, lax.ppermute(held, 'band', pairs)])]
    ppermute x0 -> x12, starting transfers between devices: none -> 24.5 us  [the longest x6 16.8 us: gather_places(): held = jnp.concatenate([held, lax.ppermute(held, 'band', pairs)])]
    all_to_all x1 -> x0, blocking collectives: 17.8 us -> none  [local(): lax.all_to_all(image, 'wp', split_axis=0, concat_axis=0, tiled=True)]
    pallas_call x7 -> x5, Pallas kernels: 122 us -> 113 us  [the longest x2 98.4 us: grid_and_rows(): pl.pallas_call(grid_kernel, in_specs=[smem, smem, vmem, vmem, vmem, vmem,...]
    all_to_all x1 -> x0, waiting for transfers between devices: 7.45 us -> none  [local(): lax.all_to_all(image, 'wp', split_axis=0, concat_axis=0, tiled=True)]
    all_to_all x2, starting transfers between devices: 22.4 us -> 28.6 us  [local(): lax.all_to_all(spectrum.reshape(64, 128, 128), 'band', split_axis=0, conc...]
  transfers between devices with their start and end apart: 5 -> 16, of which waited for: 4 -> 13; matrix products, arithmetic and copies ran while one was open for 3% -> 7% of each run, Pallas kernels for 19% -> 30%
where the time goes in v2:
time: 370 us; the launch traced here: 367 us
  waiting for transfers between devices  134 us (36%)
  Pallas kernels  127 us (34%)
  starting transfers between devices  72.1 us (19%)
  other arithmetic  20.5 us (6%)
  local copies, waits for them, and re-layouts  11.9 us (3%)
    pallas_call x2, Pallas kernels, grid_and_rows(): pl.pallas_call(grid_kernel, in_specs=[smem, smem, vmem, vmem, vmem, vmem,...  98.4 us
    ppermute x6, waiting for transfers between devices, gather_places(): held = jnp.concatenate([held, lax.ppermute(held, 'band', pairs)])  50.6 us
    all_to_all x2, waiting for transfers between devices, local(): lax.all_to_all(packed.reshape(64, 128, 128), 'band', split_axis=0, concat...  42.8 us
    all_to_all x2, starting transfers between devices, local(): lax.all_to_all(spectrum.reshape(64, 128, 128), 'band', split_axis=0, conc...  28.6 us
    all_to_all x2, waiting for transfers between devices, local(): lax.all_to_all(spectrum.reshape(64, 128, 128), 'band', split_axis=0, conc...  27.3 us
    all_to_all x2, starting transfers between devices, local(): lax.all_to_all(packed.reshape(64, 128, 128), 'band', split_axis=0, concat...  19 us
    sin x1, other arithmetic, w_phases(): return (jnp.cos(angle), jnp.sin(angle))  18.4 us
    ppermute x6, starting transfers between devices, gather_places(): held = jnp.concatenate([held, lax.ppermute(held, 'band', pairs)])  16.8 us
  transfers between devices with their start and end apart: 16, of which 13 were waited for; matrix products, arithmetic and copies ran while one was open for 7% of the time, Pallas kernels for 30%

profile of v2, /device:TPU:33, one launch (start us, length us, event | category | flops | bytes accessed | tf_op | source)
XLA Modules:
  0.0 367.1 jit_solution(1381614769955440657)
XLA Ops:
  0.0 1.4 copy.15.offset_ref
  2.0 7.1 %pack_rows.2 = bf16[8192,128]{1,0:T(8,128)(2,1)} custom-call(s32[1,1]{1,0:T(1,128)S(6)} %copy.20.count_ref, s32[64,2]{1,0:T(8,128)} %copy.15.offset_ref, bf16[64,2,128,128]{3,2,1,0:T(8,128)(2,1)} %bitcast.45), custom_call_target="tpu_custom_call" | custom-call | flops 8388608 | bytes 4194304 | tf_op jit(solution)/shard_map/pack_rows/pallas_call | solution.py:98
  9.2 11.9 %all-to-all-start = ((bf16[64,128,128]{2,1,0:T(8,128)(2,1)}), bf16[64,128,128]{2,1,0:T(8,128)(2,1)S(1)}, u32[]{:S(2)}, u32[]{:S(2)}) async-start(bf16[64,128,128]{2,1,0:T(8,128)(2,1)} %bitcast.48), calls=%async_computation | async-start | bytes 4194304 | tf_op jit(solution)/shard_map/all_to_all | solution.py:333
  21.1 7.1 %pack_rows.3 = bf16[8192,128]{1,0:T(8,128)(2,1)} custom-call(s32[1,1]{1,0:T(1,128)S(6)} %copy.20.count_ref, s32[64,2]{1,0:T(8,128)} %copy.15.offset_ref, bf16[64,2,128,128]{3,2,1,0:T(8,128)(2,1)} %bitcast.46), custom_call_target="tpu_custom_call" | custom-call | flops 8388608 | bytes 4194304 | tf_op jit(solution)/shard_map/pack_rows/pallas_call | solution.py:98
  28.2 42.8 %all-to-all-done = bf16[64,128,128]{2,1,0:T(8,128)(2,1)S(1)} async-done(((bf16[64,128,128]{2,1,0:T(8,128)(2,1)}), bf16[64,128,128]{2,1,0:T(8,128)(2,1)S(1)}, u32[]{:S(2)}, u32[]{:S(2)}) %all-to-all-start) | async-done | bytes 2097184 | tf_op jit(solution)/shard_map/all_to_all | solution.py:333
  71.0 1.4 copy-done.4
  72.4 7.1 %all-to-all-start.2 = ((bf16[64,128,128]{2,1,0:T(8,128)(2,1)}), bf16[64,128,128]{2,1,0:T(8,128)(2,1)S(1)}, u32[]{:S(2)}, u32[]{:S(2)}) async-start(bf16[64,128,128]{2,1,0:T(8,128)(2,1)} %bitcast.47), calls=%async_computation.2 | async-start | bytes 4194304 | tf_op jit(solution)/shard_map/all_to_all | solution.py:333
  79.5 0.4 collective-permute-start
  80.0 45.4 %collective-permute-done = s32[64]{0:T(128)S(1)} collective-permute-done((s32[64]{0:T(128)S(1)}, s32[64]{0:T(128)S(1)}, u32[]{:S(2)}, u32[]{:S(2)}) %collective-permute-start) | collective-permute-done | bytes 288 | tf_op jit(solution)/shard_map/ppermute | solution.py:311
  125.5 1.4 collective-permute-start.1
  127.0 1.1 collective-permute-done.1
  128.2 5.1 %collective-permute-start.2 = (s32[256]{0:T(256)S(1)}, s32[256]{0:T(256)S(1)}, u32[]{:S(2)}, u32[]{:S(2)}) collective-permute-start(s32[256]{0:T(256)S(1)} %pad_add_fusion.1), channel_id=1, source_target_pairs={{0,240},{4,244},{8,248},{12,252},{16,0},{20,4},{24,8},{28,12},{32,... | collective-permute-start | bytes 3080 | tf_op jit(solution)/shard_map/ppermute | solution.py:311
  133.5 0.9 collective-permute-done.2
  134.5 5.4 %collective-permute-start.3 = (s32[512]{0:T(512)S(1)}, s32[512]{0:T(512)S(1)}, u32[]{:S(2)}, u32[]{:S(2)}) collective-permute-start(s32[512]{0:T(512)S(1)} %pad_add_fusion), channel_id=1, source_target_pairs={{0,224},{4,228},{8,232},{12,236},{16,240},{20,244},{24,248},{28,25... | collective-permute-start | bytes 6152 | tf_op jit(solution)/shard_map/ppermute | solution.py:311
  139.9 0.9 collective-permute-done.3
  140.9 2.6 collective-permute-start.4
  143.5 0.7 collective-permute-done.4
  144.3 1.9 collective-permute-start.5
  146.2 0.6 pad_maximum_fusion.1.bands_ref
  146.8 1.5 collective-permute-done.5
  148.3 0.7 concatenate.50.place_ref
  149.0 49.2 %place_and_transform.2 = bf16[8192,128]{1,0:T(8,128)(2,1)} custom-call(s32[4096]{0:T(1024)} %concatenate.50.place_ref, s32[1]{0:T(128)} %bitcast.3.me_ref, bf16[8192,128]{1,0:T(8,128)(2,1)} %bitcast.53, bf16[128,384]{1,0:T(8,128)(2,1)} %constant.118.clone.first_ref, f32[2,128,128]{2,1,0:T(8,128)} %constant.119.clone.twiddle_ref, ...), custom_call_target="tpu_custom_call" | custom-call | flops 20000000000 | bytes 4194304 | tf_op jit(solution)/shard_map/place_and_transform/pallas_call | solution.py:199
  198.2 1.3 copy-done.3
  199.5 18.2 %all-to-all-start.1 = ((bf16[64,128,128]{2,1,0:T(8,128)(2,1)}), bf16[64,128,128]{2,1,0:T(8,128)(2,1)S(1)}, u32[]{:S(2)}, u32[]{:S(2)}) async-start(bf16[64,128,128]{2,1,0:T(8,128)(2,1)} %bitcast.55), calls=%async_computation.1 | async-start | bytes 4194304 | tf_op jit(solution)/shard_map/all_to_all | solution.py:343
  218.1 0.6 pad_maximum_fusion.3.bands_ref
  218.8 49.2 %place_and_transform.3 = bf16[8192,128]{1,0:T(8,128)(2,1)} custom-call(s32[4096]{0:T(1024)} %concatenate.50.place_ref, s32[1]{0:T(128)} %bitcast.3.me_ref, bf16[8192,128]{1,0:T(8,128)(2,1)} %bitcast.52, bf16[128,384]{1,0:T(8,128)(2,1)} %constant.118.clone.first_ref, f32[2,128,128]{2,1,0:T(8,128)} %constant.119.clone.twiddle_ref, ...), custom_call_target="tpu_custom_call" | custom-call | flops 20000000000 | bytes 4194304 | tf_op jit(solution)/shard_map/place_and_transform/pallas_call | solution.py:199
  268.0 1.4 copy-done.1
  269.4 10.3 %all-to-all-start.3 = ((bf16[64,128,128]{2,1,0:T(8,128)(2,1)}), bf16[64,128,128]{2,1,0:T(8,128)(2,1)S(1)}, u32[]{:S(2)}, u32[]{:S(2)}) async-start(bf16[64,128,128]{2,1,0:T(8,128)(2,1)} %bitcast.54), calls=%async_computation.3 | async-start | bytes 4194304 | tf_op jit(solution)/shard_map/all_to_all | solution.py:343
  280.4 0.7 constant_dynamic-slice_fusion
  281.2 18.4 %fusion = (f32[64,128,128]{2,1,0:T(8,128)}, f32[64,128,128]{2,1,0:T(8,128)}) fusion(f32[128]{0:T(128)S(1)} %multiply_multiply_fusion.1, f32[64,128]{1,0:T(8,128)S(1)} %multiply_multiply_fusion, f32[]{:T(128)} %bitcast.21), kind=kLoop, calls=%fused_computation.1 | loop fusion | flops 4194304 | bytes 8421892 | tf_op jit(solution)/shard_map/sin | solution.py:289
  299.6 2.7 copy.17
  302.3 27.3 %all-to-all-done.3.late_ref = bf16[64,128,128]{2,1,0:T(8,128)(2,1)S(1)} async-done(((bf16[64,128,128]{2,1,0:T(8,128)(2,1)}), bf16[64,128,128]{2,1,0:T(8,128)(2,1)S(1)}, u32[]{:S(2)}, u32[]{:S(2)}) %all-to-all-start.3) | async-done | bytes 2097184 | tf_op jit(solution)/shard_map/all_to_all | solution.py:343
  329.6 1.4 copy-done
  331.0 5.9 %column_transform.3 = (f32[32,32,128]{2,1,0:T(8,128)}, bf16[32,32,128]{2,1,0:T(8,128)(2,1)}, bf16[32,32,128]{2,1,0:T(8,128)(2,1)}, bf16[32,32,128]{2,1,0:T(8,128)(2,1)}) custom-call(bf16[64,128,128]{2,1,0:T(8,128)(2,1)} %bitcast.43, bf16[64,128,128]{2,1,0:T(8,128)(2,1)} %copy-done, bf16[256,512]{1,0:T(8,128)(2,1)} %bitcast.50, ...), custom_call_target="tpu_custom_call" | custom-call | flops 2240000000 | bytes 6553600 | tf_op jit(solution)/shard_map/column_transform/pallas_call | solution.py:233
  336.9 3.0 collective-permute-start.10
  339.9 0.8 collective-permute-start.11
  340.6 0.7 collective-permute-start.9
  341.3 5.9 %column_transform.2 = (f32[32,32,128]{2,1,0:T(8,128)}, bf16[32,32,128]{2,1,0:T(8,128)(2,1)}, bf16[32,32,128]{2,1,0:T(8,128)(2,1)}, bf16[32,32,128]{2,1,0:T(8,128)(2,1)}) custom-call(bf16[64,128,128]{2,1,0:T(8,128)(2,1)} %bitcast.44, bf16[64,128,128]{2,1,0:T(8,128)(2,1)} %copy-done, bf16[256,512]{1,0:T(8,128)(2,1)} %bitcast.51, ...), custom_call_target="tpu_custom_call" | custom-call | flops 2240000000 | bytes 6553600 | tf_op jit(solution)/shard_map/column_transform/pallas_call | solution.py:233
  347.2 0.4 collective-permute-start.6
  347.7 2.8 collective-permute-start.7
  350.5 1.9 collective-permute-done.11.refs_7_
  352.3 0.2 collective-permute-done.9.refs_5_
  352.5 5.8 %collective-permute-done.6.refs_1_ = bf16[32,32,128]{2,1,0:T(8,128)(2,1)S(1)} collective-permute-done((bf16[32,32,128]{2,1,0:T(8,128)(2,1)}, bf16[32,32,128]{2,1,0:T(8,128)(2,1)S(1)}, u32[]{:S(2)}, u32[]{:S(2)}) %collective-permute-start.6) | collective-permute-done | bytes 262176 | tf_op jit(solution)/shard_map/ppermute | solution.py:358
  358.3 4.7 %collective-permute-done.7.refs_2_ = bf16[32,32,128]{2,1,0:T(8,128)(2,1)S(1)} collective-permute-done((bf16[32,32,128]{2,1,0:T(8,128)(2,1)}, bf16[32,32,128]{2,1,0:T(8,128)(2,1)S(1)}, u32[]{:S(2)}, u32[]{:S(2)}) %collective-permute-start.7) | collective-permute-done | bytes 262176 | tf_op jit(solution)/shard_map/ppermute | solution.py:358
  363.0 0.4 collective-permute-done.8.refs_3_
  363.4 0.3 copy-done.9
  363.7 0.4 copy-done.10
  364.1 3.0 window_sum.1
  (46 shorter events, 1.1 us)
Async XLA Ops:
  9.2 61.8 %all-to-all-start = ((bf16[64,128,128]{2,1,0:T(8,128)(2,1)}), bf16[64,128,128]{2,1,0:T(8,128)(2,1)S(1)}, u32[]{:S(2)}, u32[]{:S(2)}) async-start(bf16[64,128,128]{2,1,0:T(8,128)(2,1)} %bitcast.48), calls=%async_computation | async-start | bytes 4194304 | tf_op jit(solution)/shard_map/all_to_all | solution.py:333
  21.1 58.4 %copy-start.12 = (s32[1,64,2]{1,2,0:T(2,128)S(1)}, s32[1,64,2]{1,2,0:T(2,128)}, u32[]{:S(2)}) copy-start(s32[1,64,2]{1,2,0:T(2,128)} %param.11) | copy-start | bytes 1540
  21.1 58.4 %copy-start.13 = (s32[1,64,1]{1,2,0:T(1,128)S(1)}, s32[1,64,1]{1,2,0:T(1,128)}, u32[]{:S(2)}) copy-start(s32[1,64,1]{1,2,0:T(1,128)} %param.10) | copy-start | bytes 772
  71.0 1.4 copy-start.4
  72.4 125.8 %all-to-all-start.2 = ((bf16[64,128,128]{2,1,0:T(8,128)(2,1)}), bf16[64,128,128]{2,1,0:T(8,128)(2,1)S(1)}, u32[]{:S(2)}, u32[]{:S(2)}) async-start(bf16[64,128,128]{2,1,0:T(8,128)(2,1)} %bitcast.47), calls=%async_computation.2 | async-start | bytes 4194304 | tf_op jit(solution)/shard_map/all_to_all | solution.py:333
  79.5 45.8 %collective-permute-start = (s32[64]{0:T(128)S(1)}, s32[64]{0:T(128)S(1)}, u32[]{:S(2)}, u32[]{:S(2)}) collective-permute-start(s32[64]{0:T(128)S(1)} %fusion.20), channel_id=1, source_target_pairs={{0,252},{4,0},{8,4},{12,8},{16,12},{20,16},{24,20},{28,24},{32,28}... | collective-permute-start | bytes 776 | tf_op jit(solution)/shard_map/ppermute | solution.py:311
  125.5 2.7 collective-permute-start.1
  128.2 6.2 %collective-permute-start.2 = (s32[256]{0:T(256)S(1)}, s32[256]{0:T(256)S(1)}, u32[]{:S(2)}, u32[]{:S(2)}) collective-permute-start(s32[256]{0:T(256)S(1)} %pad_add_fusion.1), channel_id=1, source_target_pairs={{0,240},{4,244},{8,248},{12,252},{16,0},{20,4},{24,8},{28,12},{32,... | collective-permute-start | bytes 3080 | tf_op jit(solution)/shard_map/ppermute | solution.py:311
  134.5 6.4 %collective-permute-start.3 = (s32[512]{0:T(512)S(1)}, s32[512]{0:T(512)S(1)}, u32[]{:S(2)}, u32[]{:S(2)}) collective-permute-start(s32[512]{0:T(512)S(1)} %pad_add_fusion), channel_id=1, source_target_pairs={{0,224},{4,228},{8,232},{12,236},{16,240},{20,244},{24,248},{28,25... | collective-permute-start | bytes 6152 | tf_op jit(solution)/shard_map/ppermute | solution.py:311
  140.9 3.3 collective-permute-start.4
  144.3 4.0 %collective-permute-start.5 = (s32[2048]{0:T(1024)S(1)}, s32[2048]{0:T(1024)S(1)}, u32[]{:S(2)}, u32[]{:S(2)}) collective-permute-start(s32[2048]{0:T(1024)S(1)} %concatenate.49), channel_id=1, source_target_pairs={{0,128},{4,132},{8,136},{12,140},{16,144},{20,148},{24,152},{28,15... | collective-permute-start | bytes 24584 | tf_op jit(solution)/shard_map/ppermute | solution.py:311
  198.2 1.3 copy-start.3
  199.5 68.5 %all-to-all-start.1 = ((bf16[64,128,128]{2,1,0:T(8,128)(2,1)}), bf16[64,128,128]{2,1,0:T(8,128)(2,1)S(1)}, u32[]{:S(2)}, u32[]{:S(2)}) async-start(bf16[64,128,128]{2,1,0:T(8,128)(2,1)} %bitcast.55), calls=%async_computation.1 | async-start | bytes 4194304 | tf_op jit(solution)/shard_map/all_to_all | solution.py:343
  268.0 12.4 %copy-start.11 = (bf16[2,256,512]{2,1,0:T(8,128)(2,1)S(1)}, bf16[2,256,512]{2,1,0:T(8,128)(2,1)}, u32[]{:S(2)}) copy-start(bf16[2,256,512]{2,1,0:T(8,128)(2,1)} %constant.128) | copy-start | bytes 1572868
  268.0 1.4 copy-start.1
  269.4 60.3 %all-to-all-start.3 = ((bf16[64,128,128]{2,1,0:T(8,128)(2,1)}), bf16[64,128,128]{2,1,0:T(8,128)(2,1)S(1)}, u32[]{:S(2)}, u32[]{:S(2)}) async-start(bf16[64,128,128]{2,1,0:T(8,128)(2,1)} %bitcast.54), calls=%async_computation.3 | async-start | bytes 4194304 | tf_op jit(solution)/shard_map/all_to_all | solution.py:343
  281.2 18.4 %copy-start.2 = (bf16[64,128,128]{2,1,0:T(8,128)(2,1)S(1)}, bf16[64,128,128]{2,1,0:T(8,128)(2,1)}, u32[]{:S(2)}) copy-start(bf16[64,128,128]{2,1,0:T(8,128)(2,1)} %copy-done.1) | copy-start | bytes 6291460
  329.6 1.4 copy-start
  336.9 13.5 %collective-permute-start.10 = (bf16[32,32,128]{2,1,0:T(8,128)(2,1)}, bf16[32,32,128]{2,1,0:T(8,128)(2,1)S(1)}, u32[]{:S(2)}, u32[]{:S(2)}) collective-permute-start(bf16[32,32,128]{2,1,0:T(8,128)(2,1)} %get-tuple-element.19), channel_id=1, source_target_pairs={{0,2},{1,3},{2,0},{3,1},{4,6},{5,7},{6,4},{7,5},{8,10},{9,11},{10,... | collective-permute-start | bytes 786440 | tf_op jit(solution)/shard_map/ppermute | solution.py:358
  339.9 12.5 %collective-permute-start.11 = (bf16[32,32,128]{2,1,0:T(8,128)(2,1)}, bf16[32,32,128]{2,1,0:T(8,128)(2,1)S(1)}, u32[]{:S(2)}, u32[]{:S(2)}) collective-permute-start(bf16[32,32,128]{2,1,0:T(8,128)(2,1)} %get-tuple-element.20), channel_id=1, source_target_pairs={{0,3},{1,0},{2,1},{3,2},{4,7},{5,4},{6,5},{7,6},{8,11},{9,8},{10,9... | collective-permute-start | bytes 786440 | tf_op jit(solution)/shard_map/ppermute | solution.py:358
  340.6 11.9 %collective-permute-start.9 = (bf16[32,32,128]{2,1,0:T(8,128)(2,1)}, bf16[32,32,128]{2,1,0:T(8,128)(2,1)S(1)}, u32[]{:S(2)}, u32[]{:S(2)}) collective-permute-start(bf16[32,32,128]{2,1,0:T(8,128)(2,1)} %get-tuple-element.18), channel_id=1, source_target_pairs={{0,1},{1,2},{2,3},{3,0},{4,5},{5,6},{6,7},{7,4},{8,9},{9,10},{10,1... | collective-permute-start | bytes 786440 | tf_op jit(solution)/shard_map/ppermute | solution.py:358
  347.2 11.1 %collective-permute-start.6 = (bf16[32,32,128]{2,1,0:T(8,128)(2,1)}, bf16[32,32,128]{2,1,0:T(8,128)(2,1)S(1)}, u32[]{:S(2)}, u32[]{:S(2)}) collective-permute-start(bf16[32,32,128]{2,1,0:T(8,128)(2,1)} %get-tuple-element.14), channel_id=1, source_target_pairs={{0,1},{1,2},{2,3},{3,0},{4,5},{5,6},{6,7},{7,4},{8,9},{9,10},{10,1... | collective-permute-start | bytes 786440 | tf_op jit(solution)/shard_map/ppermute | solution.py:358
  347.7 15.3 %collective-permute-start.7 = (bf16[32,32,128]{2,1,0:T(8,128)(2,1)}, bf16[32,32,128]{2,1,0:T(8,128)(2,1)S(1)}, u32[]{:S(2)}, u32[]{:S(2)}) collective-permute-start(bf16[32,32,128]{2,1,0:T(8,128)(2,1)} %get-tuple-element.15), channel_id=1, source_target_pairs={{0,2},{1,3},{2,0},{3,1},{4,6},{5,7},{6,4},{7,5},{8,10},{9,11},{10,... | collective-permute-start | bytes 786440 | tf_op jit(solution)/shard_map/ppermute | solution.py:358
  350.5 13.0 %copy-start.5 = (bf16[32,32,128]{2,1,0:T(8,128)(2,1)}, bf16[32,32,128]{2,1,0:T(8,128)(2,1)S(1)}, u32[]{:S(2)}) copy-start(bf16[32,32,128]{2,1,0:T(8,128)(2,1)S(1)} %collective-permute-done.10.refs_6_) | copy-start | bytes 786436
  350.5 13.0 %collective-permute-start.8 = (bf16[32,32,128]{2,1,0:T(8,128)(2,1)}, bf16[32,32,128]{2,1,0:T(8,128)(2,1)S(1)}, u32[]{:S(2)}, u32[]{:S(2)}) collective-permute-start(bf16[32,32,128]{2,1,0:T(8,128)(2,1)} %get-tuple-element.16), channel_id=1, source_target_pairs={{0,3},{1,0},{2,1},{3,2},{4,7},{5,4},{6,5},{7,6},{8,11},{9,8},{10,9... | collective-permute-start | bytes 786440 | tf_op jit(solution)/shard_map/ppermute | solution.py:358
  352.3 11.1 %copy-start.6 = (bf16[32,32,128]{2,1,0:T(8,128)(2,1)}, bf16[32,32,128]{2,1,0:T(8,128)(2,1)S(1)}, u32[]{:S(2)}) copy-start(bf16[32,32,128]{2,1,0:T(8,128)(2,1)S(1)} %collective-permute-done.11.refs_7_) | copy-start | bytes 786436
  352.5 10.9 %copy-start.7 = (bf16[32,32,128]{2,1,0:T(8,128)(2,1)}, bf16[32,32,128]{2,1,0:T(8,128)(2,1)S(1)}, u32[]{:S(2)}) copy-start(bf16[32,32,128]{2,1,0:T(8,128)(2,1)S(1)} %collective-permute-done.9.refs_5_) | copy-start | bytes 786436
  358.3 5.1 %copy-start.8 = (bf16[32,32,128]{2,1,0:T(8,128)(2,1)}, bf16[32,32,128]{2,1,0:T(8,128)(2,1)S(1)}, u32[]{:S(2)}) copy-start(bf16[32,32,128]{2,1,0:T(8,128)(2,1)S(1)} %collective-permute-done.6.refs_1_) | copy-start | bytes 786436
  363.0 0.7 copy-start.9
  363.4 0.7 copy-start.10

commit v3 on v2

--- a/solution.py
+++ b/solution.py
@@ -18,7 +18,7 @@
 STRIDE = 129
 F32 = jnp.float32
 BF16 = jnp.bfloat16
-VMEM_LIMIT = 56 * 1024 * 1024
+MIB = 1 << 20
 
 
 def circle(numerator, length):
@@ -68,54 +68,95 @@
     return np.concatenate([high, low], axis=1)
 
 
-def pack_kernel(count_ref, offset_ref, tiles_ref, out_ref, rows_ref, *, per_step):
-    step = pl.program_id(0)
-
-    def one(index, carry):
-        slot = step * per_step + index
-        shift = offset_ref[slot, 1] & 127
-        keep = slot < count_ref[0, 0]
+def pack_kernel(
+    count_ref, band_ref, offset_ref, tiles_ref, out_ref, held_ref, rows_ref, done_ref, in_sems, out_sems,
+    *, half
+):
+    groups = 8
+    each = SLOTS // groups
+    incoming = []
+    for group in range(groups):
+        where = pl.ds(each * group, each)
+        copy = pltpu.make_async_copy(
+            tiles_ref.at[where, :, pl.ds(64 * half, 64), :], held_ref.at[where], in_sems.at[group]
+        )
+        copy.start()
+        incoming.append(copy)
+
+    count = count_ref[0, 0]
+    if half == 0:
+        row = lax.broadcasted_iota(jnp.int32, (8, 128), 0)
+        lane = lax.broadcasted_iota(jnp.int32, (8, 128), 1)
+
+        def number(slot, values):
+            column = offset_ref[1, slot]
+            values = jnp.where((row == 0) & (lane == slot), band_ref[0, slot], values)
+            values = jnp.where((row == 1) & (lane == slot), column >> 7, values)
+            return jnp.where((row == 2) & (lane == slot), column & 127, values)
+
+        values = lax.fori_loop(0, SLOTS, number, jnp.zeros((8, 128), jnp.int32), unroll=4)
+        places = values.astype(F32).astype(BF16)
+
+    def one(slot, carry):
+        shift = offset_ref[1, slot] & 127
+        keep = slot < count
+        tile = pltpu.roll(held_ref[slot].astype(F32).reshape(128, 128), shift, 1)
+        tile = jnp.where(keep, tile, 0.0)
         for part in range(2):
-            block = tiles_ref[index, part].astype(F32)
-            block = jnp.where(keep, pltpu.roll(block, shift, 1), 0.0)
-            rows_ref[pl.ds(slot * 2 + part, 64, stride=STRIDE), :] = block
-        return carry
-
-    lax.fori_loop(0, per_step, one, 0, unroll=4)
-
-    @pl.when(step == pl.num_programs(0) - 1)
-    def _():
-        def cast(index, carry):
-            rows = rows_ref[pl.ds(index * STRIDE, 128), :].astype(BF16)
-            out_ref[pl.ds(pl.multiple_of(index * 128, 128), 128), :] = rows
-            return carry
-
-        lax.fori_loop(0, 64, cast, 0, unroll=2)
-
-
-def pack(count, offsets, tiles, half):
-    per_step = 8
+            where = pl.ds(slot * 2 + part, 64, stride=STRIDE)
+            rows_ref[where, :] = tile[64 * part : 64 * part + 64]
+        return carry
+
+    for group in range(groups):
+        incoming[group].wait()
+        lax.fori_loop(each * group, each * group + each, one, 0, unroll=8)
+
+    def cast(block, carry):
+        done_ref[block, :128] = rows_ref[pl.ds(block * STRIDE, 128), :].astype(BF16)
+        if half == 0:
+            done_ref[block, 128:] = places
+        return carry
+
+    outgoing = []
+    for group in range(4):
+        lax.fori_loop(16 * group, 16 * group + 16, cast, 0, unroll=4)
+        where = pl.ds(16 * group, 16)
+        copy = pltpu.make_async_copy(done_ref.at[where], out_ref.at[where], out_sems.at[group])
+        copy.start()
+        outgoing.append(copy)
+    for copy in outgoing:
+        copy.wait()
+
+
+def pack(count, bands, offsets, tiles, half):
+    length = 128 if half else 136
+    smem = pl.BlockSpec(memory_space=pltpu.SMEM)
+    anywhere = pl.BlockSpec(memory_space=pl.ANY)
     return pl.pallas_call(
-        functools.partial(pack_kernel, per_step=per_step),
-        grid=(SLOTS // per_step,),
-        in_specs=[
-            pl.BlockSpec(memory_space=pltpu.SMEM),
-            pl.BlockSpec(memory_space=pltpu.SMEM),
-            pl.BlockSpec((per_step, 2, 64, 128), lambda i: (i, 0, half, 0)),
+        functools.partial(pack_kernel, half=half),
+        in_specs=[smem, smem, smem, anywhere],
+        out_specs=anywhere,
+        out_shape=jax.ShapeDtypeStruct((64, length, 128), BF16),
+        scratch_shapes=[
+            pltpu.VMEM((SLOTS, 2, 64, 128), BF16),
+            pltpu.VMEM((64 * STRIDE, 128), F32),
+            pltpu.VMEM((64, length, 128), BF16),
+            pltpu.SemaphoreType.DMA((8,)),
+            pltpu.SemaphoreType.DMA((4,)),
         ],
-        out_specs=pl.BlockSpec((ROWS, 128), lambda i: (0, 0)),
-        out_shape=jax.ShapeDtypeStruct((ROWS, 128), BF16),
-        scratch_shapes=[pltpu.VMEM((64 * STRIDE, 128), F32)],
-        compiler_params=pltpu.CompilerParams(vmem_limit_bytes=VMEM_LIMIT),
+        compiler_params=pltpu.CompilerParams(vmem_limit_bytes=62 * MIB),
         cost_estimate=pl.CostEstimate(flops=8 << 20, bytes_accessed=4 << 20, transcendentals=0),
         name="pack_rows",
-    )(count, offsets, tiles)
+    )(count, bands, offsets, tiles)
 
 
 def grid_kernel(
-    place_ref, me_ref, pieces_ref, first_ref, twiddle_ref, second_ref, bands_ref, out_ref,
-    grid_a, grid_b, rows_ref,
+    place_ref, arrived_ref, first_ref, twiddle_ref, second_ref, bands_ref, out_ref,
+    grid_a, grid_b, rows_ref, pieces_ref, done_ref, in_sem, out_sems,
 ):
+    incoming = pltpu.make_async_copy(arrived_ref.at[:, pl.ds(0, 128), :], pieces_ref, in_sem)
+    incoming.start()
+
     def clear(index, carry):
         where = pl.ds(pl.multiple_of(index * 64, 64), 64)
         grid_a[where, :] = jnp.zeros((64, 128), F32)
@@ -126,21 +167,22 @@
     grid_a[pl.ds(ROWS, 8), :] = jnp.zeros((8, 128), F32)
     grid_b[pl.ds(ROWS, 8), :] = jnp.zeros((8, 128), F32)
 
-    me = me_ref[0]
+    incoming.wait()
     sublane = lax.broadcasted_iota(jnp.int32, (8, 128), 0)
     lane = lax.broadcasted_iota(jnp.int32, (8, 128), 1)
     position = lane + (sublane // 2) * 128
     upper = sublane < 2
 
     def place(index, carry):
-        pieces = pieces_ref[pl.ds(pl.multiple_of(index * 16, 16), 16), :].astype(F32)
-        source = ((index // 8 - me) & 63) * 64 + (index & 7) * 8
+        source = index >> 3
+        slot = (index & 7) * 8
+        pieces = pieces_ref[source, pl.ds(pl.multiple_of(slot * 2, 16), 16), :].astype(F32)
         for part in range(2):
             block = pieces[8 * part : 8 * part + 8]
             turned = [block] + [pltpu.roll(block, 8 - 2 * turn, 0) for turn in (1, 2, 3)]
             for piece in range(4):
                 both = jnp.where(upper, turned[piece], turned[(piece + 3) % 4])
-                packed = place_ref[source + part * 4 + piece]
+                packed = place_ref[source, slot + part * 4 + piece]
                 shift = packed & 127
                 row = packed >> 7
                 offset = position - shift
@@ -150,7 +192,7 @@
                 grid[window, :] = grid[window, :] + jnp.where(inside, both, 0.0)
         return carry
 
-    lax.fori_loop(0, BANDS * SLOTS // 8, place, 0)
+    lax.fori_loop(0, BANDS * SLOTS // 8, place, 0, unroll=4)
 
     first = first_ref[...]
     second = second_ref[...]
@@ -180,49 +222,69 @@
         rows_ref[pl.ds(64 + band, 64, stride=STRIDE), :] = spectrum[64:]
         return carry
 
-    lax.fori_loop(0, BANDS, band_step, 0, unroll=2)
+    lax.fori_loop(0, BANDS, band_step, 0, unroll=4)
 
     table = bands_ref[...]
 
     def block_step(index, carry):
         rows = rows_ref[pl.ds(index * STRIDE, 128), :].astype(BF16)
         section = jnp.dot(table, jnp.concatenate([rows, rows], axis=0), preferred_element_type=F32)
-        out_ref[pl.ds(pl.multiple_of(index * 128, 128), 128), :] = section.astype(BF16)
-        return carry
-
-    lax.fori_loop(0, 64, block_step, 0, unroll=2)
-
-
-def grid_and_rows(places, me, pieces, first, twiddle, second, bands):
+        done_ref[index] = section.astype(BF16)
+        return carry
+
+    outgoing = []
+    for group in range(4):
+        lax.fori_loop(16 * group, 16 * group + 16, block_step, 0, unroll=4)
+        where = pl.ds(16 * group, 16)
+        copy = pltpu.make_async_copy(done_ref.at[where], out_ref.at[where], out_sems.at[group])
+        copy.start()
+        outgoing.append(copy)
+    for copy in outgoing:
+        copy.wait()
+
+
+def grid_and_rows(places, arrived, first, twiddle, second, bands):
     vmem = pl.BlockSpec(memory_space=pltpu.VMEM)
-    smem = pl.BlockSpec(memory_space=pltpu.SMEM)
+    anywhere = pl.BlockSpec(memory_space=pl.ANY)
     return pl.pallas_call(
         grid_kernel,
-        in_specs=[smem, smem, vmem, vmem, vmem, vmem, vmem],
-        out_specs=vmem,
-        out_shape=jax.ShapeDtypeStruct((ROWS, 128), BF16),
+        in_specs=[pl.BlockSpec(memory_space=pltpu.SMEM), anywhere, vmem, vmem, vmem, vmem],
+        out_specs=anywhere,
+        out_shape=jax.ShapeDtypeStruct((64, 128, 128), BF16),
         scratch_shapes=[
             pltpu.VMEM((ROWS + 8, 128), F32),
             pltpu.VMEM((ROWS + 8, 128), F32),
             pltpu.VMEM((64 * STRIDE, 128), F32),
+            pltpu.VMEM((64, 128, 128), BF16),
+            pltpu.VMEM((64, 128, 128), BF16),
+            pltpu.SemaphoreType.DMA,
+            pltpu.SemaphoreType.DMA((4,)),
         ],
-        compiler_params=pltpu.CompilerParams(vmem_limit_bytes=VMEM_LIMIT),
+        compiler_params=pltpu.CompilerParams(vmem_limit_bytes=62 * MIB),
         cost_estimate=pl.CostEstimate(flops=20_000_000_000, bytes_accessed=4 << 20, transcendentals=0),
         name="place_and_transform",
-    )(places, me, pieces, first, twiddle, second, bands)
+    )(places, arrived, first, twiddle, second, bands)
 
 
 def column_kernel(early_ref, late_ref, table_ref, cosine_ref, sine_ref, own_ref, *sent):
     table = table_ref[...]
     count = early_ref.shape[0]
     late = jnp.swapaxes(late_ref[...], 0, 1).reshape(count, 128, 128)
-    for index in range(count):
-        cells = jnp.concatenate([early_ref[index], late[index]], axis=0)
-        sky = jnp.dot(table, jnp.concatenate([cells, cells], axis=0), preferred_element_type=F32)
-        image = sky[:128] * cosine_ref[index] - sky[128:] * sine_ref[index]
-        own_ref[index] = image[:32]
-        for step in range(3):
-            sent[step][index] = image[32 * step + 32 : 32 * step + 64].astype(BF16)
+    for pair in range(0, count, 2):
+        cells = jnp.concatenate(
+            [
+                jnp.concatenate([early_ref[index], late[index]], axis=0)
+                for index in (pair, pair + 1)
+            ],
+            axis=1,
+        )
+        both = jnp.dot(table, jnp.concatenate([cells, cells], axis=0), preferred_element_type=F32)
+        for index in (pair, pair + 1):
+            sky = both[:, 128 * (index - pair) : 128 * (index - pair) + 128]
+            image = sky[:128] * cosine_ref[index] - sky[128:] * sine_ref[index]
+            own_ref[index] = image[:32]
+            for step in range(3):
+                sent[step][index] = image[32 * step + 32 : 32 * step + 64].astype(BF16)
 
 
 def column_transform(early, late, table, cosine, sine, begin, count):
@@ -243,7 +305,7 @@
         out_specs=[result] * 4,
         out_shape=[jax.ShapeDtypeStruct((count, 32, 128), F32)]
         + [jax.ShapeDtypeStruct((count, 32, 128), BF16)] * 3,
-        compiler_params=pltpu.CompilerParams(vmem_limit_bytes=VMEM_LIMIT),
+        compiler_params=pltpu.CompilerParams(vmem_limit_bytes=16 * MIB),
         cost_estimate=pl.CostEstimate(
             flops=count * 70_000_000, bytes_accessed=count * (200 << 10), transcendentals=0
         ),
@@ -272,7 +334,7 @@
         in_specs=[vmem] * len(flat),
         out_specs=vmem,
         out_shape=jax.ShapeDtypeStruct((32, 64, 128), F32),
-        compiler_params=pltpu.CompilerParams(vmem_limit_bytes=VMEM_LIMIT),
+        compiler_params=pltpu.CompilerParams(vmem_limit_bytes=16 * MIB),
         cost_estimate=pl.CostEstimate(flops=1 << 20, bytes_accessed=3 << 20, transcendentals=0),
         name="window_sum",
     )(*flat)
@@ -298,62 +360,46 @@
     real = jnp.concatenate([cosine, -sine], axis=1)
     imag = jnp.concatenate([sine, cosine], axis=1)
     table = jnp.stack([real, imag], axis=1).reshape(128, 128)
-    high = table.astype(BF16)
-    low = (table - high.astype(F32)).astype(BF16)
-    return jnp.concatenate([high, low], axis=1)
-
-
-def gather_places(place):
-    held = place
-    reach = 1
-    while reach < BANDS:
-        pairs = [(source, (source - reach) % BANDS) for source in range(BANDS)]
-        held = jnp.concatenate([held, lax.ppermute(held, "band", pairs)])
-        reach *= 2
-    return held
+    high = lax.reduce_precision(table, 8, 7)
+    low = lax.reduce_precision(table - high, 8, 7)
+    return jnp.concatenate([high, low], axis=1).astype(BF16)
 
 
 def local(uv_tiles, target_bands, uv_offsets, tile_counts, plane_w):
-    tiles = uv_tiles[0]
-    offsets = uv_offsets[0]
     me = lax.axis_index("band")
     turn = lax.axis_index("wp")
-    column = offsets[:, 1]
-    place = (target_bands[0, :, 0] * 64 + column // 128) * 256 + column % 128
-    places = gather_places(place)
-
     first = jnp.asarray(row_first_table())
     twiddle = jnp.asarray(row_twiddles())
     second = jnp.asarray(row_second_table())
 
     arrived = []
     for half in range(2):
-        packed = pack(tile_counts, offsets, tiles, half)
+        packed = pack(tile_counts, target_bands[0].T, uv_offsets[0].T, uv_tiles[0], half)
         arrived.append(
-            lax.all_to_all(
-                packed.reshape(64, 128, 128), "band", split_axis=0, concat_axis=0, tiled=True
-            ).reshape(ROWS, 128)
-        )
+            lax.all_to_all(packed, "band", split_axis=0, concat_axis=0, tiled=True)
+        )
+    numbers = arrived[0][:, 128:131, :64].astype(jnp.int32)
+    places = (numbers[:, 0] * 64 + numbers[:, 1]) * 256 + numbers[:, 2]
     columns = []
     for half in range(2):
         spectrum = grid_and_rows(
-            places, me[None], arrived[half], first, twiddle, second, band_table(me + 64 * half)
+            places, arrived[half], first, twiddle, second, band_table(me + 64 * half)
         )
         columns.append(
-            lax.all_to_all(
-                spectrum.reshape(64, 128, 128), "band", split_axis=0, concat_axis=0, tiled=True
-            )
+            lax.all_to_all(spectrum, "band", split_axis=0, concat_axis=0, tiled=True)
         )
     early = jnp.swapaxes(columns[0], 0, 1).reshape(64, 128, 128)
 
     cosine, sine = w_phases(plane_w[0], turn)
     table = jnp.roll(jnp.asarray(column_second_table()).reshape(2, 128, 512), -32 * turn, axis=1)
     table = table.reshape(256, 512)
-    counts = (32, 32)
+    counts = (24, 40)
     parts = []
     begin = 0
+    late = columns[1]
     for count in counts:
-        own, *sent = column_transform(early, columns[1], table, cosine, sine, begin, count)
+        own, *sent = column_transform(early, late, table, cosine, sine, begin, count)
+        late, own = lax.optimization_barrier((late, own))
         moved = [
             lax.ppermute(block, "wp", [(plane, (plane + step + 1) % 4) for plane in range(4)])
             for step, block in enumerate(sent)

time: 370 us -> 283 us (0.76)
  Pallas kernels: 127 us -> 79.6 us
  starting transfers between devices: 72.1 us -> 41.8 us
  waiting for transfers between devices: 134 us -> 124 us
    ppermute x6 -> x0, waiting for transfers between devices: 50.6 us -> none  [gather_places(): held = jnp.concatenate([held, lax.ppermute(held, 'band', pairs)])]
    pallas_call x4, Pallas kernels: 113 us -> 74.3 us  [the longest x2 65.6 us: grid_and_rows(): pl.pallas_call(grid_kernel, in_specs=[pl.BlockSpec(memory_space=pltpu.SME...]
    all_to_all x4, waiting for transfers between devices: 70.1 us -> 105 us  [the longest x2 62.7 us: local(): lax.all_to_all(packed, 'band', split_axis=0, concat_axis=0, tiled=True)]
    ppermute x6 -> x0, starting transfers between devices: 16.8 us -> none  [gather_places(): held = jnp.concatenate([held, lax.ppermute(held, 'band', pairs)])]
    all_to_all x4, starting transfers between devices: 47.6 us -> 33.8 us  [the longest x2 19.4 us: local(): lax.all_to_all(packed, 'band', split_axis=0, concat_axis=0, tiled=True)]
    pallas_call x2, Pallas kernels: 11.8 us -> 4.02 us  [column_transform(): pl.pallas_call(column_kernel, grid=(count // per_step,), in_specs=[block,...]
    ppermute x6, waiting for transfers between devices: 12.9 us -> 19.3 us  [local(): lax.ppermute(block, 'wp', [(plane, (plane + step + 1) % 4) for plane in r...]
  transfers between devices with their start and end apart: 16 -> 10, of which waited for: 13 -> 6; matrix products, arithmetic and copies ran while one was open for 7% -> 9% of each run, Pallas kernels for 30% -> 26%
where the time goes in v3:
time: 283 us; the launch traced here: 280 us
  waiting for transfers between devices  124 us (44%)
  Pallas kernels  79.6 us (28%)
  starting transfers between devices  41.8 us (15%)
  other arithmetic  22 us (8%)
  local copies, waits for them, and re-layouts  10.3 us (4%)
    pallas_call x2, Pallas kernels, grid_and_rows(): pl.pallas_call(grid_kernel, in_specs=[pl.BlockSpec(memory_space=pltpu.SME...  65.6 us
    all_to_all x2, waiting for transfers between devices, local(): lax.all_to_all(packed, 'band', split_axis=0, concat_axis=0, tiled=True)  62.7 us
    all_to_all x2, waiting for transfers between devices, local(): lax.all_to_all(spectrum, 'band', split_axis=0, concat_axis=0, tiled=True)  42.4 us
    all_to_all x2, starting transfers between devices, local(): lax.all_to_all(packed, 'band', split_axis=0, concat_axis=0, tiled=True)  19.4 us
    ppermute x6, waiting for transfers between devices, local(): lax.ppermute(block, 'wp', [(plane, (plane + step + 1) % 4) for plane in r...  19.3 us
    sin x1, other arithmetic, w_phases(): return (jnp.cos(angle), jnp.sin(angle))  18.5 us
    all_to_all x2, starting transfers between devices, local(): lax.all_to_all(spectrum, 'band', split_axis=0, concat_axis=0, tiled=True)  14.5 us
    pallas_call x2, Pallas kernels, pack(): pl.pallas_call(functools.partial(pack_kernel, half=half), in_specs=[smem,...  8.63 us
  transfers between devices with their start and end apart: 10, of which 6 were waited for; matrix products, arithmetic and copies ran while one was open for 9% of the time, Pallas kernels for 26%

profile of v3, /device:TPU:33, one launch (start us, length us, event | category | flops | bytes accessed | tf_op | source)
XLA Modules:
  0.0 279.8 jit_solution(3128845085263416489)
XLA Ops:
  0.7 4.3 %pack_rows.2 = bf16[64,136,128]{2,1,0:T(8,128)(2,1)} custom-call(s32[1,1]{1,0:T(1,128)S(6)} %copy.13.count_ref, s32[1,64]{1,0:T(1,128)} %bitcast.35, s32[2,64]{1,0:T(2,128)} %bitcast.33, bf16[64,2,128,128]{3,2,1,0:T(8,128)(2,1)} %bitcast.25), custom_call_target="tpu_custom_call" | custom-call | flops 8388608 | bytes 4194304 | tf_op jit(solution)/shard_map/pack_rows/pallas_call | solution.py:135
  5.0 12.1 %all-to-all-start = ((bf16[64,136,128]{2,1,0:T(8,128)(2,1)}), bf16[64,136,128]{2,1,0:T(8,128)(2,1)}, u32[]{:S(2)}, u32[]{:S(2)}) async-start(bf16[64,136,128]{2,1,0:T(8,128)(2,1)} %pack_rows.2), calls=%async_computation | async-start | bytes 4456448 | tf_op jit(solution)/shard_map/all_to_all | solution.py:379
  17.1 4.3 %pack_rows.3 = bf16[64,128,128]{2,1,0:T(8,128)(2,1)} custom-call(s32[1,1]{1,0:T(1,128)S(6)} %copy.13.count_ref, s32[1,64]{1,0:T(1,128)} %bitcast.36, s32[2,64]{1,0:T(2,128)} %bitcast.34, bf16[64,2,128,128]{3,2,1,0:T(8,128)(2,1)} %bitcast.26), custom_call_target="tpu_custom_call" | custom-call | flops 8388608 | bytes 4194304 | tf_op jit(solution)/shard_map/pack_rows/pallas_call | solution.py:135
  21.4 48.3 %all-to-all-done.arrived_ref = bf16[64,136,128]{2,1,0:T(8,128)(2,1)} async-done(((bf16[64,136,128]{2,1,0:T(8,128)(2,1)}), bf16[64,136,128]{2,1,0:T(8,128)(2,1)}, u32[]{:S(2)}, u32[]{:S(2)}) %all-to-all-start) | async-done | bytes 2228256 | tf_op jit(solution)/shard_map/all_to_all | solution.py:379
  69.7 7.3 %all-to-all-start.1 = ((bf16[64,128,128]{2,1,0:T(8,128)(2,1)}), bf16[64,128,128]{2,1,0:T(8,128)(2,1)}, u32[]{:S(2)}, u32[]{:S(2)}) async-start(bf16[64,128,128]{2,1,0:T(8,128)(2,1)} %pack_rows.3), calls=%async_computation.1 | async-start | bytes 4194304 | tf_op jit(solution)/shard_map/all_to_all | solution.py:379
  77.1 0.1 fusion.24
  77.2 0.1 pad_maximum_fusion.4
  77.3 0.1 pad_maximum_fusion.2
  77.4 0.6 pad_maximum_fusion.3.bands_ref
  78.0 0.9 slice_convert_fusion
  79.0 0.7 slice_add_fusion
  79.7 32.8 %place_and_transform.3 = bf16[64,128,128]{2,1,0:T(8,128)(2,1)} custom-call(s32[64,64]{1,0:T(8,128)} %bitcast.31, bf16[64,136,128]{2,1,0:T(8,128)(2,1)} %all-to-all-done.arrived_ref, bf16[128,384]{1,0:T(8,128)(2,1)} %constant.97.clone.first_ref, f32[2,128,128]{2,1,0:T(8,128)} %constant.98.clone.twiddle_ref, bf16[256,256]{1,0:T(8,128)(2,1)} %constant.99.clone.second_ref, ...), custom_call_target="tpu_custom_call" | custom-call | flops 20000000000 | bytes 4194304 | tf_op jit(solution)/shard_map/place_and_transform/pallas_call | solution.py:249
  112.5 14.4 %all-to-all-done.1.arrived_ref = bf16[64,128,128]{2,1,0:T(8,128)(2,1)} async-done(((bf16[64,128,128]{2,1,0:T(8,128)(2,1)}), bf16[64,128,128]{2,1,0:T(8,128)(2,1)}, u32[]{:S(2)}, u32[]{:S(2)}) %all-to-all-start.1) | async-done | bytes 2097184 | tf_op jit(solution)/shard_map/all_to_all | solution.py:379
  126.9 7.3 %all-to-all-start.3 = ((bf16[64,128,128]{2,1,0:T(8,128)(2,1)}), bf16[64,128,128]{2,1,0:T(8,128)(2,1)}, u32[]{:S(2)}, u32[]{:S(2)}) async-start(bf16[64,128,128]{2,1,0:T(8,128)(2,1)} %place_and_transform.3), calls=%async_computation.3 | async-start | bytes 4194304 | tf_op jit(solution)/shard_map/all_to_all | solution.py:389
  134.2 0.1 fusion.23
  134.4 0.1 maximum_bitcast_fusion
  134.5 0.1 copy.10
  134.6 0.6 pad_maximum_fusion.1.bands_ref
  135.2 32.8 %place_and_transform.2 = bf16[64,128,128]{2,1,0:T(8,128)(2,1)} custom-call(s32[64,64]{1,0:T(8,128)} %bitcast.32, bf16[64,128,128]{2,1,0:T(8,128)(2,1)} %all-to-all-done.1.arrived_ref, bf16[128,384]{1,0:T(8,128)(2,1)} %constant.97.clone.first_ref, f32[2,128,128]{2,1,0:T(8,128)} %constant.98.clone.twiddle_ref, bf16[256,256]{1,0:T(8,128)(2,1)} %constant.99.clone.second_ref, ...), custom_call_target="tpu_custom_call" | custom-call | flops 20000000000 | bytes 4194304 | tf_op jit(solution)/shard_map/place_and_transform/pallas_call | solution.py:249
  168.0 0.0 copy-start.3
  168.1 16.0 %all-to-all-done.3 = bf16[64,128,128]{2,1,0:T(8,128)(2,1)} async-done(((bf16[64,128,128]{2,1,0:T(8,128)(2,1)}), bf16[64,128,128]{2,1,0:T(8,128)(2,1)}, u32[]{:S(2)}, u32[]{:S(2)}) %all-to-all-start.3) | async-done | bytes 2097184 | tf_op jit(solution)/shard_map/all_to_all | solution.py:389
  184.1 7.1 %all-to-all-start.2 = ((bf16[64,128,128]{2,1,0:T(8,128)(2,1)}), bf16[64,128,128]{2,1,0:T(8,128)(2,1)S(1)}, u32[]{:S(2)}, u32[]{:S(2)}) async-start(bf16[64,128,128]{2,1,0:T(8,128)(2,1)} %place_and_transform.2), calls=%async_computation.2 | async-start | bytes 4194304 | tf_op jit(solution)/shard_map/all_to_all | solution.py:389
  191.9 0.0 copy-done.3
  192.0 18.5 %fusion = (f32[64,128,128]{2,1,0:T(8,128)}, f32[64,128,128]{2,1,0:T(8,128)}) fusion(f32[128]{0:T(128)S(1)} %multiply_multiply_fusion.1, f32[64,128]{1,0:T(8,128)S(1)} %multiply_multiply_fusion, f32[]{:T(128)} %bitcast.16), kind=kLoop, calls=%fused_computation.1 | loop fusion | flops 4194304 | bytes 8421892 | tf_op jit(solution)/shard_map/sin | solution.py:351
  210.5 4.3 %copy.12 = bf16[128,64,128]{2,1,0:T(8,128)(2,1)} copy(bf16[128,64,128]{2,0,1:T(8,128)(2,1)} %bitcast.13) | data formatting | bytes 4194304 | tf_op jit(solution)/shard_map/transpose | solution.py:391
  214.7 26.4 %all-to-all-done.2.late_ref = bf16[64,128,128]{2,1,0:T(8,128)(2,1)S(1)} async-done(((bf16[64,128,128]{2,1,0:T(8,128)(2,1)}), bf16[64,128,128]{2,1,0:T(8,128)(2,1)S(1)}, u32[]{:S(2)}, u32[]{:S(2)}) %all-to-all-start.2) | async-done | bytes 2097184 | tf_op jit(solution)/shard_map/all_to_all | solution.py:389
  241.1 0.0 copy-start
  241.1 2.2 copy-done
  243.3 0.0 copy-start.1
  243.3 2.2 copy-done.1
  245.5 0.0 copy-start.2
  245.5 1.6 copy-done.2
  247.1 1.5 column_transform.2
  248.6 1.4 collective-permute-start
  250.0 2.5 column_transform.3
  252.5 1.4 collective-permute-start.3
  253.9 1.4 collective-permute-start.4
  255.3 2.0 collective-permute-start.5
  257.2 0.4 collective-permute-start.1
  257.6 0.0 collective-permute-done.refs_1_
  257.6 1.5 collective-permute-start.2
  259.1 16.5 %collective-permute-done.1.refs_2_ = bf16[24,32,128]{2,1,0:T(8,128)(2,1)S(1)} collective-permute-done((bf16[24,32,128]{2,1,0:T(8,128)(2,1)S(1)}, bf16[24,32,128]{2,1,0:T(8,128)(2,1)S(1)}, u32[]{:S(2)}, u32[]{:S(2)}) %collective-permute-start.1) | collective-permute-done | bytes 196640 | tf_op jit(solution)/shard_map/ppermute | solution.py:404
  275.6 2.8 collective-permute-done.2.refs_3_
  278.4 0.0 collective-permute-done.3.refs_5_
  278.4 0.0 collective-permute-done.4.refs_6_
  278.4 0.0 collective-permute-done.5.refs_7_
  278.4 1.4 window_sum.1
  (9 shorter events, 0.1 us)
Async XLA Ops:
  5.0 64.8 %all-to-all-start = ((bf16[64,136,128]{2,1,0:T(8,128)(2,1)}), bf16[64,136,128]{2,1,0:T(8,128)(2,1)}, u32[]{:S(2)}, u32[]{:S(2)}) async-start(bf16[64,136,128]{2,1,0:T(8,128)(2,1)} %pack_rows.2), calls=%async_computation | async-start | bytes 4456448 | tf_op jit(solution)/shard_map/all_to_all | solution.py:379
  69.7 57.2 %all-to-all-start.1 = ((bf16[64,128,128]{2,1,0:T(8,128)(2,1)}), bf16[64,128,128]{2,1,0:T(8,128)(2,1)}, u32[]{:S(2)}, u32[]{:S(2)}) async-start(bf16[64,128,128]{2,1,0:T(8,128)(2,1)} %pack_rows.3), calls=%async_computation.1 | async-start | bytes 4194304 | tf_op jit(solution)/shard_map/all_to_all | solution.py:379
  126.9 57.2 %all-to-all-start.3 = ((bf16[64,128,128]{2,1,0:T(8,128)(2,1)}), bf16[64,128,128]{2,1,0:T(8,128)(2,1)}, u32[]{:S(2)}, u32[]{:S(2)}) async-start(bf16[64,128,128]{2,1,0:T(8,128)(2,1)} %place_and_transform.3), calls=%async_computation.3 | async-start | bytes 4194304 | tf_op jit(solution)/shard_map/all_to_all | solution.py:389
  168.0 23.9 %copy-start.3 = (bf16[2,256,512]{2,1,0:T(8,128)(2,1)S(1)}, bf16[2,256,512]{2,1,0:T(8,128)(2,1)}, u32[]{:S(2)}) copy-start(bf16[2,256,512]{2,1,0:T(8,128)(2,1)} %constant.107) | copy-start | bytes 1572868
  184.1 57.1 %all-to-all-start.2 = ((bf16[64,128,128]{2,1,0:T(8,128)(2,1)}), bf16[64,128,128]{2,1,0:T(8,128)(2,1)S(1)}, u32[]{:S(2)}, u32[]{:S(2)}) async-start(bf16[64,128,128]{2,1,0:T(8,128)(2,1)} %place_and_transform.2), calls=%async_computation.2 | async-start | bytes 4194304 | tf_op jit(solution)/shard_map/all_to_all | solution.py:389
  241.1 2.2 copy-start
  243.3 2.2 copy-start.1
  245.5 1.6 copy-start.2
  248.6 9.0 %collective-permute-start = (bf16[24,32,128]{2,1,0:T(8,128)(2,1)S(1)}, bf16[24,32,128]{2,1,0:T(8,128)(2,1)S(1)}, u32[]{:S(2)}, u32[]{:S(2)}) collective-permute-start(bf16[24,32,128]{2,1,0:T(8,128)(2,1)S(1)} %get-tuple-element.18), channel_id=1, source_target_pairs={{0,1},{1,2},{2,3},{3,0},{4,5},{5,6},{6,7},{7,4},{8,9},{9,10},{10,1... | collective-permute-start | bytes 589832 | tf_op jit(solution)/shard_map/ppermute | solution.py:404
  252.5 25.9 %collective-permute-start.3 = (bf16[40,32,128]{2,1,0:T(8,128)(2,1)S(1)}, bf16[40,32,128]{2,1,0:T(8,128)(2,1)S(1)}, u32[]{:S(2)}, u32[]{:S(2)}) collective-permute-start(bf16[40,32,128]{2,1,0:T(8,128)(2,1)S(1)} %get-tuple-element.24), channel_id=1, source_target_pairs={{0,1},{1,2},{2,3},{3,0},{4,5},{5,6},{6,7},{7,4},{8,9},{9,10},{10,1... | collective-permute-start | bytes 983048 | tf_op jit(solution)/shard_map/ppermute | solution.py:404
  253.9 24.6 %collective-permute-start.4 = (bf16[40,32,128]{2,1,0:T(8,128)(2,1)S(1)}, bf16[40,32,128]{2,1,0:T(8,128)(2,1)S(1)}, u32[]{:S(2)}, u32[]{:S(2)}) collective-permute-start(bf16[40,32,128]{2,1,0:T(8,128)(2,1)S(1)} %get-tuple-element.25), channel_id=1, source_target_pairs={{0,2},{1,3},{2,0},{3,1},{4,6},{5,7},{6,4},{7,5},{8,10},{9,11},{10,... | collective-permute-start | bytes 983048 | tf_op jit(solution)/shard_map/ppermute | solution.py:404
  255.3 23.2 %collective-permute-start.5 = (bf16[40,32,128]{2,1,0:T(8,128)(2,1)S(1)}, bf16[40,32,128]{2,1,0:T(8,128)(2,1)S(1)}, u32[]{:S(2)}, u32[]{:S(2)}) collective-permute-start(bf16[40,32,128]{2,1,0:T(8,128)(2,1)S(1)} %get-tuple-element.26), channel_id=1, source_target_pairs={{0,3},{1,0},{2,1},{3,2},{4,7},{5,4},{6,5},{7,6},{8,11},{9,8},{10,9... | collective-permute-start | bytes 983048 | tf_op jit(solution)/shard_map/ppermute | solution.py:404
  257.2 18.4 %collective-permute-start.1 = (bf16[24,32,128]{2,1,0:T(8,128)(2,1)S(1)}, bf16[24,32,128]{2,1,0:T(8,128)(2,1)S(1)}, u32[]{:S(2)}, u32[]{:S(2)}) collective-permute-start(bf16[24,32,128]{2,1,0:T(8,128)(2,1)S(1)} %get-tuple-element.19), channel_id=1, source_target_pairs={{0,2},{1,3},{2,0},{3,1},{4,6},{5,7},{6,4},{7,5},{8,10},{9,11},{10,... | collective-permute-start | bytes 589832 | tf_op jit(solution)/shard_map/ppermute | solution.py:404
  257.6 20.8 %collective-permute-start.2 = (bf16[24,32,128]{2,1,0:T(8,128)(2,1)S(1)}, bf16[24,32,128]{2,1,0:T(8,128)(2,1)S(1)}, u32[]{:S(2)}, u32[]{:S(2)}) collective-permute-start(bf16[24,32,128]{2,1,0:T(8,128)(2,1)S(1)} %get-tuple-element.20), channel_id=1, source_target_pairs={{0,3},{1,0},{2,1},{3,2},{4,7},{5,4},{6,5},{7,6},{8,11},{9,8},{10,9... | collective-permute-start | bytes 589832 | tf_op jit(solution)/shard_map/ppermute | solution.py:404

commit v4 on v3

--- a/solution.py
+++ b/solution.py
@@ -229,34 +229,40 @@
     def block_step(index, carry):
         rows = rows_ref[pl.ds(index * STRIDE, 128), :].astype(BF16)
         section = jnp.dot(table, jnp.concatenate([rows, rows], axis=0), preferred_element_type=F32)
-        done_ref[index] = section.astype(BF16)
+        section = section.astype(BF16)
+        parts, _, length, _ = done_ref.shape
+        for part in range(parts):
+            done_ref[part, index] = section[length * part : length * part + length]
         return carry
 
     outgoing = []
     for group in range(4):
         lax.fori_loop(16 * group, 16 * group + 16, block_step, 0, unroll=4)
         where = pl.ds(16 * group, 16)
-        copy = pltpu.make_async_copy(done_ref.at[where], out_ref.at[where], out_sems.at[group])
+        copy = pltpu.make_async_copy(
+            done_ref.at[:, where], out_ref.at[:, where], out_sems.at[group]
+        )
         copy.start()
         outgoing.append(copy)
     for copy in outgoing:
         copy.wait()
 
 
-def grid_and_rows(places, arrived, first, twiddle, second, bands):
+def grid_and_rows(places, arrived, first, twiddle, second, bands, parts):
+    shape = (parts, 64, 128 // parts, 128)
     vmem = pl.BlockSpec(memory_space=pltpu.VMEM)
     anywhere = pl.BlockSpec(memory_space=pl.ANY)
     return pl.pallas_call(
         grid_kernel,
         in_specs=[pl.BlockSpec(memory_space=pltpu.SMEM), anywhere, vmem, vmem, vmem, vmem],
         out_specs=anywhere,
-        out_shape=jax.ShapeDtypeStruct((64, 128, 128), BF16),
+        out_shape=jax.ShapeDtypeStruct(shape, BF16),
         scratch_shapes=[
             pltpu.VMEM((ROWS + 8, 128), F32),
             pltpu.VMEM((ROWS + 8, 128), F32),
             pltpu.VMEM((64 * STRIDE, 128), F32),
             pltpu.VMEM((64, 128, 128), BF16),
-            pltpu.VMEM((64, 128, 128), BF16),
+            pltpu.VMEM(shape, BF16),
             pltpu.SemaphoreType.DMA,
             pltpu.SemaphoreType.DMA((4,)),
         ],
@@ -266,89 +272,141 @@
     )(places, arrived, first, twiddle, second, bands)
 
 
-def column_kernel(early_ref, late_ref, table_ref, cosine_ref, sine_ref, own_ref, *sent):
+def deal_kernel(turn_ref, columns_ref, *out_refs):
+    for step, out_ref in enumerate(out_refs):
+        begin = ((turn_ref[0] + step) & 3) * 32
+        for group in range(2):
+            where = pl.ds(pl.multiple_of(begin + 16 * group, 16), 16)
+            rows = jnp.swapaxes(columns_ref[:, where, :], 0, 1).reshape(8, 128, 128)
+            out_ref[8 * group : 8 * group + 8] = rows
+
+
+def deal_rows(turn, columns):
+    vmem = pl.BlockSpec(memory_space=pltpu.VMEM)
+    return pl.pallas_call(
+        deal_kernel,
+        in_specs=[pl.BlockSpec(memory_space=pltpu.SMEM), vmem],
+        out_specs=[vmem] * 4,
+        out_shape=[jax.ShapeDtypeStruct((16, 128, 128), BF16)] * 4,
+        compiler_params=pltpu.CompilerParams(vmem_limit_bytes=16 * MIB),
+        cost_estimate=pl.CostEstimate(flops=1 << 20, bytes_accessed=4 << 20, transcendentals=0),
+        name="deal_rows",
+    )(turn, columns)
+
+
+def phase_kernel(turn_ref, me_ref, w_ref, cosine_ref, sine_ref):
+    turn = turn_ref[0]
+    k = 16 * turn + pl.program_id(0)
+    j = (lax.broadcasted_iota(jnp.int32, (128, 128), 0) + 32 * turn) & 127
+    column = lax.broadcasted_iota(jnp.int32, (128, 128), 1) + 128 * me_ref[0]
+    x = ((64 * j + k).astype(F32) - N // 2) / N
+    y = (column.astype(F32) - N // 2) / N
+    term = jnp.sqrt(1.0 - (x * x + y * y)) - 1.0
+    for step in range(4):
+        angle = (2.0 * math.pi * w_ref[step]) * term
+        cosine_ref[step, 0] = jnp.cos(angle)
+        sine_ref[step, 0] = jnp.sin(angle)
+
+
+def phases(turn, me, w):
+    smem = pl.BlockSpec(memory_space=pltpu.SMEM)
+    block = pl.BlockSpec((4, 1, 128, 128), lambda i: (0, i, 0, 0))
+    return pl.pallas_call(
+        phase_kernel,
+        grid=(16,),
+        in_specs=[smem] * 3,
+        out_specs=[block] * 2,
+        out_shape=[jax.ShapeDtypeStruct((4, 16, 128, 128), F32)] * 2,
+        compiler_params=pltpu.CompilerParams(vmem_limit_bytes=16 * MIB),
+        cost_estimate=pl.CostEstimate(flops=200 << 20, bytes_accessed=8 << 20, transcendentals=2 << 20),
+        name="w_phases",
+    )(turn, me, w)
+
+
+def column_kernel(
+    turn_ref, early_0, early_1, early_2, early_3, late_ref, table_ref, cosine_ref, sine_ref,
+    own_ref, *sent
+):
     table = table_ref[...]
-    count = early_ref.shape[0]
-    late = jnp.swapaxes(late_ref[...], 0, 1).reshape(count, 128, 128)
-    for pair in range(0, count, 2):
-        cells = jnp.concatenate(
-            [
-                jnp.concatenate([early_ref[index], late[index]], axis=0)
-                for index in (pair, pair + 1)
-            ],
-            axis=1,
-        )
-        both = jnp.dot(table, jnp.concatenate([cells, cells], axis=0), preferred_element_type=F32)
-        for index in (pair, pair + 1):
-            sky = both[:, 128 * (index - pair) : 128 * (index - pair) + 128]
-            image = sky[:128] * cosine_ref[index] - sky[128:] * sine_ref[index]
-            own_ref[index] = image[:32]
-            for step in range(3):
-                sent[step][index] = image[32 * step + 32 : 32 * step + 64].astype(BF16)
-
-
-def column_transform(early, late, table, cosine, sine, begin, count):
-    per_step = 8
-    skip = begin // per_step
-    block = pl.BlockSpec((per_step, 128, 128), lambda i: (i + skip, 0, 0))
-    result = pl.BlockSpec((per_step, 32, 128), lambda i: (i, 0, 0))
+    early = (early_0, early_1, early_2, early_3)
+    count = early_0.shape[0]
+    late = [
+        jnp.swapaxes(late_ref[(turn_ref[0] - step) & 3], 0, 1).reshape(count, 128, 128)
+        for step in range(4)
+    ]
+    for index in range(count):
+        image = jnp.zeros((128, 128), F32)
+        for pair in (0, 2):
+            cells = jnp.concatenate(
+                [
+                    jnp.concatenate([early[step][index], late[step][index]], axis=0)
+                    for step in (pair, pair + 1)
+                ],
+                axis=1,
+            )
+            sky = jnp.dot(
+                table, jnp.concatenate([cells, cells], axis=0), preferred_element_type=F32
+            )
+            for step in (pair, pair + 1):
+                part = sky[:, 128 * (step - pair) : 128 * (step - pair) + 128]
+                image += part[:128] * cosine_ref[step, index] - part[128:] * sine_ref[step, index]
+        own_ref[index] = image[:32]
+        for step in range(3):
+            sent[step][index] = image[32 * step + 32 : 32 * step + 64].astype(BF16)
+
+
+def column_transform(turn, early, late, table, cosine, sine):
+    each = 8
+    block = pl.BlockSpec((each, 128, 128), lambda i: (i, 0, 0))
+    phase = pl.BlockSpec((4, each, 128, 128), lambda i: (0, i, 0, 0))
+    result = pl.BlockSpec((each, 32, 128), lambda i: (i, 0, 0))
     return pl.pallas_call(
         column_kernel,
-        grid=(count // per_step,),
-        in_specs=[
-            block,
-            pl.BlockSpec((64, 2 * per_step, 128), lambda i: (0, i + skip, 0)),
+        grid=(16 // each,),
+        in_specs=[pl.BlockSpec(memory_space=pltpu.SMEM)]
+        + [block] * 4
+        + [
+            pl.BlockSpec((4, 64, 2 * each, 128), lambda i: (0, 0, i, 0)),
             pl.BlockSpec((256, 512), lambda i: (0, 0)),
-            block,
-            block,
+            phase,
+            phase,
         ],
         out_specs=[result] * 4,
-        out_shape=[jax.ShapeDtypeStruct((count, 32, 128), F32)]
-        + [jax.ShapeDtypeStruct((count, 32, 128), BF16)] * 3,
-        compiler_params=pltpu.CompilerParams(vmem_limit_bytes=16 * MIB),
+        out_shape=[jax.ShapeDtypeStruct((16, 32, 128), F32)]
+        + [jax.ShapeDtypeStruct((16, 32, 128), BF16)] * 3,
+        compiler_params=pltpu.CompilerParams(vmem_limit_bytes=24 * MIB),
         cost_estimate=pl.CostEstimate(
-            flops=count * 70_000_000, bytes_accessed=count * (200 << 10), transcendentals=0
+            flops=4_300_000_000, bytes_accessed=13 << 20, transcendentals=0
         ),
         name="column_transform",
-    )(early, late, table, cosine, sine)
-
-
-def sum_kernel(*refs, counts):
+    )(turn, *early, late, table, cosine, sine)
+
+
+def place_kernel(turn_ref, *refs):
     out_ref = refs[-1]
-    begin = 0
-    for part, count in enumerate(counts):
-        own, *others = refs[4 * part : 4 * part + 4]
-        for group in range(0, count, 8):
-            total = own[group : group + 8]
-            for other in others:
-                total = total + other[group : group + 8].astype(F32)
-            out_ref[:, begin + group : begin + group + 8, :] = jnp.swapaxes(total, 0, 1)
-        begin += count
-
-
-def window_sum(parts, counts):
+    for step, block_ref in enumerate(refs[:-1]):
+        begin = ((turn_ref[0] - step) & 3) * 16
+        for group in (0, 8):
+            rows = jnp.swapaxes(block_ref[group : group + 8].astype(F32), 0, 1)
+            out_ref[:, pl.ds(pl.multiple_of(begin + group, 8), 8), :] = rows
+
+
+def place_rows(turn, blocks):
     vmem = pl.BlockSpec(memory_space=pltpu.VMEM)
-    flat = [block for part in parts for block in part]
-    return pl.pallas_call(
-        functools.partial(sum_kernel, counts=counts),
-        in_specs=[vmem] * len(flat),
+    return pl.pallas_call(
+        place_kernel,
+        in_specs=[pl.BlockSpec(memory_space=pltpu.SMEM)] + [vmem] * 4,
         out_specs=vmem,
         out_shape=jax.ShapeDtypeStruct((32, 64, 128), F32),
         compiler_params=pltpu.CompilerParams(vmem_limit_bytes=16 * MIB),
-        cost_estimate=pl.CostEstimate(flops=1 << 20, bytes_accessed=3 << 20, transcendentals=0),
-        name="window_sum",
-    )(*flat)
-
-
-def w_phases(plane_w, turn):
-    k = jnp.arange(64, dtype=jnp.int32)[:, None, None]
-    j = (jnp.arange(128, dtype=jnp.int32)[None, :, None] + 32 * turn) % 128
-    column = lax.axis_index("band") * 128 + jnp.arange(128, dtype=jnp.int32)[None, None, :]
-    x = ((64 * j + k).astype(F32) - N // 2) / N
-    y = (column.astype(F32) - N // 2) / N
-    radius = x**2 + y**2
-    angle = 2.0 * math.pi * plane_w * (jnp.sqrt(1.0 - radius) - 1.0)
-    return jnp.cos(angle), jnp.sin(angle)
+        cost_estimate=pl.CostEstimate(flops=1 << 20, bytes_accessed=2 << 20, transcendentals=0),
+        name="place_image_rows",
+    )(turn, *blocks)
+
+
+def along_wp(block, step):
+    pairs = [(plane, (plane + step) % 4) for plane in range(4)]
+    return lax.ppermute(block, "wp", pairs)
 
 
 def band_table(row):
@@ -380,33 +438,31 @@
         )
     numbers = arrived[0][:, 128:131, :64].astype(jnp.int32)
     places = (numbers[:, 0] * 64 + numbers[:, 1]) * 256 + numbers[:, 2]
-    columns = []
+    early = late = None
     for half in range(2):
         spectrum = grid_and_rows(
-            places, arrived[half], first, twiddle, second, band_table(me + 64 * half)
-        )
-        columns.append(
-            lax.all_to_all(spectrum, "band", split_axis=0, concat_axis=0, tiled=True)
-        )
-    early = jnp.swapaxes(columns[0], 0, 1).reshape(64, 128, 128)
-
-    cosine, sine = w_phases(plane_w[0], turn)
-    table = jnp.roll(jnp.asarray(column_second_table()).reshape(2, 128, 512), -32 * turn, axis=1)
-    table = table.reshape(256, 512)
-    counts = (24, 40)
-    parts = []
-    begin = 0
-    late = columns[1]
-    for count in counts:
-        own, *sent = column_transform(early, late, table, cosine, sine, begin, count)
-        late, own = lax.optimization_barrier((late, own))
-        moved = [
-            lax.ppermute(block, "wp", [(plane, (plane + step + 1) % 4) for plane in range(4)])
-            for step, block in enumerate(sent)
-        ]
-        parts.append([own, *moved])
-        begin += count
-    return window_sum(parts, counts).reshape(2048, 128)
+            places, arrived[half], first, twiddle, second, band_table(me + 64 * half), 4 if half else 1
+        )
+        if half == 0:
+            early = lax.all_to_all(
+                spectrum.reshape(64, 128, 128), "band", split_axis=0, concat_axis=0, tiled=True
+            )
+        else:
+            late = lax.all_to_all(
+                spectrum.reshape(256, 32, 128), ("wp", "band"), split_axis=0, concat_axis=0, tiled=True
+            ).reshape(4, 64, 32, 128)
+
+    early, w = lax.optimization_barrier((early, plane_w))
+    w = jnp.concatenate([w, along_wp(w, 1)])
+    w = jnp.concatenate([w, along_wp(w, 2)])
+    turn = turn[None]
+    cosine, sine = phases(turn, me[None], w)
+    dealt = deal_rows(turn, early)
+    dealt = [dealt[0]] + [along_wp(dealt[step], step) for step in (1, 2, 3)]
+    table = jnp.roll(jnp.asarray(column_second_table()).reshape(2, 128, 512), -32 * turn[0], axis=1)
+    own, *sent = column_transform(turn, dealt, late, table.reshape(256, 512), cosine, sine)
+    blocks = [own] + [along_wp(block, step + 1) for step, block in enumerate(sent)]
+    return place_rows(turn, blocks).reshape(2048, 128)
 
 
 def solution(mesh):

time: 283 us -> 287 us (1.014)
  Pallas kernels: 79.6 us -> 99.6 us
  other arithmetic: 22 us -> 4.01 us
  starting transfers between devices: 41.8 us -> 49.8 us
  waiting for transfers between devices: 124 us -> 118 us
    all_to_all x2, waiting for transfers between devices: 42.4 us -> 16 us  [the longest x1 16 us: local(): lax.all_to_all(spectrum.reshape(64, 128, 128), 'band', split_axis=0, conc...]
    ppermute x6 -> x8, waiting for transfers between devices: 19.3 us -> 39.4 us  [along_wp(): return lax.ppermute(block, 'wp', pairs)]
    pallas_call x3 -> x4, Pallas kernels: 5.37 us -> 25.3 us  [the longest x1 17.1 us: phases(): pl.pallas_call(phase_kernel, grid=(16,), in_specs=[smem] * 3, out_specs=[...]
    sin x1 -> x0, other arithmetic: 18.5 us -> none  [w_phases(): return (jnp.cos(angle), jnp.sin(angle))]
    ppermute x6 -> x8, starting transfers between devices: 8 us -> 13.2 us  [along_wp(): return lax.ppermute(block, 'wp', pairs)]
    transpose x1 -> x0, local copies, waits for them, and re-layouts: 4.25 us -> none  [local(): early = jnp.swapaxes(columns[0], 0, 1).reshape(64, 128, 128)]
  transfers between devices with their start and end apart: 10 -> 12, of which waited for: 6 -> 8; matrix products, arithmetic and copies ran while one was open for 9% -> 2% of each run, Pallas kernels for 26% -> 32%
where the time goes in v4:
time: 287 us; the launch traced here: 283 us
  waiting for transfers between devices  118 us (41%)
  Pallas kernels  99.6 us (35%)
  starting transfers between devices  49.8 us (17%)
  local copies, waits for them, and re-layouts  10.3 us (4%)
  other arithmetic  4.01 us (1%)
    pallas_call x2, Pallas kernels, grid_and_rows(): pl.pallas_call(grid_kernel, in_specs=[pl.BlockSpec(memory_space=pltpu.SME...  65.7 us
    all_to_all x2, waiting for transfers between devices, local(): lax.all_to_all(packed, 'band', split_axis=0, concat_axis=0, tiled=True)  62.8 us
    ppermute x8, waiting for transfers between devices, along_wp(): return lax.ppermute(block, 'wp', pairs)  39.4 us
    all_to_all x2, starting transfers between devices, local(): lax.all_to_all(packed, 'band', split_axis=0, concat_axis=0, tiled=True)  19.4 us
    pallas_call x1, Pallas kernels, phases(): pl.pallas_call(phase_kernel, grid=(16,), in_specs=[smem] * 3, out_specs=[...  17.1 us
    all_to_all x1, waiting for transfers between devices, local(): lax.all_to_all(spectrum.reshape(64, 128, 128), 'band', split_axis=0, conc...  16 us
    ppermute x8, starting transfers between devices, along_wp(): return lax.ppermute(block, 'wp', pairs)  13.2 us
    all_to_all x1, starting transfers between devices, local(): lax.all_to_all(spectrum.reshape(256, 32, 128), ('wp', 'band'), split_axis...  9.93 us
  transfers between devices with their start and end apart: 12, of which 8 were waited for; matrix products, arithmetic and copies ran while one was open for 2% of the time, Pallas kernels for 32%

profile of v4, /device:TPU:33, one launch (start us, length us, event | category | flops | bytes accessed | tf_op | source)
XLA Modules:
  0.0 283.4 jit_solution(16021905817911133511)
XLA Ops:
  0.7 4.3 %pack_rows.2 = bf16[64,136,128]{2,1,0:T(8,128)(2,1)} custom-call(s32[1,1]{1,0:T(1,128)S(6)} %copy.19.count_ref, s32[1,64]{1,0:T(1,128)} %bitcast.36, s32[2,64]{1,0:T(2,128)} %bitcast.34, bf16[64,2,128,128]{3,2,1,0:T(8,128)(2,1)} %bitcast.26), custom_call_target="tpu_custom_call" | custom-call | flops 8388608 | bytes 4194304 | tf_op jit(solution)/shard_map/pack_rows/pallas_call | solution.py:135
  5.0 12.1 %all-to-all-start = ((bf16[64,136,128]{2,1,0:T(8,128)(2,1)}), bf16[64,136,128]{2,1,0:T(8,128)(2,1)}, u32[]{:S(2)}, u32[]{:S(2)}) async-start(bf16[64,136,128]{2,1,0:T(8,128)(2,1)} %pack_rows.2), calls=%async_computation | async-start | bytes 4456448 | tf_op jit(solution)/shard_map/all_to_all | solution.py:437
  17.0 4.3 %pack_rows.3 = bf16[64,128,128]{2,1,0:T(8,128)(2,1)} custom-call(s32[1,1]{1,0:T(1,128)S(6)} %copy.19.count_ref, s32[1,64]{1,0:T(1,128)} %bitcast.37, s32[2,64]{1,0:T(2,128)} %bitcast.35, bf16[64,2,128,128]{3,2,1,0:T(8,128)(2,1)} %bitcast.27), custom_call_target="tpu_custom_call" | custom-call | flops 8388608 | bytes 4194304 | tf_op jit(solution)/shard_map/pack_rows/pallas_call | solution.py:135
  21.4 48.3 %all-to-all-done.arrived_ref = bf16[64,136,128]{2,1,0:T(8,128)(2,1)} async-done(((bf16[64,136,128]{2,1,0:T(8,128)(2,1)}), bf16[64,136,128]{2,1,0:T(8,128)(2,1)}, u32[]{:S(2)}, u32[]{:S(2)}) %all-to-all-start) | async-done | bytes 2228256 | tf_op jit(solution)/shard_map/all_to_all | solution.py:437
  69.7 7.3 %all-to-all-start.2 = ((bf16[64,128,128]{2,1,0:T(8,128)(2,1)}), bf16[64,128,128]{2,1,0:T(8,128)(2,1)}, u32[]{:S(2)}, u32[]{:S(2)}) async-start(bf16[64,128,128]{2,1,0:T(8,128)(2,1)} %pack_rows.3), calls=%async_computation.2 | async-start | bytes 4194304 | tf_op jit(solution)/shard_map/all_to_all | solution.py:437
  77.0 0.1 fusion.22
  77.2 0.1 maximum_bitcast_fusion
  77.3 0.1 copy.15
  77.4 0.6 pad_maximum_fusion.1.bands_ref
  78.0 0.9 slice.16
  79.0 0.6 fusion.10.place_ref
  79.6 32.8 %place_and_transform.2 = bf16[1,64,128,128]{3,2,1,0:T(8,128)(2,1)} custom-call(s32[64,64]{1,0:T(8,128)} %fusion.10.place_ref, bf16[64,136,128]{2,1,0:T(8,128)(2,1)} %all-to-all-done.arrived_ref, bf16[128,384]{1,0:T(8,128)(2,1)} %constant.68.clone.first_ref, f32[2,128,128]{2,1,0:T(8,128)} %constant.69.clone.twiddle_ref, ...), custom_call_target="tpu_custom_call" | custom-call | flops 20000000000 | bytes 4194304 | tf_op jit(solution)/shard_map/place_and_transform/pallas_call | solution.py:255
  112.4 14.4 %all-to-all-done.2.arrived_ref = bf16[64,128,128]{2,1,0:T(8,128)(2,1)} async-done(((bf16[64,128,128]{2,1,0:T(8,128)(2,1)}), bf16[64,128,128]{2,1,0:T(8,128)(2,1)}, u32[]{:S(2)}, u32[]{:S(2)}) %all-to-all-start.2) | async-done | bytes 2097184 | tf_op jit(solution)/shard_map/all_to_all | solution.py:437
  126.9 7.3 %all-to-all-start.1 = ((bf16[64,128,128]{2,1,0:T(8,128)(2,1)}), bf16[64,128,128]{2,1,0:T(8,128)(2,1)}, u32[]{:S(2)}, u32[]{:S(2)}) async-start(bf16[64,128,128]{2,1,0:T(8,128)(2,1)} %bitcast.29), calls=%async_computation.1 | async-start | bytes 4194304 | tf_op jit(solution)/shard_map/all_to_all | solution.py:447
  134.2 0.1 fusion.23
  134.4 0.1 pad_maximum_fusion.4
  134.5 0.1 pad_maximum_fusion.2
  134.6 0.6 pad_maximum_fusion.3.bands_ref
  135.2 32.9 %place_and_transform.3 = bf16[4,64,32,128]{3,2,1,0:T(8,128)(2,1)} custom-call(s32[64,64]{1,0:T(8,128)} %fusion.10.place_ref, bf16[64,128,128]{2,1,0:T(8,128)(2,1)} %all-to-all-done.2.arrived_ref, bf16[128,384]{1,0:T(8,128)(2,1)} %constant.68.clone.first_ref, f32[2,128,128]{2,1,0:T(8,128)} %constant.69.clone.twiddle_ref, ...), custom_call_target="tpu_custom_call" | custom-call | flops 20000000000 | bytes 4194304 | tf_op jit(solution)/shard_map/place_and_transform/pallas_call | solution.py:255
  168.1 16.0 %all-to-all-done.1.columns_ref = bf16[64,128,128]{2,1,0:T(8,128)(2,1)} async-done(((bf16[64,128,128]{2,1,0:T(8,128)(2,1)}), bf16[64,128,128]{2,1,0:T(8,128)(2,1)}, u32[]{:S(2)}, u32[]{:S(2)}) %all-to-all-start.1) | async-done | bytes 2097184 | tf_op jit(solution)/shard_map/all_to_all | solution.py:447
  184.0 9.9 %all-to-all-start.3 = ((bf16[256,32,128]{2,1,0:T(8,128)(2,1)}), bf16[256,32,128]{2,1,0:T(8,128)(2,1)S(1)}, u32[]{:S(2)}, u32[]{:S(2)}) async-start(bf16[256,32,128]{2,1,0:T(8,128)(2,1)} %bitcast.28), calls=%async_computation.3 | async-start | bytes 4194304 | tf_op jit(solution)/shard_map/all_to_all | solution.py:451
  194.0 3.1 %deal_rows.1 = (bf16[16,128,128]{2,1,0:T(8,128)(2,1)S(1)}, bf16[16,128,128]{2,1,0:T(8,128)(2,1)}, bf16[16,128,128]{2,1,0:T(8,128)(2,1)}, bf16[16,128,128]{2,1,0:T(8,128)(2,1)}) custom-call(s32[1]{0:T(128)} %bitcast.turn_ref, bf16[64,128,128]{2,1,0:T(8,128)(2,1)} %all-to-all-done.1.columns_ref), custom_call_target="tpu_custom_call" | custom-call | flops 1048576 | bytes 4194304 | tf_op jit(solution)/shard_map/deal_rows/pallas_call | solution.py:286
  197.1 1.3 collective-permute-start
  198.3 2.5 collective-permute-start.1
  200.8 1.1 collective-permute-start.2
  202.6 1.0 constant_dynamic-slice_fusion
  203.6 0.4 collective-permute-start.3
  204.0 32.8 %collective-permute-done.3 = f32[1]{0:T(128)} collective-permute-done((f32[1]{0:T(128)}, f32[1]{0:T(128)}, u32[]{:S(2)}, u32[]{:S(2)}) %collective-permute-start.3) | collective-permute-done | bytes 36 | tf_op jit(solution)/shard_map/ppermute | solution.py:409
  236.8 0.8 pad_maximum_fusion.6
  237.6 2.6 collective-permute-start.4
  240.2 1.6 collective-permute-done.4
  241.8 0.8 pad_maximum_fusion.7.w_ref
  242.6 17.1 %w_phases.1 = (f32[4,16,128,128]{3,2,1,0:T(8,128)S(1)}, f32[4,16,128,128]{3,2,1,0:T(8,128)S(1)}) custom-call(s32[1]{0:T(128)} %bitcast.turn_ref, s32[1]{0:T(128)} %bitcast.18.me_ref, f32[4]{0:T(128)S(1)} %pad_maximum_fusion.7.w_ref), custom_call_target="tpu_custom_call" | custom-call | flops 209715200 | bytes 8388608 | tf_op jit(solution)/shard_map/w_phases/pallas_call | solution.py:314
  259.7 1.9 copy-done
  261.6 2.0 copy-done.2
  263.6 0.0 all-to-all-done.3
  263.6 0.0 collective-permute-done.early_1
  263.6 0.0 collective-permute-done.2.early_3
  263.7 2.2 copy-done.1
  265.8 2.2 copy-done.3
  268.0 4.0 %column_transform.1 = (f32[16,32,128]{2,1,0:T(8,128)S(1)}, bf16[16,32,128]{2,1,0:T(8,128)(2,1)S(1)}, bf16[16,32,128]{2,1,0:T(8,128)(2,1)S(1)}, bf16[16,32,128]{2,1,0:T(8,128)(2,1)S(1)}) custom-call(s32[1]{0:T(128)} %bitcast.turn_ref, bf16[16,128,128]{2,1,0:T(8,128)(2,1)S(1)} %get-tuple-element.18.early_0, ...), custom_call_target="tpu_custom_call" | custom-call | flops 4300000256 | bytes 13631488 | tf_op jit(solution)/shard_map/column_transform/pallas_call | solution.py:363
  272.0 2.6 collective-permute-start.5
  274.6 2.6 collective-permute-start.6
  277.2 0.0 collective-permute-start.7
  277.2 1.2 collective-permute-done.5.refs_1_
  278.4 3.1 %collective-permute-done.6.refs_2_ = bf16[16,32,128]{2,1,0:T(8,128)(2,1)S(1)} collective-permute-done((bf16[16,32,128]{2,1,0:T(8,128)(2,1)S(1)}, bf16[16,32,128]{2,1,0:T(8,128)(2,1)S(1)}, u32[]{:S(2)}, u32[]{:S(2)}) %collective-permute-start.6) | collective-permute-done | bytes 131104 | tf_op jit(solution)/shard_map/ppermute | solution.py:409
  281.5 0.7 collective-permute-done.7.refs_3_
  282.2 1.2 place_image_rows.1
  (11 shorter events, 0.1 us)
Async XLA Ops:
  5.0 64.8 %all-to-all-start = ((bf16[64,136,128]{2,1,0:T(8,128)(2,1)}), bf16[64,136,128]{2,1,0:T(8,128)(2,1)}, u32[]{:S(2)}, u32[]{:S(2)}) async-start(bf16[64,136,128]{2,1,0:T(8,128)(2,1)} %pack_rows.2), calls=%async_computation | async-start | bytes 4456448 | tf_op jit(solution)/shard_map/all_to_all | solution.py:437
  69.7 57.2 %all-to-all-start.2 = ((bf16[64,128,128]{2,1,0:T(8,128)(2,1)}), bf16[64,128,128]{2,1,0:T(8,128)(2,1)}, u32[]{:S(2)}, u32[]{:S(2)}) async-start(bf16[64,128,128]{2,1,0:T(8,128)(2,1)} %pack_rows.3), calls=%async_computation.2 | async-start | bytes 4194304 | tf_op jit(solution)/shard_map/all_to_all | solution.py:437
  126.9 57.2 %all-to-all-start.1 = ((bf16[64,128,128]{2,1,0:T(8,128)(2,1)}), bf16[64,128,128]{2,1,0:T(8,128)(2,1)}, u32[]{:S(2)}, u32[]{:S(2)}) async-start(bf16[64,128,128]{2,1,0:T(8,128)(2,1)} %bitcast.29), calls=%async_computation.1 | async-start | bytes 4194304 | tf_op jit(solution)/shard_map/all_to_all | solution.py:447
  184.0 79.6 %all-to-all-start.3 = ((bf16[256,32,128]{2,1,0:T(8,128)(2,1)}), bf16[256,32,128]{2,1,0:T(8,128)(2,1)S(1)}, u32[]{:S(2)}, u32[]{:S(2)}) async-start(bf16[256,32,128]{2,1,0:T(8,128)(2,1)} %bitcast.28), calls=%async_computation.3 | async-start | bytes 4194304 | tf_op jit(solution)/shard_map/all_to_all | solution.py:451
  197.1 66.6 %collective-permute-start = (bf16[16,128,128]{2,1,0:T(8,128)(2,1)}, bf16[16,128,128]{2,1,0:T(8,128)(2,1)S(1)}, u32[]{:S(2)}, u32[]{:S(2)}) collective-permute-start(bf16[16,128,128]{2,1,0:T(8,128)(2,1)} %get-tuple-element.19), channel_id=1, source_target_pairs={{0,1},{1,2},{2,3},{3,0},{4,5},{5,6},{6,7},{7,4},{8,9},{9,10},{10,1... | collective-permute-start | bytes 1572872 | tf_op jit(solution)/shard_map/ppermute | solution.py:409
  198.3 65.3 %collective-permute-start.1 = (bf16[16,128,128]{2,1,0:T(8,128)(2,1)}, bf16[16,128,128]{2,1,0:T(8,128)(2,1)}, u32[]{:S(2)}, u32[]{:S(2)}) collective-permute-start(bf16[16,128,128]{2,1,0:T(8,128)(2,1)} %get-tuple-element.20), channel_id=1, source_target_pairs={{0,2},{1,3},{2,0},{3,1},{4,6},{5,7},{6,4},{7,5},{8,10},{9,11},{10,... | collective-permute-start | bytes 1572872 | tf_op jit(solution)/shard_map/ppermute | solution.py:409
  200.8 62.8 %collective-permute-start.2 = (bf16[16,128,128]{2,1,0:T(8,128)(2,1)}, bf16[16,128,128]{2,1,0:T(8,128)(2,1)}, u32[]{:S(2)}, u32[]{:S(2)}) collective-permute-start(bf16[16,128,128]{2,1,0:T(8,128)(2,1)} %get-tuple-element.21), channel_id=1, source_target_pairs={{0,3},{1,0},{2,1},{3,2},{4,7},{5,4},{6,5},{7,6},{8,11},{9,8},{10,9... | collective-permute-start | bytes 1572872 | tf_op jit(solution)/shard_map/ppermute | solution.py:409
  203.6 33.2 %collective-permute-start.3 = (f32[1]{0:T(128)}, f32[1]{0:T(128)}, u32[]{:S(2)}, u32[]{:S(2)}) collective-permute-start(f32[1]{0:T(128)} %param.13), channel_id=1, source_target_pairs={{0,1},{1,2},{2,3},{3,0},{4,5},{5,6},{6,7},{7,4},{8,9},{9,10},{10,1... | collective-permute-start | bytes 20 | tf_op jit(solution)/shard_map/ppermute | solution.py:409
  237.6 4.2 %collective-permute-start.4 = (f32[2]{0:T(128)S(1)}, f32[2]{0:T(128)S(1)}, u32[]{:S(2)}, u32[]{:S(2)}) collective-permute-start(f32[2]{0:T(128)S(1)} %pad_maximum_fusion.6), channel_id=1, source_target_pairs={{0,2},{1,3},{2,0},{3,1},{4,6},{5,7},{6,4},{7,5},{8,10},{9,11},{10,... | collective-permute-start | bytes 32 | tf_op jit(solution)/shard_map/ppermute | solution.py:409
  259.7 1.9 copy-start
  261.6 2.0 copy-start.2
  263.7 2.2 copy-start.1
  265.8 2.2 copy-start.3
  272.0 6.4 %collective-permute-start.5 = (bf16[16,32,128]{2,1,0:T(8,128)(2,1)S(1)}, bf16[16,32,128]{2,1,0:T(8,128)(2,1)S(1)}, u32[]{:S(2)}, u32[]{:S(2)}) collective-permute-start(bf16[16,32,128]{2,1,0:T(8,128)(2,1)S(1)} %get-tuple-element.26), channel_id=1, source_target_pairs={{0,1},{1,2},{2,3},{3,0},{4,5},{5,6},{6,7},{7,4},{8,9},{9,10},{10,1... | collective-permute-start | bytes 393224 | tf_op jit(solution)/shard_map/ppermute | solution.py:409
  274.6 6.9 %collective-permute-start.6 = (bf16[16,32,128]{2,1,0:T(8,128)(2,1)S(1)}, bf16[16,32,128]{2,1,0:T(8,128)(2,1)S(1)}, u32[]{:S(2)}, u32[]{:S(2)}) collective-permute-start(bf16[16,32,128]{2,1,0:T(8,128)(2,1)S(1)} %get-tuple-element.27), channel_id=1, source_target_pairs={{0,2},{1,3},{2,0},{3,1},{4,6},{5,7},{6,4},{7,5},{8,10},{9,11},{10,... | collective-permute-start | bytes 393224 | tf_op jit(solution)/shard_map/ppermute | solution.py:409
  277.2 5.0 %collective-permute-start.7 = (bf16[16,32,128]{2,1,0:T(8,128)(2,1)S(1)}, bf16[16,32,128]{2,1,0:T(8,128)(2,1)S(1)}, u32[]{:S(2)}, u32[]{:S(2)}) collective-permute-start(bf16[16,32,128]{2,1,0:T(8,128)(2,1)S(1)} %get-tuple-element.28), channel_id=1, source_target_pairs={{0,3},{1,0},{2,1},{3,2},{4,7},{5,4},{6,5},{7,6},{8,11},{9,8},{10,9... | collective-permute-start | bytes 393224 | tf_op jit(solution)/shard_map/ppermute | solution.py:409

commit v5 on v4

--- a/solution.py
+++ b/solution.py
@@ -294,92 +294,106 @@
     )(turn, columns)
 
 
-def phase_kernel(turn_ref, me_ref, w_ref, cosine_ref, sine_ref):
+def base_phases(turn, me, w):
+    k = jnp.arange(16, dtype=jnp.int32)[:, None, None]
+    row = 64 * ((jnp.arange(128, dtype=jnp.int32)[:, None] + 32 * turn) % 128) + 16 * turn + k
+    column = 128 * me + jnp.arange(128, dtype=jnp.int32)
+    x = (row.astype(F32) - N // 2) / N
+    y = (column.astype(F32) - N // 2) / N
+    term = jnp.sqrt(1.0 - (x**2 + y**2)) - 1.0
+    angle = (2.0 * math.pi) * w[:, None, None] * term[8]
+    return jnp.stack([jnp.cos(angle), jnp.sin(angle)]), term - term[8]
+
+
+def column_kernel(
+    turn_ref, w_ref, early_0, early_1, early_2, early_3, late_ref, table_ref, base_hbm, change_hbm,
+    own_ref, sent_1, sent_2, sent_3, early, late, rows, base_ref, change_ref, sems,
+):
+    arrivals = ([], [])
+
+    def fetch(half, source, target):
+        number = len(arrivals[0]) + len(arrivals[1])
+        copy = pltpu.make_async_copy(source, target, sems.at[number])
+        copy.start()
+        arrivals[half].append(copy)
+
+    for half in range(2):
+        k = pl.ds(8 * half, 8)
+        pairs = pl.ds(16 * half, 16)
+        fetch(half, late_ref.at[:, :, pairs], late.at[:, :, pairs])
+        for step, source in enumerate((early_0, early_1, early_2, early_3)):
+            fetch(half, source.at[k], early.at[step, k])
+        fetch(half, change_hbm.at[k], change_ref.at[k])
+        if half == 0:
+            fetch(half, base_hbm, base_ref)
+
     turn = turn_ref[0]
-    k = 16 * turn + pl.program_id(0)
-    j = (lax.broadcasted_iota(jnp.int32, (128, 128), 0) + 32 * turn) & 127
-    column = lax.broadcasted_iota(jnp.int32, (128, 128), 1) + 128 * me_ref[0]
-    x = ((64 * j + k).astype(F32) - N // 2) / N
-    y = (column.astype(F32) - N // 2) / N
-    term = jnp.sqrt(1.0 - (x * x + y * y)) - 1.0
-    for step in range(4):
-        angle = (2.0 * math.pi * w_ref[step]) * term
-        cosine_ref[step, 0] = jnp.cos(angle)
-        sine_ref[step, 0] = jnp.sin(angle)
-
-
-def phases(turn, me, w):
-    smem = pl.BlockSpec(memory_space=pltpu.SMEM)
-    block = pl.BlockSpec((4, 1, 128, 128), lambda i: (0, i, 0, 0))
-    return pl.pallas_call(
-        phase_kernel,
-        grid=(16,),
-        in_specs=[smem] * 3,
-        out_specs=[block] * 2,
-        out_shape=[jax.ShapeDtypeStruct((4, 16, 128, 128), F32)] * 2,
-        compiler_params=pltpu.CompilerParams(vmem_limit_bytes=16 * MIB),
-        cost_estimate=pl.CostEstimate(flops=200 << 20, bytes_accessed=8 << 20, transcendentals=2 << 20),
-        name="w_phases",
-    )(turn, me, w)
-
-
-def column_kernel(
-    turn_ref, early_0, early_1, early_2, early_3, late_ref, table_ref, cosine_ref, sine_ref,
-    own_ref, *sent
-):
     table = table_ref[...]
-    early = (early_0, early_1, early_2, early_3)
-    count = early_0.shape[0]
-    late = [
-        jnp.swapaxes(late_ref[(turn_ref[0] - step) & 3], 0, 1).reshape(count, 128, 128)
-        for step in range(4)
-    ]
-    for index in range(count):
-        image = jnp.zeros((128, 128), F32)
+    targets = (own_ref, sent_1, sent_2, sent_3)
+
+    def one(k, carry):
+        sky = []
         for pair in (0, 2):
             cells = jnp.concatenate(
                 [
-                    jnp.concatenate([early[step][index], late[step][index]], axis=0)
+                    jnp.concatenate([early[step, k], rows[step, k]], axis=0)
                     for step in (pair, pair + 1)
                 ],
                 axis=1,
             )
-            sky = jnp.dot(
-                table, jnp.concatenate([cells, cells], axis=0), preferred_element_type=F32
+            sky.append(
+                jnp.dot(table, jnp.concatenate([cells, cells], axis=0), preferred_element_type=F32)
             )
-            for step in (pair, pair + 1):
-                part = sky[:, 128 * (step - pair) : 128 * (step - pair) + 128]
-                image += part[:128] * cosine_ref[step, index] - part[128:] * sine_ref[step, index]
-        own_ref[index] = image[:32]
-        for step in range(3):
-            sent[step][index] = image[32 * step + 32 : 32 * step + 64].astype(BF16)
-
-
-def column_transform(turn, early, late, table, cosine, sine):
-    each = 8
-    block = pl.BlockSpec((each, 128, 128), lambda i: (i, 0, 0))
-    phase = pl.BlockSpec((4, each, 128, 128), lambda i: (0, i, 0, 0))
-    result = pl.BlockSpec((each, 32, 128), lambda i: (i, 0, 0))
+        for block, target in enumerate(targets):
+            where = slice(32 * block, 32 * block + 32)
+            change = change_ref[k, where]
+            image = jnp.zeros((32, 128), F32)
+            for step in range(4):
+                part = sky[step // 2][:, 128 * (step % 2) : 128 * (step % 2) + 128]
+                real = part[:128][where]
+                imag = part[128:][where]
+                angle = (2.0 * math.pi * w_ref[step]) * change
+                square = angle * angle
+                sine = angle * (1.0 - square * (1.0 / 6.0))
+                cosine = 1.0 - square * (0.5 - square * (1.0 / 24.0))
+                image += (real * cosine - imag * sine) * base_ref[0, step, where]
+                image -= (real * sine + imag * cosine) * base_ref[1, step, where]
+            target[k] = image.astype(target.dtype)
+        return carry
+
+    for half in range(2):
+        for copy in arrivals[half]:
+            copy.wait()
+        for step in range(4):
+            block = late[(turn - step) & 3, :, 16 * half : 16 * half + 16]
+            rows[step, 8 * half : 8 * half + 8] = jnp.swapaxes(block, 0, 1).reshape(8, 128, 128)
+        lax.fori_loop(8 * half, 8 * half + 8, one, 0, unroll=4)
+
+
+def column_transform(turn, w, early, late, table, base, change):
+    smem = pl.BlockSpec(memory_space=pltpu.SMEM)
+    vmem = pl.BlockSpec(memory_space=pltpu.VMEM)
+    anywhere = pl.BlockSpec(memory_space=pl.ANY)
     return pl.pallas_call(
         column_kernel,
-        grid=(16 // each,),
-        in_specs=[pl.BlockSpec(memory_space=pltpu.SMEM)]
-        + [block] * 4
-        + [
-            pl.BlockSpec((4, 64, 2 * each, 128), lambda i: (0, 0, i, 0)),
-            pl.BlockSpec((256, 512), lambda i: (0, 0)),
-            phase,
-            phase,
-        ],
-        out_specs=[result] * 4,
+        in_specs=[smem] * 2 + [anywhere] * 5 + [vmem] + [anywhere] * 2,
+        out_specs=[vmem] * 4,
         out_shape=[jax.ShapeDtypeStruct((16, 32, 128), F32)]
         + [jax.ShapeDtypeStruct((16, 32, 128), BF16)] * 3,
-        compiler_params=pltpu.CompilerParams(vmem_limit_bytes=24 * MIB),
+        scratch_shapes=[
+            pltpu.VMEM((4, 16, 128, 128), BF16),
+            pltpu.VMEM((4, 64, 32, 128), BF16),
+            pltpu.VMEM((4, 16, 128, 128), BF16),
+            pltpu.VMEM((2, 4, 128, 128), F32),
+            pltpu.VMEM((16, 128, 128), F32),
+            pltpu.SemaphoreType.DMA((13,)),
+        ],
+        compiler_params=pltpu.CompilerParams(vmem_limit_bytes=62 * MIB),
         cost_estimate=pl.CostEstimate(
-            flops=4_300_000_000, bytes_accessed=13 << 20, transcendentals=0
+            flops=4_300_000_000, bytes_accessed=5 << 20, transcendentals=0
         ),
         name="column_transform",
-    )(turn, *early, late, table, cosine, sine)
+    )(turn, w, *early, late, table, base, change)
 
 
 def place_kernel(turn_ref, *refs):
@@ -425,7 +439,6 @@
 
 def local(uv_tiles, target_bands, uv_offsets, tile_counts, plane_w):
     me = lax.axis_index("band")
-    turn = lax.axis_index("wp")
     first = jnp.asarray(row_first_table())
     twiddle = jnp.asarray(row_twiddles())
     second = jnp.asarray(row_second_table())
@@ -438,6 +451,12 @@
         )
     numbers = arrived[0][:, 128:131, :64].astype(jnp.int32)
     places = (numbers[:, 0] * 64 + numbers[:, 1]) * 256 + numbers[:, 2]
+    turn = lax.axis_index("wp")[None]
+    w = jnp.concatenate([plane_w, along_wp(plane_w, 1)])
+    w = jnp.concatenate([w, along_wp(w, 2)])
+    base, change = base_phases(turn[0], me, w)
+    places, base, change = lax.optimization_barrier((places, base, change))
+
     early = late = None
     for half in range(2):
         spectrum = grid_and_rows(
@@ -452,15 +471,12 @@
                 spectrum.reshape(256, 32, 128), ("wp", "band"), split_axis=0, concat_axis=0, tiled=True
             ).reshape(4, 64, 32, 128)
 
-    early, w = lax.optimization_barrier((early, plane_w))
-    w = jnp.concatenate([w, along_wp(w, 1)])
-    w = jnp.concatenate([w, along_wp(w, 2)])
-    turn = turn[None]
-    cosine, sine = phases(turn, me[None], w)
     dealt = deal_rows(turn, early)
     dealt = [dealt[0]] + [along_wp(dealt[step], step) for step in (1, 2, 3)]
     table = jnp.roll(jnp.asarray(column_second_table()).reshape(2, 128, 512), -32 * turn[0], axis=1)
-    own, *sent = column_transform(turn, dealt, late, table.reshape(256, 512), cosine, sine)
+    own, *sent = column_transform(
+        turn, w, dealt, late, table.reshape(256, 512), base, change
+    )
     blocks = [own] + [along_wp(block, step + 1) for step, block in enumerate(sent)]
     return place_rows(turn, blocks).reshape(2048, 128)
 

time: 287 us -> 271 us (0.944)
  Pallas kernels: 99.6 us -> 86.3 us
  local copies, waits for them, and re-layouts: 10.3 us -> 4.39 us
  other arithmetic: 4.01 us -> 8.04 us
    all_to_all x1, waiting for transfers between devices: 0.01 us -> 44.3 us  [local(): lax.all_to_all(spectrum.reshape(256, 32, 128), ('wp', 'band'), split_axis...]
    ppermute x8, waiting for transfers between devices: 39.4 us -> 8.69 us  [along_wp(): return lax.ppermute(block, 'wp', pairs)]
    pallas_call x2 -> x1, Pallas kernels: 21 us -> 8.24 us  [column_transform(): pl.pallas_call(column_kernel, in_specs=[smem] * 2 + [anywhere] * 5 + [vme...]
    all_to_all x2, waiting for transfers between devices: 62.8 us -> 50.8 us  [local(): lax.all_to_all(packed, 'band', split_axis=0, concat_axis=0, tiled=True)]
    unnamed x8 -> x10, local copies, waits for them, and re-layouts: 8.34 us -> 2.7 us
  transfers between devices with their start and end apart: 12 -> 12, of which waited for: 8 -> 7; matrix products, arithmetic and copies ran while one was open for 2% -> 4% of each run, Pallas kernels for 32% -> 27%
where the time goes in v5:
time: 271 us; the launch traced here: 270 us
  waiting for transfers between devices  120 us (44%)
  Pallas kernels  86.3 us (32%)
  starting transfers between devices  49.8 us (18%)
  other arithmetic  8.04 us (3%)
  local copies, waits for them, and re-layouts  4.39 us (2%)
    pallas_call x2, Pallas kernels, grid_and_rows(): pl.pallas_call(grid_kernel, in_specs=[pl.BlockSpec(memory_space=pltpu.SME...  65.7 us
    all_to_all x2, waiting for transfers between devices, local(): lax.all_to_all(packed, 'band', split_axis=0, concat_axis=0, tiled=True)  50.8 us
    all_to_all x1, waiting for transfers between devices, local(): lax.all_to_all(spectrum.reshape(256, 32, 128), ('wp', 'band'), split_axis...  44.3 us
    all_to_all x2, starting transfers between devices, local(): lax.all_to_all(packed, 'band', split_axis=0, concat_axis=0, tiled=True)  19.4 us
    all_to_all x1, waiting for transfers between devices, local(): lax.all_to_all(spectrum.reshape(64, 128, 128), 'band', split_axis=0, conc...  16 us
    ppermute x8, starting transfers between devices, along_wp(): return lax.ppermute(block, 'wp', pairs)  12.1 us
    all_to_all x1, starting transfers between devices, local(): lax.all_to_all(spectrum.reshape(256, 32, 128), ('wp', 'band'), split_axis...  10.9 us
    ppermute x8, waiting for transfers between devices, along_wp(): return lax.ppermute(block, 'wp', pairs)  8.69 us
  transfers between devices with their start and end apart: 12, of which 7 were waited for; matrix products, arithmetic and copies ran while one was open for 4% of the time, Pallas kernels for 27%

profile of v5, /device:TPU:33, one launch (start us, length us, event | category | flops | bytes accessed | tf_op | source)
XLA Modules:
  0.0 269.8 jit_solution(16815579606803292765)
XLA Ops:
  0.7 4.3 %pack_rows.2 = bf16[64,136,128]{2,1,0:T(8,128)(2,1)} custom-call(s32[1,1]{1,0:T(1,128)S(6)} %copy.19.count_ref, s32[1,64]{1,0:T(1,128)} %bitcast.36, s32[2,64]{1,0:T(2,128)} %bitcast.34, bf16[64,2,128,128]{3,2,1,0:T(8,128)(2,1)} %bitcast.25), custom_call_target="tpu_custom_call" | custom-call | flops 8388608 | bytes 4194304 | tf_op jit(solution)/shard_map/pack_rows/pallas_call | solution.py:135
  5.0 12.1 %all-to-all-start = ((bf16[64,136,128]{2,1,0:T(8,128)(2,1)}), bf16[64,136,128]{2,1,0:T(8,128)(2,1)}, u32[]{:S(2)}, u32[]{:S(2)}) async-start(bf16[64,136,128]{2,1,0:T(8,128)(2,1)} %pack_rows.2), calls=%async_computation | async-start | bytes 4456448 | tf_op jit(solution)/shard_map/all_to_all | solution.py:450
  17.1 1.4 collective-permute-start
  18.5 0.2 fusion.22
  18.6 0.1 maximum_bitcast_fusion
  18.7 0.1 copy.15
  18.8 4.3 %pack_rows.3 = bf16[64,128,128]{2,1,0:T(8,128)(2,1)} custom-call(s32[1,1]{1,0:T(1,128)S(6)} %copy.19.count_ref, s32[1,64]{1,0:T(1,128)} %bitcast.37, s32[2,64]{1,0:T(2,128)} %bitcast.35, bf16[64,2,128,128]{3,2,1,0:T(8,128)(2,1)} %bitcast.26), custom_call_target="tpu_custom_call" | custom-call | flops 8388608 | bytes 4194304 | tf_op jit(solution)/shard_map/pack_rows/pallas_call | solution.py:135
  23.1 46.7 %all-to-all-done.arrived_ref = bf16[64,136,128]{2,1,0:T(8,128)(2,1)} async-done(((bf16[64,136,128]{2,1,0:T(8,128)(2,1)}), bf16[64,136,128]{2,1,0:T(8,128)(2,1)}, u32[]{:S(2)}, u32[]{:S(2)}) %all-to-all-start) | async-done | bytes 2228256 | tf_op jit(solution)/shard_map/all_to_all | solution.py:450
  69.8 7.3 %all-to-all-start.2 = ((bf16[64,128,128]{2,1,0:T(8,128)(2,1)}), bf16[64,128,128]{2,1,0:T(8,128)(2,1)}, u32[]{:S(2)}, u32[]{:S(2)}) async-start(bf16[64,128,128]{2,1,0:T(8,128)(2,1)} %pack_rows.3), calls=%async_computation.2 | async-start | bytes 4194304 | tf_op jit(solution)/shard_map/all_to_all | solution.py:450
  77.7 0.6 pad_maximum_fusion.2.bands_ref
  78.4 0.4 sqrt_add_fusion
  78.8 1.4 broadcast_subtract_fusion.change_hbm
  80.3 0.6 pad_maximum_fusion.7
  80.9 2.9 %collective-permute-start.1 = (f32[2]{0:T(128)S(1)}, f32[2]{0:T(128)S(1)}, u32[]{:S(2)}, u32[]{:S(2)}) collective-permute-start(f32[2]{0:T(128)S(1)} %pad_maximum_fusion.7), channel_id=1, source_target_pairs={{0,2},{1,3},{2,0},{3,1},{4,6},{5,7},{6,4},{7,5},{8,10},{9,11},{10,... | collective-permute-start | bytes 32 | tf_op jit(solution)/shard_map/ppermute | solution.py:423
  83.8 1.4 collective-permute-done.1
  85.2 1.2 broadcast_multiply_fusion
  86.5 1.0 multiply_cosine_fusion
  87.4 0.8 pad_maximum_fusion.base_hbm
  88.3 0.9 slice.21
  89.2 0.6 fusion.10.place_ref
  89.9 32.9 %place_and_transform.2 = bf16[1,64,128,128]{3,2,1,0:T(8,128)(2,1)} custom-call(s32[64,64]{1,0:T(8,128)} %fusion.10.place_ref, bf16[64,136,128]{2,1,0:T(8,128)(2,1)} %all-to-all-done.arrived_ref, bf16[128,384]{1,0:T(8,128)(2,1)} %constant.98.clone.first_ref, f32[2,128,128]{2,1,0:T(8,128)} %constant.99.clone.twiddle_ref, ...), custom_call_target="tpu_custom_call" | custom-call | flops 20000000000 | bytes 4194304 | tf_op jit(solution)/shard_map/place_and_transform/pallas_call | solution.py:255
  122.7 4.2 %all-to-all-done.2.arrived_ref = bf16[64,128,128]{2,1,0:T(8,128)(2,1)} async-done(((bf16[64,128,128]{2,1,0:T(8,128)(2,1)}), bf16[64,128,128]{2,1,0:T(8,128)(2,1)}, u32[]{:S(2)}, u32[]{:S(2)}) %all-to-all-start.2) | async-done | bytes 2097184 | tf_op jit(solution)/shard_map/all_to_all | solution.py:450
  126.9 7.3 %all-to-all-start.1 = ((bf16[64,128,128]{2,1,0:T(8,128)(2,1)}), bf16[64,128,128]{2,1,0:T(8,128)(2,1)}, u32[]{:S(2)}, u32[]{:S(2)}) async-start(bf16[64,128,128]{2,1,0:T(8,128)(2,1)} %bitcast.28), calls=%async_computation.1 | async-start | bytes 4194304 | tf_op jit(solution)/shard_map/all_to_all | solution.py:466
  134.3 0.1 fusion.23
  134.4 0.1 pad_maximum_fusion.5
  134.5 0.1 pad_maximum_fusion.3
  134.6 0.6 pad_maximum_fusion.4.bands_ref
  135.2 32.8 %place_and_transform.3 = bf16[4,64,32,128]{3,2,1,0:T(8,128)(2,1)} custom-call(s32[64,64]{1,0:T(8,128)} %fusion.10.place_ref, bf16[64,128,128]{2,1,0:T(8,128)(2,1)} %all-to-all-done.2.arrived_ref, bf16[128,384]{1,0:T(8,128)(2,1)} %constant.98.clone.first_ref, f32[2,128,128]{2,1,0:T(8,128)} %constant.99.clone.twiddle_ref, ...), custom_call_target="tpu_custom_call" | custom-call | flops 20000000000 | bytes 4194304 | tf_op jit(solution)/shard_map/place_and_transform/pallas_call | solution.py:255
  168.1 16.0 %all-to-all-done.1.columns_ref = bf16[64,128,128]{2,1,0:T(8,128)(2,1)} async-done(((bf16[64,128,128]{2,1,0:T(8,128)(2,1)}), bf16[64,128,128]{2,1,0:T(8,128)(2,1)}, u32[]{:S(2)}, u32[]{:S(2)}) %all-to-all-start.1) | async-done | bytes 2097184 | tf_op jit(solution)/shard_map/all_to_all | solution.py:466
  184.1 10.9 %all-to-all-start.3 = ((bf16[256,32,128]{2,1,0:T(8,128)(2,1)}), bf16[256,32,128]{2,1,0:T(8,128)(2,1)}, u32[]{:S(2)}, u32[]{:S(2)}) async-start(bf16[256,32,128]{2,1,0:T(8,128)(2,1)} %bitcast.27), calls=%async_computation.3 | async-start | bytes 4194304 | tf_op jit(solution)/shard_map/all_to_all | solution.py:470
  195.0 0.0 copy-start.2
  195.0 2.5 deal_rows.1
  197.6 0.8 copy-done.1
  198.3 1.2 collective-permute-start.2
  199.6 2.5 collective-permute-start.3
  202.1 1.1 collective-permute-start.4
  203.2 0.7 constant_dynamic-slice_fusion
  203.9 44.3 %all-to-all-done.3 = bf16[256,32,128]{2,1,0:T(8,128)(2,1)} async-done(((bf16[256,32,128]{2,1,0:T(8,128)(2,1)}), bf16[256,32,128]{2,1,0:T(8,128)(2,1)}, u32[]{:S(2)}, u32[]{:S(2)}) %all-to-all-start.3) | async-done | bytes 2097184 | tf_op jit(solution)/shard_map/all_to_all | solution.py:470
  248.3 0.8 copy-done.3
  249.0 0.2 copy-done.4
  249.2 8.2 %column_transform.1 = (f32[16,32,128]{2,1,0:T(8,128)}, bf16[16,32,128]{2,1,0:T(8,128)(2,1)}, bf16[16,32,128]{2,1,0:T(8,128)(2,1)}, bf16[16,32,128]{2,1,0:T(8,128)(2,1)}) custom-call(s32[1]{0:T(128)} %bitcast.turn_ref, f32[4]{0:T(128)} %get-tuple-element.28.w_ref, bf16[16,128,128]{2,1,0:T(8,128)(2,1)} %copy-done.1, bf16[16,128,128]{2,1,0:T(8,128)(2,1)} %copy-done.3, ...), custom_call_target="tpu_custom_call" | custom-call | flops 4300000256 | bytes 5242880 | tf_op jit(solution)/shard_map/column_transform/pallas_call | solution.py:377
  257.5 0.4 collective-permute-start.5
  257.9 1.7 collective-permute-start.6
  259.5 0.8 collective-permute-start.7
  260.4 6.2 %collective-permute-done.5.refs_1_ = bf16[16,32,128]{2,1,0:T(8,128)(2,1)S(1)} collective-permute-done((bf16[16,32,128]{2,1,0:T(8,128)(2,1)}, bf16[16,32,128]{2,1,0:T(8,128)(2,1)S(1)}, u32[]{:S(2)}, u32[]{:S(2)}) %collective-permute-start.5) | collective-permute-done | bytes 131104 | tf_op jit(solution)/shard_map/ppermute | solution.py:423
  266.6 1.1 collective-permute-done.7.refs_3_
  267.7 0.9 copy-done
  268.6 1.2 place_image_rows.1
  (20 shorter events, 0.1 us)
Async XLA Ops:
  5.0 64.8 %all-to-all-start = ((bf16[64,136,128]{2,1,0:T(8,128)(2,1)}), bf16[64,136,128]{2,1,0:T(8,128)(2,1)}, u32[]{:S(2)}, u32[]{:S(2)}) async-start(bf16[64,136,128]{2,1,0:T(8,128)(2,1)} %pack_rows.2), calls=%async_computation | async-start | bytes 4456448 | tf_op jit(solution)/shard_map/all_to_all | solution.py:450
  17.1 63.2 %collective-permute-start = (f32[1]{0:T(128)}, f32[1]{0:T(128)}, u32[]{:S(2)}, u32[]{:S(2)}) collective-permute-start(f32[1]{0:T(128)} %param.13), channel_id=1, source_target_pairs={{0,1},{1,2},{2,3},{3,0},{4,5},{5,6},{6,7},{7,4},{8,9},{9,10},{10,1... | collective-permute-start | bytes 20 | tf_op jit(solution)/shard_map/ppermute | solution.py:423
  69.8 57.2 %all-to-all-start.2 = ((bf16[64,128,128]{2,1,0:T(8,128)(2,1)}), bf16[64,128,128]{2,1,0:T(8,128)(2,1)}, u32[]{:S(2)}, u32[]{:S(2)}) async-start(bf16[64,128,128]{2,1,0:T(8,128)(2,1)} %pack_rows.3), calls=%async_computation.2 | async-start | bytes 4194304 | tf_op jit(solution)/shard_map/all_to_all | solution.py:450
  80.9 4.3 %collective-permute-start.1 = (f32[2]{0:T(128)S(1)}, f32[2]{0:T(128)S(1)}, u32[]{:S(2)}, u32[]{:S(2)}) collective-permute-start(f32[2]{0:T(128)S(1)} %pad_maximum_fusion.7), channel_id=1, source_target_pairs={{0,2},{1,3},{2,0},{3,1},{4,6},{5,7},{6,4},{7,5},{8,10},{9,11},{10,... | collective-permute-start | bytes 32 | tf_op jit(solution)/shard_map/ppermute | solution.py:423
  126.9 57.2 %all-to-all-start.1 = ((bf16[64,128,128]{2,1,0:T(8,128)(2,1)}), bf16[64,128,128]{2,1,0:T(8,128)(2,1)}, u32[]{:S(2)}, u32[]{:S(2)}) async-start(bf16[64,128,128]{2,1,0:T(8,128)(2,1)} %bitcast.28), calls=%async_computation.1 | async-start | bytes 4194304 | tf_op jit(solution)/shard_map/all_to_all | solution.py:466
  184.1 64.1 %all-to-all-start.3 = ((bf16[256,32,128]{2,1,0:T(8,128)(2,1)}), bf16[256,32,128]{2,1,0:T(8,128)(2,1)}, u32[]{:S(2)}, u32[]{:S(2)}) async-start(bf16[256,32,128]{2,1,0:T(8,128)(2,1)} %bitcast.27), calls=%async_computation.3 | async-start | bytes 4194304 | tf_op jit(solution)/shard_map/all_to_all | solution.py:470
  195.0 8.2 %copy-start.2 = (bf16[2,256,512]{2,1,0:T(8,128)(2,1)S(1)}, bf16[2,256,512]{2,1,0:T(8,128)(2,1)}, u32[]{:S(2)}) copy-start(bf16[2,256,512]{2,1,0:T(8,128)(2,1)} %constant.108) | copy-start | bytes 1572868
  197.5 0.8 copy-start.1
  198.3 49.9 %collective-permute-start.2 = (bf16[16,128,128]{2,1,0:T(8,128)(2,1)S(1)}, bf16[16,128,128]{2,1,0:T(8,128)(2,1)S(1)}, u32[]{:S(2)}, u32[]{:S(2)}) collective-permute-start(bf16[16,128,128]{2,1,0:T(8,128)(2,1)S(1)} %get-tuple-element.18), channel_id=1, source_target_pairs={{0,1},{1,2},{2,3},{3,0},{4,5},{5,6},{6,7},{7,4},{8,9},{9,10},{10,1... | collective-permute-start | bytes 1572872 | tf_op jit(solution)/shard_map/ppermute | solution.py:423
  199.6 48.6 %collective-permute-start.3 = (bf16[16,128,128]{2,1,0:T(8,128)(2,1)S(1)}, bf16[16,128,128]{2,1,0:T(8,128)(2,1)S(1)}, u32[]{:S(2)}, u32[]{:S(2)}) collective-permute-start(bf16[16,128,128]{2,1,0:T(8,128)(2,1)S(1)} %get-tuple-element.19), channel_id=1, source_target_pairs={{0,2},{1,3},{2,0},{3,1},{4,6},{5,7},{6,4},{7,5},{8,10},{9,11},{10,... | collective-permute-start | bytes 1572872 | tf_op jit(solution)/shard_map/ppermute | solution.py:423
  202.1 46.1 %collective-permute-start.4 = (bf16[16,128,128]{2,1,0:T(8,128)(2,1)S(1)}, bf16[16,128,128]{2,1,0:T(8,128)(2,1)}, u32[]{:S(2)}, u32[]{:S(2)}) collective-permute-start(bf16[16,128,128]{2,1,0:T(8,128)(2,1)S(1)} %get-tuple-element.20), channel_id=1, source_target_pairs={{0,3},{1,0},{2,1},{3,2},{4,7},{5,4},{6,5},{7,6},{8,11},{9,8},{10,9... | collective-permute-start | bytes 1572872 | tf_op jit(solution)/shard_map/ppermute | solution.py:423
  248.2 0.8 copy-start.3
  248.2 1.0 copy-start.4
  257.5 9.1 %collective-permute-start.5 = (bf16[16,32,128]{2,1,0:T(8,128)(2,1)}, bf16[16,32,128]{2,1,0:T(8,128)(2,1)S(1)}, u32[]{:S(2)}, u32[]{:S(2)}) collective-permute-start(bf16[16,32,128]{2,1,0:T(8,128)(2,1)} %get-tuple-element.24), channel_id=1, source_target_pairs={{0,1},{1,2},{2,3},{3,0},{4,5},{5,6},{6,7},{7,4},{8,9},{9,10},{10,1... | collective-permute-start | bytes 393224 | tf_op jit(solution)/shard_map/ppermute | solution.py:423
  257.9 8.7 %collective-permute-start.6 = (bf16[16,32,128]{2,1,0:T(8,128)(2,1)}, bf16[16,32,128]{2,1,0:T(8,128)(2,1)S(1)}, u32[]{:S(2)}, u32[]{:S(2)}) collective-permute-start(bf16[16,32,128]{2,1,0:T(8,128)(2,1)} %get-tuple-element.25), channel_id=1, source_target_pairs={{0,2},{1,3},{2,0},{3,1},{4,6},{5,7},{6,4},{7,5},{8,10},{9,11},{10,... | collective-permute-start | bytes 393224 | tf_op jit(solution)/shard_map/ppermute | solution.py:423
  259.5 8.1 %collective-permute-start.7 = (bf16[16,32,128]{2,1,0:T(8,128)(2,1)}, bf16[16,32,128]{2,1,0:T(8,128)(2,1)S(1)}, u32[]{:S(2)}, u32[]{:S(2)}) collective-permute-start(bf16[16,32,128]{2,1,0:T(8,128)(2,1)} %get-tuple-element.26), channel_id=1, source_target_pairs={{0,3},{1,0},{2,1},{3,2},{4,7},{5,4},{6,5},{7,6},{8,11},{9,8},{10,9... | collective-permute-start | bytes 393224 | tf_op jit(solution)/shard_map/ppermute | solution.py:423
  267.7 1.0 copy-start

commit v6 on v5

--- a/solution.py
+++ b/solution.py
@@ -55,7 +55,7 @@
     return np.concatenate([high, low], axis=0)
 
 
-def column_second_table():
+def column_second_table(half):
     cosine, sine = circle(np.arange(128)[:, None] * np.arange(128)[None, :], 128)
     table = np.zeros((2, 128, 2, 2, 64))
     cosine = cosine.reshape(128, 2, 64) / N
@@ -64,7 +64,7 @@
     table[0, :, :, 1] = -sine
     table[1, :, :, 0] = sine
     table[1, :, :, 1] = cosine
-    high, low = split(table.reshape(256, 256))
+    high, low = split(table[:, :, half].reshape(256, 128))
     return np.concatenate([high, low], axis=1)
 
 
@@ -302,98 +302,148 @@
     y = (column.astype(F32) - N // 2) / N
     term = jnp.sqrt(1.0 - (x**2 + y**2)) - 1.0
     angle = (2.0 * math.pi) * w[:, None, None] * term[8]
-    return jnp.stack([jnp.cos(angle), jnp.sin(angle)]), term - term[8]
-
-
-def column_kernel(
-    turn_ref, w_ref, early_0, early_1, early_2, early_3, late_ref, table_ref, base_hbm, change_hbm,
-    own_ref, sent_1, sent_2, sent_3, early, late, rows, base_ref, change_ref, sems,
+    return jnp.stack([jnp.cos(angle), jnp.sin(angle)]), (term - term[8]).astype(BF16)
+
+
+def transform_planes(table_ref, cells):
+    sky = []
+    for pair in (0, 2):
+        both = jnp.concatenate([cells[pair], cells[pair + 1]], axis=1)
+        sky.append(
+            jnp.dot(
+                table_ref[...], jnp.concatenate([both, both], axis=0), preferred_element_type=F32
+            )
+        )
+    return sky
+
+
+def add_planes(image, sky, where, change, w_ref, base_ref):
+    for step in range(4):
+        part = sky[step // 2][:, 128 * (step % 2) : 128 * (step % 2) + 128]
+        real = part[:128][where]
+        imag = part[128:][where]
+        angle = (2.0 * math.pi * w_ref[step]) * change
+        square = angle * angle
+        sine = angle * (1.0 - square * (1.0 / 6.0))
+        cosine = 1.0 - square * (0.5 - square * (1.0 / 24.0))
+        image += (real * cosine - imag * sine) * base_ref[0, step, where]
+        image -= (real * sine + imag * cosine) * base_ref[1, step, where]
+    return image
+
+
+def early_kernel(w_ref, early_0, early_1, early_2, early_3, table_ref, base_ref, change_ref, out_ref):
+    def one(k, carry):
+        sky = transform_planes(table_ref, [ref[k] for ref in (early_0, early_1, early_2, early_3)])
+        for block in range(4):
+            where = slice(32 * block, 32 * block + 32)
+            change = change_ref[k, where].astype(F32)
+            out_ref[k, where] = add_planes(
+                jnp.zeros((32, 128), F32), sky, where, change, w_ref, base_ref
+            )
+        return carry
+
+    lax.fori_loop(0, 16, one, 0, unroll=2)
+
+
+def early_image(w, early, table, base, change):
+    vmem = pl.BlockSpec(memory_space=pltpu.VMEM)
+    return pl.pallas_call(
+        early_kernel,
+        in_specs=[pl.BlockSpec(memory_space=pltpu.SMEM)] + [vmem] * 7,
+        out_specs=vmem,
+        out_shape=jax.ShapeDtypeStruct((16, 128, 128), F32),
+        compiler_params=pltpu.CompilerParams(vmem_limit_bytes=62 * MIB),
+        cost_estimate=pl.CostEstimate(
+            flops=2_200_000_000, bytes_accessed=5 << 20, transcendentals=0
+        ),
+        name="early_column_transform",
+    )(w, *early, table, base, change)
+
+
+def late_kernel(
+    turn_ref, w_ref, early_hbm, late_hbm, table_hbm, base_hbm, change_hbm,
+    own_hbm, sent_1, sent_2, sent_3, early_ref, late_ref, rows_ref, table_ref, base_ref, change_ref,
+    own_ref, sent_ref, in_sems, out_sems,
 ):
-    arrivals = ([], [])
-
-    def fetch(half, source, target):
-        number = len(arrivals[0]) + len(arrivals[1])
-        copy = pltpu.make_async_copy(source, target, sems.at[number])
-        copy.start()
-        arrivals[half].append(copy)
-
-    for half in range(2):
+    def fetch(half):
         k = pl.ds(8 * half, 8)
         pairs = pl.ds(16 * half, 16)
-        fetch(half, late_ref.at[:, :, pairs], late.at[:, :, pairs])
-        for step, source in enumerate((early_0, early_1, early_2, early_3)):
-            fetch(half, source.at[k], early.at[step, k])
-        fetch(half, change_hbm.at[k], change_ref.at[k])
+        moves = [
+            (late_hbm.at[:, :, pairs], late_ref.at[:, :, pairs]),
+            (early_hbm.at[k], early_ref.at[k]),
+            (change_hbm.at[k], change_ref.at[k]),
+        ]
         if half == 0:
-            fetch(half, base_hbm, base_ref)
+            moves += [(table_hbm, table_ref), (base_hbm, base_ref)]
+        copies = []
+        for number, (source, target) in enumerate(moves):
+            copy = pltpu.make_async_copy(source, target, in_sems.at[5 * half + number])
+            copy.start()
+            copies.append(copy)
+        return copies
+
+    def one(k, carry):
+        sky = transform_planes(table_ref, [rows_ref[step, k] for step in range(4)])
+        for block in range(4):
+            where = slice(32 * block, 32 * block + 32)
+            change = change_ref[k, where].astype(F32)
+            image = add_planes(early_ref[k, where], sky, where, change, w_ref, base_ref)
+            if block == 0:
+                own_ref[k] = image
+            else:
+                sent_ref[block - 1, k] = image.astype(BF16)
+        return carry
 
     turn = turn_ref[0]
-    table = table_ref[...]
-    targets = (own_ref, sent_1, sent_2, sent_3)
-
-    def one(k, carry):
-        sky = []
-        for pair in (0, 2):
-            cells = jnp.concatenate(
-                [
-                    jnp.concatenate([early[step, k], rows[step, k]], axis=0)
-                    for step in (pair, pair + 1)
-                ],
-                axis=1,
-            )
-            sky.append(
-                jnp.dot(table, jnp.concatenate([cells, cells], axis=0), preferred_element_type=F32)
-            )
-        for block, target in enumerate(targets):
-            where = slice(32 * block, 32 * block + 32)
-            change = change_ref[k, where]
-            image = jnp.zeros((32, 128), F32)
-            for step in range(4):
-                part = sky[step // 2][:, 128 * (step % 2) : 128 * (step % 2) + 128]
-                real = part[:128][where]
-                imag = part[128:][where]
-                angle = (2.0 * math.pi * w_ref[step]) * change
-                square = angle * angle
-                sine = angle * (1.0 - square * (1.0 / 6.0))
-                cosine = 1.0 - square * (0.5 - square * (1.0 / 24.0))
-                image += (real * cosine - imag * sine) * base_ref[0, step, where]
-                image -= (real * sine + imag * cosine) * base_ref[1, step, where]
-            target[k] = image.astype(target.dtype)
-        return carry
-
+    incoming = fetch(0)
+    outgoing = []
     for half in range(2):
-        for copy in arrivals[half]:
+        for copy in incoming:
             copy.wait()
+        if half == 0:
+            incoming = fetch(1)
         for step in range(4):
-            block = late[(turn - step) & 3, :, 16 * half : 16 * half + 16]
-            rows[step, 8 * half : 8 * half + 8] = jnp.swapaxes(block, 0, 1).reshape(8, 128, 128)
+            block = late_ref[(turn - step) & 3, :, 16 * half : 16 * half + 16]
+            rows_ref[step, 8 * half : 8 * half + 8] = jnp.swapaxes(block, 0, 1).reshape(8, 128, 128)
         lax.fori_loop(8 * half, 8 * half + 8, one, 0, unroll=4)
-
-
-def column_transform(turn, w, early, late, table, base, change):
+        k = pl.ds(8 * half, 8)
+        moves = [(sent_ref.at[0, k], sent_1.at[k]), (sent_ref.at[1, k], sent_2.at[k])]
+        moves += [(sent_ref.at[2, k], sent_3.at[k]), (own_ref.at[k], own_hbm.at[k])]
+        for number, (source, target) in enumerate(moves):
+            copy = pltpu.make_async_copy(source, target, out_sems.at[4 * half + number])
+            copy.start()
+            outgoing.append(copy)
+    for copy in outgoing:
+        copy.wait()
+
+
+def late_image(turn, w, early, late, table, base, change):
     smem = pl.BlockSpec(memory_space=pltpu.SMEM)
-    vmem = pl.BlockSpec(memory_space=pltpu.VMEM)
     anywhere = pl.BlockSpec(memory_space=pl.ANY)
     return pl.pallas_call(
-        column_kernel,
-        in_specs=[smem] * 2 + [anywhere] * 5 + [vmem] + [anywhere] * 2,
-        out_specs=[vmem] * 4,
+        late_kernel,
+        in_specs=[smem] * 2 + [anywhere] * 5,
+        out_specs=[anywhere] * 4,
         out_shape=[jax.ShapeDtypeStruct((16, 32, 128), F32)]
         + [jax.ShapeDtypeStruct((16, 32, 128), BF16)] * 3,
         scratch_shapes=[
-            pltpu.VMEM((4, 16, 128, 128), BF16),
+            pltpu.VMEM((16, 128, 128), F32),
             pltpu.VMEM((4, 64, 32, 128), BF16),
             pltpu.VMEM((4, 16, 128, 128), BF16),
+            pltpu.VMEM((256, 256), BF16),
             pltpu.VMEM((2, 4, 128, 128), F32),
-            pltpu.VMEM((16, 128, 128), F32),
-            pltpu.SemaphoreType.DMA((13,)),
+            pltpu.VMEM((16, 128, 128), BF16),
+            pltpu.VMEM((16, 32, 128), F32),
+            pltpu.VMEM((3, 16, 32, 128), BF16),
+            pltpu.SemaphoreType.DMA((10,)),
+            pltpu.SemaphoreType.DMA((8,)),
         ],
         compiler_params=pltpu.CompilerParams(vmem_limit_bytes=62 * MIB),
         cost_estimate=pl.CostEstimate(
-            flops=4_300_000_000, bytes_accessed=5 << 20, transcendentals=0
+            flops=2_200_000_000, bytes_accessed=5 << 20, transcendentals=0
         ),
-        name="column_transform",
-    )(turn, w, *early, late, table, base, change)
+        name="late_column_transform",
+    )(turn, w, early, late, table, base, change)
 
 
 def place_kernel(turn_ref, *refs):
@@ -412,7 +462,7 @@
         in_specs=[pl.BlockSpec(memory_space=pltpu.SMEM)] + [vmem] * 4,
         out_specs=vmem,
         out_shape=jax.ShapeDtypeStruct((32, 64, 128), F32),
-        compiler_params=pltpu.CompilerParams(vmem_limit_bytes=16 * MIB),
+        compiler_params=pltpu.CompilerParams(vmem_limit_bytes=62 * MIB),
         cost_estimate=pl.CostEstimate(flops=1 << 20, bytes_accessed=2 << 20, transcendentals=0),
         name="place_image_rows",
     )(turn, *blocks)
@@ -473,10 +523,13 @@
 
     dealt = deal_rows(turn, early)
     dealt = [dealt[0]] + [along_wp(dealt[step], step) for step in (1, 2, 3)]
-    table = jnp.roll(jnp.asarray(column_second_table()).reshape(2, 128, 512), -32 * turn[0], axis=1)
-    own, *sent = column_transform(
-        turn, w, dealt, late, table.reshape(256, 512), base, change
-    )
+    tables = [
+        jnp.roll(jnp.asarray(column_second_table(half)).reshape(2, 128, 256), -32 * turn[0], axis=1)
+        for half in range(2)
+    ]
+    tables = [table.reshape(256, 256) for table in tables]
+    early = early_image(w, dealt, tables[0], base, change)
+    own, *sent = late_image(turn, w, early, late, tables[1], base, change)
     blocks = [own] + [along_wp(block, step + 1) for step, block in enumerate(sent)]
     return place_rows(turn, blocks).reshape(2048, 128)
 

time: 271 us -> 273 us (level)
  waiting for transfers between devices: 120 us -> 110 us
  Pallas kernels: 86.3 us -> 93.3 us
    all_to_all x1, waiting for transfers between devices: 44.3 us -> 0.01 us  [local(): lax.all_to_all(spectrum.reshape(256, 32, 128), ('wp', 'band'), split_axis...]
    ppermute x8, waiting for transfers between devices: 8.69 us -> 43.5 us  [along_wp(): return lax.ppermute(block, 'wp', pairs)]
    pallas_call x1 -> x2, Pallas kernels: 8.24 us -> 14.2 us  [the longest x1 7.48 us: late_image(): pl.pallas_call(late_kernel, in_specs=[smem] * 2 + [anywhere] * 5, out_spe...]
  transfers between devices with their start and end apart: 12 -> 12, of which waited for: 7 -> 8; matrix products, arithmetic and copies ran while one was open for 4% -> 4% of each run, Pallas kernels for 27% -> 29%
where the time goes in v6:
time: 273 us; the launch traced here: 269 us
  waiting for transfers between devices  110 us (40%)
  Pallas kernels  93.3 us (34%)
  starting transfers between devices  51.4 us (19%)
  other arithmetic  7.98 us (3%)
  local copies, waits for them, and re-layouts  4.6 us (2%)
    pallas_call x2, Pallas kernels, grid_and_rows(): pl.pallas_call(grid_kernel, in_specs=[pl.BlockSpec(memory_space=pltpu.SME...  65.6 us
    all_to_all x2, waiting for transfers between devices, local(): lax.all_to_all(packed, 'band', split_axis=0, concat_axis=0, tiled=True)  50.9 us
    ppermute x8, waiting for transfers between devices, along_wp(): return lax.ppermute(block, 'wp', pairs)  43.5 us
    all_to_all x2, starting transfers between devices, local(): lax.all_to_all(packed, 'band', split_axis=0, concat_axis=0, tiled=True)  19.4 us
    all_to_all x1, waiting for transfers between devices, local(): lax.all_to_all(spectrum.reshape(64, 128, 128), 'band', split_axis=0, conc...  16 us
    ppermute x8, starting transfers between devices, along_wp(): return lax.ppermute(block, 'wp', pairs)  13.8 us
    all_to_all x1, starting transfers between devices, local(): lax.all_to_all(spectrum.reshape(256, 32, 128), ('wp', 'band'), split_axis...  10.9 us
    pallas_call x2, Pallas kernels, pack(): pl.pallas_call(functools.partial(pack_kernel, half=half), in_specs=[smem,...  8.64 us
  transfers between devices with their start and end apart: 12, of which 8 were waited for; matrix products, arithmetic and copies ran while one was open for 4% of the time, Pallas kernels for 29%

profile of v6, /device:TPU:33, one launch (start us, length us, event | category | flops | bytes accessed | tf_op | source)
XLA Modules:
  0.0 269.3 jit_solution(6732959274520672582)
XLA Ops:
  0.7 4.3 %pack_rows.2 = bf16[64,136,128]{2,1,0:T(8,128)(2,1)} custom-call(s32[1,1]{1,0:T(1,128)S(6)} %copy.20.count_ref, s32[1,64]{1,0:T(1,128)} %bitcast.38, s32[2,64]{1,0:T(2,128)} %bitcast.36, bf16[64,2,128,128]{3,2,1,0:T(8,128)(2,1)} %bitcast.26), custom_call_target="tpu_custom_call" | custom-call | flops 8388608 | bytes 4194304 | tf_op jit(solution)/shard_map/pack_rows/pallas_call | solution.py:135
  5.0 12.1 %all-to-all-start = ((bf16[64,136,128]{2,1,0:T(8,128)(2,1)}), bf16[64,136,128]{2,1,0:T(8,128)(2,1)}, u32[]{:S(2)}, u32[]{:S(2)}) async-start(bf16[64,136,128]{2,1,0:T(8,128)(2,1)} %pack_rows.2), calls=%async_computation | async-start | bytes 4456448 | tf_op jit(solution)/shard_map/all_to_all | solution.py:500
  17.1 1.4 collective-permute-start
  18.4 0.2 fusion.22
  18.6 0.1 maximum_bitcast_fusion
  18.8 4.3 %pack_rows.3 = bf16[64,128,128]{2,1,0:T(8,128)(2,1)} custom-call(s32[1,1]{1,0:T(1,128)S(6)} %copy.20.count_ref, s32[1,64]{1,0:T(1,128)} %bitcast.39, s32[2,64]{1,0:T(2,128)} %bitcast.37, bf16[64,2,128,128]{3,2,1,0:T(8,128)(2,1)} %bitcast.27), custom_call_target="tpu_custom_call" | custom-call | flops 8388608 | bytes 4194304 | tf_op jit(solution)/shard_map/pack_rows/pallas_call | solution.py:135
  23.1 46.6 %all-to-all-done.arrived_ref = bf16[64,136,128]{2,1,0:T(8,128)(2,1)} async-done(((bf16[64,136,128]{2,1,0:T(8,128)(2,1)}), bf16[64,136,128]{2,1,0:T(8,128)(2,1)}, u32[]{:S(2)}, u32[]{:S(2)}) %all-to-all-start) | async-done | bytes 2228256 | tf_op jit(solution)/shard_map/all_to_all | solution.py:500
  69.7 7.3 %all-to-all-start.2 = ((bf16[64,128,128]{2,1,0:T(8,128)(2,1)}), bf16[64,128,128]{2,1,0:T(8,128)(2,1)}, u32[]{:S(2)}, u32[]{:S(2)}) async-start(bf16[64,128,128]{2,1,0:T(8,128)(2,1)} %pack_rows.3), calls=%async_computation.2 | async-start | bytes 4194304 | tf_op jit(solution)/shard_map/all_to_all | solution.py:500
  77.7 0.6 pad_maximum_fusion.2.bands_ref
  78.4 0.4 sqrt_add_fusion
  78.8 1.3 subtract_convert_fusion.change_ref.change_hbm
  80.1 0.7 pad_maximum_fusion.7
  80.8 2.9 %collective-permute-start.1 = (f32[2]{0:T(128)S(1)}, f32[2]{0:T(128)S(1)}, u32[]{:S(2)}, u32[]{:S(2)}) collective-permute-start(f32[2]{0:T(128)S(1)} %pad_maximum_fusion.7), channel_id=1, source_target_pairs={{0,2},{1,3},{2,0},{3,1},{4,6},{5,7},{6,4},{7,5},{8,10},{9,11},{10,... | collective-permute-start | bytes 32 | tf_op jit(solution)/shard_map/ppermute | solution.py:473
  83.7 1.4 collective-permute-done.1
  85.1 1.2 broadcast_multiply_fusion
  86.4 1.0 multiply_cosine_fusion
  87.4 0.8 pad_maximum_fusion.base_ref.base_hbm
  88.2 0.9 slice.21
  89.1 0.6 fusion.10.place_ref
  89.8 32.8 %place_and_transform.2 = bf16[1,64,128,128]{3,2,1,0:T(8,128)(2,1)} custom-call(s32[64,64]{1,0:T(8,128)} %fusion.10.place_ref, bf16[64,136,128]{2,1,0:T(8,128)(2,1)} %all-to-all-done.arrived_ref, bf16[128,384]{1,0:T(8,128)(2,1)} %constant.101.clone.first_ref, f32[2,128,128]{2,1,0:T(8,128)} %constant.102.clone.twiddle_ref, ...), custom_call_target="tpu_custom_call" | custom-call | flops 20000000000 | bytes 4194304 | tf_op jit(solution)/shard_map/place_and_transform/pallas_call | solution.py:255
  122.6 4.3 %all-to-all-done.2.arrived_ref = bf16[64,128,128]{2,1,0:T(8,128)(2,1)} async-done(((bf16[64,128,128]{2,1,0:T(8,128)(2,1)}), bf16[64,128,128]{2,1,0:T(8,128)(2,1)}, u32[]{:S(2)}, u32[]{:S(2)}) %all-to-all-start.2) | async-done | bytes 2097184 | tf_op jit(solution)/shard_map/all_to_all | solution.py:500
  126.9 7.3 %all-to-all-start.1 = ((bf16[64,128,128]{2,1,0:T(8,128)(2,1)}), bf16[64,128,128]{2,1,0:T(8,128)(2,1)}, u32[]{:S(2)}, u32[]{:S(2)}) async-start(bf16[64,128,128]{2,1,0:T(8,128)(2,1)} %bitcast.29), calls=%async_computation.1 | async-start | bytes 4194304 | tf_op jit(solution)/shard_map/all_to_all | solution.py:516
  134.2 0.1 fusion.23
  134.4 0.1 pad_maximum_fusion.5
  134.5 0.1 pad_maximum_fusion.3
  134.6 0.6 pad_maximum_fusion.4.bands_ref
  135.2 32.8 %place_and_transform.3 = bf16[4,64,32,128]{3,2,1,0:T(8,128)(2,1)} custom-call(s32[64,64]{1,0:T(8,128)} %fusion.10.place_ref, bf16[64,128,128]{2,1,0:T(8,128)(2,1)} %all-to-all-done.2.arrived_ref, bf16[128,384]{1,0:T(8,128)(2,1)} %constant.101.clone.first_ref, f32[2,128,128]{2,1,0:T(8,128)} %constant.102.clone.twiddle_ref, ...), custom_call_target="tpu_custom_call" | custom-call | flops 20000000000 | bytes 4194304 | tf_op jit(solution)/shard_map/place_and_transform/pallas_call | solution.py:255
  168.0 16.0 %all-to-all-done.1.columns_ref = bf16[64,128,128]{2,1,0:T(8,128)(2,1)} async-done(((bf16[64,128,128]{2,1,0:T(8,128)(2,1)}), bf16[64,128,128]{2,1,0:T(8,128)(2,1)}, u32[]{:S(2)}, u32[]{:S(2)}) %all-to-all-start.1) | async-done | bytes 2097184 | tf_op jit(solution)/shard_map/all_to_all | solution.py:516
  184.1 10.9 %all-to-all-start.3 = ((bf16[256,32,128]{2,1,0:T(8,128)(2,1)}), bf16[256,32,128]{2,1,0:T(8,128)(2,1)}, u32[]{:S(2)}, u32[]{:S(2)}) async-start(bf16[256,32,128]{2,1,0:T(8,128)(2,1)} %bitcast.28), calls=%async_computation.3 | async-start | bytes 4194304 | tf_op jit(solution)/shard_map/all_to_all | solution.py:520
  195.0 2.5 deal_rows.1
  197.5 0.8 copy-done
  198.3 1.2 collective-permute-start.2
  199.6 2.5 collective-permute-start.3
  202.1 1.1 collective-permute-start.4
  203.2 0.7 constant_dynamic-slice_fusion.1
  203.9 0.7 constant_dynamic-slice_fusion
  204.6 17.7 %collective-permute-done.2.early_1 = bf16[16,128,128]{2,1,0:T(8,128)(2,1)S(1)} collective-permute-done((bf16[16,128,128]{2,1,0:T(8,128)(2,1)S(1)}, bf16[16,128,128]{2,1,0:T(8,128)(2,1)S(1)}, u32[]{:S(2)}, u32[]{:S(2)}) %collective-permute-start.2) | collective-permute-done | bytes 524320 | tf_op jit(solution)/shard_map/ppermute | solution.py:473
  222.2 19.4 %collective-permute-done.3.early_2 = bf16[16,128,128]{2,1,0:T(8,128)(2,1)S(1)} collective-permute-done((bf16[16,128,128]{2,1,0:T(8,128)(2,1)S(1)}, bf16[16,128,128]{2,1,0:T(8,128)(2,1)S(1)}, u32[]{:S(2)}, u32[]{:S(2)}) %collective-permute-start.3) | collective-permute-done | bytes 524320 | tf_op jit(solution)/shard_map/ppermute | solution.py:473
  241.7 0.8 copy-done.7
  242.4 6.8 %early_column_transform.1.early_hbm = f32[16,128,128]{2,1,0:T(8,128)} custom-call(f32[4]{0:T(128)} %get-tuple-element.29.w_ref, bf16[16,128,128]{2,1,0:T(8,128)(2,1)} %copy-done, bf16[16,128,128]{2,1,0:T(8,128)(2,1)} %copy-done.6, bf16[16,128,128]{2,1,0:T(8,128)(2,1)} %copy-done.7, bf16[16,128,128]{2,1,0:T(8,128)(2,1)} %collective-permute-done.4.early_3, ...), custom_call_target="tpu_custom_call" | custom-call | flops 2200000000 | bytes 5242880 | tf_op jit(solution)/shard_map/early_column_transform/pallas_call | solution.py:350
  249.2 7.5 %late_column_transform.1 = (f32[16,32,128]{2,1,0:T(8,128)}, bf16[16,32,128]{2,1,0:T(8,128)(2,1)}, bf16[16,32,128]{2,1,0:T(8,128)(2,1)}, bf16[16,32,128]{2,1,0:T(8,128)(2,1)}) custom-call(s32[1]{0:T(128)} %bitcast.turn_ref, f32[4]{0:T(128)} %get-tuple-element.29.w_ref, f32[16,128,128]{2,1,0:T(8,128)} %early_column_transform.1.early_hbm, ...), custom_call_target="tpu_custom_call" | custom-call | flops 2200000000 | bytes 5242880 | tf_op jit(solution)/shard_map/late_column_transform/pallas_call | solution.py:423
  256.7 0.1 collective-permute-start.5
  256.8 3.5 %collective-permute-start.6 = (bf16[16,32,128]{2,1,0:T(8,128)(2,1)}, bf16[16,32,128]{2,1,0:T(8,128)(2,1)S(1)}, u32[]{:S(2)}, u32[]{:S(2)}) collective-permute-start(bf16[16,32,128]{2,1,0:T(8,128)(2,1)} %get-tuple-element.26), channel_id=1, source_target_pairs={{0,2},{1,3},{2,0},{3,1},{4,6},{5,7},{6,4},{7,5},{8,10},{9,11},{10,... | collective-permute-start | bytes 393224 | tf_op jit(solution)/shard_map/ppermute | solution.py:473
  260.2 1.1 collective-permute-start.7
  261.3 0.7 collective-permute-done.5.refs_1_
  262.0 4.3 %collective-permute-done.6.refs_2_ = bf16[16,32,128]{2,1,0:T(8,128)(2,1)S(1)} collective-permute-done((bf16[16,32,128]{2,1,0:T(8,128)(2,1)}, bf16[16,32,128]{2,1,0:T(8,128)(2,1)S(1)}, u32[]{:S(2)}, u32[]{:S(2)}) %collective-permute-start.6) | collective-permute-done | bytes 131104 | tf_op jit(solution)/shard_map/ppermute | solution.py:473
  266.4 0.6 copy-done.2
  267.1 2.3 place_image_rows.1
  (28 shorter events, 0.3 us)
Async XLA Ops:
  5.0 64.8 %all-to-all-start = ((bf16[64,136,128]{2,1,0:T(8,128)(2,1)}), bf16[64,136,128]{2,1,0:T(8,128)(2,1)}, u32[]{:S(2)}, u32[]{:S(2)}) async-start(bf16[64,136,128]{2,1,0:T(8,128)(2,1)} %pack_rows.2), calls=%async_computation | async-start | bytes 4456448 | tf_op jit(solution)/shard_map/all_to_all | solution.py:500
  17.1 63.0 %collective-permute-start = (f32[1]{0:T(128)}, f32[1]{0:T(128)}, u32[]{:S(2)}, u32[]{:S(2)}) collective-permute-start(f32[1]{0:T(128)} %param.16), channel_id=1, source_target_pairs={{0,1},{1,2},{2,3},{3,0},{4,5},{5,6},{6,7},{7,4},{8,9},{9,10},{10,1... | collective-permute-start | bytes 20 | tf_op jit(solution)/shard_map/ppermute | solution.py:473
  69.7 57.2 %all-to-all-start.2 = ((bf16[64,128,128]{2,1,0:T(8,128)(2,1)}), bf16[64,128,128]{2,1,0:T(8,128)(2,1)}, u32[]{:S(2)}, u32[]{:S(2)}) async-start(bf16[64,128,128]{2,1,0:T(8,128)(2,1)} %pack_rows.3), calls=%async_computation.2 | async-start | bytes 4194304 | tf_op jit(solution)/shard_map/all_to_all | solution.py:500
  80.8 4.3 %collective-permute-start.1 = (f32[2]{0:T(128)S(1)}, f32[2]{0:T(128)S(1)}, u32[]{:S(2)}, u32[]{:S(2)}) collective-permute-start(f32[2]{0:T(128)S(1)} %pad_maximum_fusion.7), channel_id=1, source_target_pairs={{0,2},{1,3},{2,0},{3,1},{4,6},{5,7},{6,4},{7,5},{8,10},{9,11},{10,... | collective-permute-start | bytes 32 | tf_op jit(solution)/shard_map/ppermute | solution.py:473
  126.9 57.2 %all-to-all-start.1 = ((bf16[64,128,128]{2,1,0:T(8,128)(2,1)}), bf16[64,128,128]{2,1,0:T(8,128)(2,1)}, u32[]{:S(2)}, u32[]{:S(2)}) async-start(bf16[64,128,128]{2,1,0:T(8,128)(2,1)} %bitcast.29), calls=%async_computation.1 | async-start | bytes 4194304 | tf_op jit(solution)/shard_map/all_to_all | solution.py:516
  184.1 65.1 %all-to-all-start.3 = ((bf16[256,32,128]{2,1,0:T(8,128)(2,1)}), bf16[256,32,128]{2,1,0:T(8,128)(2,1)}, u32[]{:S(2)}, u32[]{:S(2)}) async-start(bf16[256,32,128]{2,1,0:T(8,128)(2,1)} %bitcast.28), calls=%async_computation.3 | async-start | bytes 4194304 | tf_op jit(solution)/shard_map/all_to_all | solution.py:520
  195.0 8.2 %copy-start.5 = (bf16[2,256,256]{2,1,0:T(8,128)(2,1)S(1)}, bf16[2,256,256]{2,1,0:T(8,128)(2,1)}, u32[]{:S(2)}) copy-start(bf16[2,256,256]{2,1,0:T(8,128)(2,1)} %constant.115) | copy-start | bytes 786436
  195.0 8.9 %copy-start.4 = (bf16[2,256,256]{2,1,0:T(8,128)(2,1)S(1)}, bf16[2,256,256]{2,1,0:T(8,128)(2,1)}, u32[]{:S(2)}) copy-start(bf16[2,256,256]{2,1,0:T(8,128)(2,1)} %constant.116) | copy-start | bytes 786436
  197.5 0.8 copy-start
  198.3 23.9 %collective-permute-start.2 = (bf16[16,128,128]{2,1,0:T(8,128)(2,1)S(1)}, bf16[16,128,128]{2,1,0:T(8,128)(2,1)S(1)}, u32[]{:S(2)}, u32[]{:S(2)}) collective-permute-start(bf16[16,128,128]{2,1,0:T(8,128)(2,1)S(1)} %get-tuple-element.19), channel_id=1, source_target_pairs={{0,1},{1,2},{2,3},{3,0},{4,5},{5,6},{6,7},{7,4},{8,9},{9,10},{10,1... | collective-permute-start | bytes 1572872 | tf_op jit(solution)/shard_map/ppermute | solution.py:473
  199.6 42.1 %collective-permute-start.3 = (bf16[16,128,128]{2,1,0:T(8,128)(2,1)S(1)}, bf16[16,128,128]{2,1,0:T(8,128)(2,1)S(1)}, u32[]{:S(2)}, u32[]{:S(2)}) collective-permute-start(bf16[16,128,128]{2,1,0:T(8,128)(2,1)S(1)} %get-tuple-element.20), channel_id=1, source_target_pairs={{0,2},{1,3},{2,0},{3,1},{4,6},{5,7},{6,4},{7,5},{8,10},{9,11},{10,... | collective-permute-start | bytes 1572872 | tf_op jit(solution)/shard_map/ppermute | solution.py:473
  202.1 39.5 %collective-permute-start.4 = (bf16[16,128,128]{2,1,0:T(8,128)(2,1)S(1)}, bf16[16,128,128]{2,1,0:T(8,128)(2,1)}, u32[]{:S(2)}, u32[]{:S(2)}) collective-permute-start(bf16[16,128,128]{2,1,0:T(8,128)(2,1)S(1)} %get-tuple-element.21), channel_id=1, source_target_pairs={{0,3},{1,0},{2,1},{3,2},{4,7},{5,4},{6,5},{7,6},{8,11},{9,8},{10,9... | collective-permute-start | bytes 1572872 | tf_op jit(solution)/shard_map/ppermute | solution.py:473
  222.2 19.4 %copy-start.6 = (bf16[16,128,128]{2,1,0:T(8,128)(2,1)}, bf16[16,128,128]{2,1,0:T(8,128)(2,1)S(1)}, u32[]{:S(2)}) copy-start(bf16[16,128,128]{2,1,0:T(8,128)(2,1)S(1)} %collective-permute-done.2.early_1) | copy-start | bytes 1572868
  241.6 0.8 copy-start.7
  256.7 5.3 %collective-permute-start.5 = (bf16[16,32,128]{2,1,0:T(8,128)(2,1)}, bf16[16,32,128]{2,1,0:T(8,128)(2,1)S(1)}, u32[]{:S(2)}, u32[]{:S(2)}) collective-permute-start(bf16[16,32,128]{2,1,0:T(8,128)(2,1)} %get-tuple-element.25), channel_id=1, source_target_pairs={{0,1},{1,2},{2,3},{3,0},{4,5},{5,6},{6,7},{7,4},{8,9},{9,10},{10,1... | collective-permute-start | bytes 393224 | tf_op jit(solution)/shard_map/ppermute | solution.py:473
  256.8 9.6 %collective-permute-start.6 = (bf16[16,32,128]{2,1,0:T(8,128)(2,1)}, bf16[16,32,128]{2,1,0:T(8,128)(2,1)S(1)}, u32[]{:S(2)}, u32[]{:S(2)}) collective-permute-start(bf16[16,32,128]{2,1,0:T(8,128)(2,1)} %get-tuple-element.26), channel_id=1, source_target_pairs={{0,2},{1,3},{2,0},{3,1},{4,6},{5,7},{6,4},{7,5},{8,10},{9,11},{10,... | collective-permute-start | bytes 393224 | tf_op jit(solution)/shard_map/ppermute | solution.py:473
  260.2 6.1 %collective-permute-start.7 = (bf16[16,32,128]{2,1,0:T(8,128)(2,1)}, bf16[16,32,128]{2,1,0:T(8,128)(2,1)S(1)}, u32[]{:S(2)}, u32[]{:S(2)}) collective-permute-start(bf16[16,32,128]{2,1,0:T(8,128)(2,1)} %get-tuple-element.27), channel_id=1, source_target_pairs={{0,3},{1,0},{2,1},{3,2},{4,7},{5,4},{6,5},{7,6},{8,11},{9,8},{10,9... | collective-permute-start | bytes 393224 | tf_op jit(solution)/shard_map/ppermute | solution.py:473
  262.0 4.4 %copy-start.1 = (bf16[16,32,128]{2,1,0:T(8,128)(2,1)}, bf16[16,32,128]{2,1,0:T(8,128)(2,1)S(1)}, u32[]{:S(2)}) copy-start(bf16[16,32,128]{2,1,0:T(8,128)(2,1)S(1)} %collective-permute-done.5.refs_1_) | copy-start | bytes 393220
  266.3 0.6 copy-start.2
  266.4 0.7 copy-start.3

commit v7 on v6

--- a/solution.py
+++ b/solution.py
@@ -248,8 +248,8 @@
         copy.wait()
 
 
-def grid_and_rows(places, arrived, first, twiddle, second, bands, parts):
-    shape = (parts, 64, 128 // parts, 128)
+def grid_and_rows(places, arrived, first, twiddle, second, bands):
+    shape = (4, 64, 32, 128)
     vmem = pl.BlockSpec(memory_space=pltpu.VMEM)
     anywhere = pl.BlockSpec(memory_space=pl.ANY)
     return pl.pallas_call(
@@ -272,28 +272,6 @@
     )(places, arrived, first, twiddle, second, bands)
 
 
-def deal_kernel(turn_ref, columns_ref, *out_refs):
-    for step, out_ref in enumerate(out_refs):
-        begin = ((turn_ref[0] + step) & 3) * 32
-        for group in range(2):
-            where = pl.ds(pl.multiple_of(begin + 16 * group, 16), 16)
-            rows = jnp.swapaxes(columns_ref[:, where, :], 0, 1).reshape(8, 128, 128)
-            out_ref[8 * group : 8 * group + 8] = rows
-
-
-def deal_rows(turn, columns):
-    vmem = pl.BlockSpec(memory_space=pltpu.VMEM)
-    return pl.pallas_call(
-        deal_kernel,
-        in_specs=[pl.BlockSpec(memory_space=pltpu.SMEM), vmem],
-        out_specs=[vmem] * 4,
-        out_shape=[jax.ShapeDtypeStruct((16, 128, 128), BF16)] * 4,
-        compiler_params=pltpu.CompilerParams(vmem_limit_bytes=16 * MIB),
-        cost_estimate=pl.CostEstimate(flops=1 << 20, bytes_accessed=4 << 20, transcendentals=0),
-        name="deal_rows",
-    )(turn, columns)
-
-
 def base_phases(turn, me, w):
     k = jnp.arange(16, dtype=jnp.int32)[:, None, None]
     row = 64 * ((jnp.arange(128, dtype=jnp.int32)[:, None] + 32 * turn) % 128) + 16 * turn + k
@@ -331,9 +309,18 @@
     return image
 
 
-def early_kernel(w_ref, early_0, early_1, early_2, early_3, table_ref, base_ref, change_ref, out_ref):
+def turn_rows(turn, rows_ref, columns_ref, half):
+    for step in range(4):
+        block = columns_ref[(turn - step) & 3, :, 16 * half : 16 * half + 16]
+        rows_ref[step, 8 * half : 8 * half + 8] = jnp.swapaxes(block, 0, 1).reshape(8, 128, 128)
+
+
+def early_kernel(turn_ref, w_ref, early_ref, table_ref, base_ref, change_ref, out_ref, rows_ref):
+    for half in range(2):
+        turn_rows(turn_ref[0], rows_ref, early_ref, half)
+
     def one(k, carry):
-        sky = transform_planes(table_ref, [ref[k] for ref in (early_0, early_1, early_2, early_3)])
+        sky = transform_planes(table_ref, [rows_ref[step, k] for step in range(4)])
         for block in range(4):
             where = slice(32 * block, 32 * block + 32)
             change = change_ref[k, where].astype(F32)
@@ -345,19 +332,21 @@
     lax.fori_loop(0, 16, one, 0, unroll=2)
 
 
-def early_image(w, early, table, base, change):
+def early_image(turn, w, early, table, base, change):
+    smem = pl.BlockSpec(memory_space=pltpu.SMEM)
     vmem = pl.BlockSpec(memory_space=pltpu.VMEM)
     return pl.pallas_call(
         early_kernel,
-        in_specs=[pl.BlockSpec(memory_space=pltpu.SMEM)] + [vmem] * 7,
+        in_specs=[smem] * 2 + [vmem] * 4,
         out_specs=vmem,
         out_shape=jax.ShapeDtypeStruct((16, 128, 128), F32),
+        scratch_shapes=[pltpu.VMEM((4, 16, 128, 128), BF16)],
         compiler_params=pltpu.CompilerParams(vmem_limit_bytes=62 * MIB),
         cost_estimate=pl.CostEstimate(
             flops=2_200_000_000, bytes_accessed=5 << 20, transcendentals=0
         ),
         name="early_column_transform",
-    )(w, *early, table, base, change)
+    )(turn, w, early, table, base, change)
 
 
 def late_kernel(
@@ -402,9 +391,7 @@
             copy.wait()
         if half == 0:
             incoming = fetch(1)
-        for step in range(4):
-            block = late_ref[(turn - step) & 3, :, 16 * half : 16 * half + 16]
-            rows_ref[step, 8 * half : 8 * half + 8] = jnp.swapaxes(block, 0, 1).reshape(8, 128, 128)
+        turn_rows(turn, rows_ref, late_ref, half)
         lax.fori_loop(8 * half, 8 * half + 8, one, 0, unroll=4)
         k = pl.ds(8 * half, 8)
         moves = [(sent_ref.at[0, k], sent_1.at[k]), (sent_ref.at[1, k], sent_2.at[k])]
@@ -462,7 +449,7 @@
         in_specs=[pl.BlockSpec(memory_space=pltpu.SMEM)] + [vmem] * 4,
         out_specs=vmem,
         out_shape=jax.ShapeDtypeStruct((32, 64, 128), F32),
-        compiler_params=pltpu.CompilerParams(vmem_limit_bytes=62 * MIB),
+        compiler_params=pltpu.CompilerParams(vmem_limit_bytes=16 * MIB),
         cost_estimate=pl.CostEstimate(flops=1 << 20, bytes_accessed=2 << 20, transcendentals=0),
         name="place_image_rows",
     )(turn, *blocks)
@@ -507,29 +494,24 @@
     base, change = base_phases(turn[0], me, w)
     places, base, change = lax.optimization_barrier((places, base, change))
 
-    early = late = None
+    columns = []
     for half in range(2):
         spectrum = grid_and_rows(
-            places, arrived[half], first, twiddle, second, band_table(me + 64 * half), 4 if half else 1
-        )
-        if half == 0:
-            early = lax.all_to_all(
-                spectrum.reshape(64, 128, 128), "band", split_axis=0, concat_axis=0, tiled=True
-            )
-        else:
-            late = lax.all_to_all(
+            places, arrived[half], first, twiddle, second, band_table(me + 64 * half)
+        )
+        columns.append(
+            lax.all_to_all(
                 spectrum.reshape(256, 32, 128), ("wp", "band"), split_axis=0, concat_axis=0, tiled=True
             ).reshape(4, 64, 32, 128)
-
-    dealt = deal_rows(turn, early)
-    dealt = [dealt[0]] + [along_wp(dealt[step], step) for step in (1, 2, 3)]
+        )
+
     tables = [
         jnp.roll(jnp.asarray(column_second_table(half)).reshape(2, 128, 256), -32 * turn[0], axis=1)
         for half in range(2)
     ]
     tables = [table.reshape(256, 256) for table in tables]
-    early = early_image(w, dealt, tables[0], base, change)
-    own, *sent = late_image(turn, w, early, late, tables[1], base, change)
+    early = early_image(turn, w, columns[0], tables[0], base, change)
+    own, *sent = late_image(turn, w, early, columns[1], tables[1], base, change)
     blocks = [own] + [along_wp(block, step + 1) for step, block in enumerate(sent)]
     return place_rows(turn, blocks).reshape(2048, 128)
 

time: 273 us -> 271 us (level); the launches traced: 269 us -> 270 us
  waiting for transfers between devices: 110 us -> 122 us
  starting transfers between devices: 51.4 us -> 44.7 us
  Pallas kernels: 93.3 us -> 90.4 us
    all_to_all x1 -> x2, waiting for transfers between devices: 0.01 us -> 62.9 us  [local(): lax.all_to_all(spectrum.reshape(256, 32, 128), ('wp', 'band'), split_axis...]
    ppermute x8 -> x5, waiting for transfers between devices: 43.5 us -> 8.64 us  [along_wp(): return lax.ppermute(block, 'wp', pairs)]
    all_to_all x1 -> x0, waiting for transfers between devices: 16 us -> none  [local(): lax.all_to_all(spectrum.reshape(64, 128, 128), 'band', split_axis=0, conc...]
    all_to_all x1 -> x0, starting transfers between devices: 7.32 us -> none  [local(): lax.all_to_all(spectrum.reshape(64, 128, 128), 'band', split_axis=0, conc...]
    all_to_all x1 -> x2, starting transfers between devices: 10.9 us -> 18.1 us  [local(): lax.all_to_all(spectrum.reshape(256, 32, 128), ('wp', 'band'), split_axis...]
    ppermute x8 -> x5, starting transfers between devices: 13.8 us -> 7.24 us  [along_wp(): return lax.ppermute(block, 'wp', pairs)]
    pallas_call x2 -> x1, Pallas kernels: 9.26 us -> 7.43 us  [early_image(): pl.pallas_call(early_kernel, in_specs=[smem] * 2 + [vmem] * 4, out_specs=...]
  transfers between devices with their start and end apart: 12 -> 9, of which waited for: 8 -> 7; matrix products, arithmetic and copies ran while one was open for 4% -> 4% of each run, Pallas kernels for 29% -> 29%
where the time goes in v7:
time: 271 us; the launch traced here: 270 us
  waiting for transfers between devices  122 us (45%)
  Pallas kernels  90.4 us (33%)
  starting transfers between devices  44.7 us (16%)
  other arithmetic  8.05 us (3%)
  local copies, waits for them, and re-layouts  3.28 us (1%)
    pallas_call x2, Pallas kernels, grid_and_rows(): pl.pallas_call(grid_kernel, in_specs=[pl.BlockSpec(memory_space=pltpu.SME...  65.7 us
    all_to_all x2, waiting for transfers between devices, local(): lax.all_to_all(spectrum.reshape(256, 32, 128), ('wp', 'band'), split_axis...  62.9 us
    all_to_all x2, waiting for transfers between devices, local(): lax.all_to_all(packed, 'band', split_axis=0, concat_axis=0, tiled=True)  50.8 us
    all_to_all x2, starting transfers between devices, local(): lax.all_to_all(packed, 'band', split_axis=0, concat_axis=0, tiled=True)  19.4 us
    all_to_all x2, starting transfers between devices, local(): lax.all_to_all(spectrum.reshape(256, 32, 128), ('wp', 'band'), split_axis...  18.1 us
    ppermute x5, waiting for transfers between devices, along_wp(): return lax.ppermute(block, 'wp', pairs)  8.64 us
    pallas_call x2, Pallas kernels, pack(): pl.pallas_call(functools.partial(pack_kernel, half=half), in_specs=[smem,...  8.63 us
    pallas_call x1, Pallas kernels, late_image(): pl.pallas_call(late_kernel, in_specs=[smem] * 2 + [anywhere] * 5, out_spe...  7.49 us
  transfers between devices with their start and end apart: 9, of which 7 were waited for; matrix products, arithmetic and copies ran while one was open for 4% of the time, Pallas kernels for 29%

profile of v7, /device:TPU:33, one launch (start us, length us, event | category | flops | bytes accessed | tf_op | source)
XLA Modules:
  0.0 270.4 jit_solution(3246785750185805187)
XLA Ops:
  0.7 4.3 %pack_rows.2 = bf16[64,136,128]{2,1,0:T(8,128)(2,1)} custom-call(s32[1,1]{1,0:T(1,128)S(6)} %copy.20.count_ref, s32[1,64]{1,0:T(1,128)} %bitcast.39, s32[2,64]{1,0:T(2,128)} %bitcast.37, bf16[64,2,128,128]{3,2,1,0:T(8,128)(2,1)} %bitcast.27), custom_call_target="tpu_custom_call" | custom-call | flops 8388608 | bytes 4194304 | tf_op jit(solution)/shard_map/pack_rows/pallas_call | solution.py:135
  5.0 12.1 %all-to-all-start = ((bf16[64,136,128]{2,1,0:T(8,128)(2,1)}), bf16[64,136,128]{2,1,0:T(8,128)(2,1)}, u32[]{:S(2)}, u32[]{:S(2)}) async-start(bf16[64,136,128]{2,1,0:T(8,128)(2,1)} %pack_rows.2), calls=%async_computation | async-start | bytes 4456448 | tf_op jit(solution)/shard_map/all_to_all | solution.py:487
  17.1 1.4 collective-permute-start
  18.4 0.2 fusion.22
  18.6 0.1 maximum_bitcast_fusion
  18.7 0.1 copy.16
  18.8 4.3 %pack_rows.3 = bf16[64,128,128]{2,1,0:T(8,128)(2,1)} custom-call(s32[1,1]{1,0:T(1,128)S(6)} %copy.20.count_ref, s32[1,64]{1,0:T(1,128)} %bitcast.40, s32[2,64]{1,0:T(2,128)} %bitcast.38, bf16[64,2,128,128]{3,2,1,0:T(8,128)(2,1)} %bitcast.28), custom_call_target="tpu_custom_call" | custom-call | flops 8388608 | bytes 4194304 | tf_op jit(solution)/shard_map/pack_rows/pallas_call | solution.py:135
  23.1 46.6 %all-to-all-done.arrived_ref = bf16[64,136,128]{2,1,0:T(8,128)(2,1)} async-done(((bf16[64,136,128]{2,1,0:T(8,128)(2,1)}), bf16[64,136,128]{2,1,0:T(8,128)(2,1)}, u32[]{:S(2)}, u32[]{:S(2)}) %all-to-all-start) | async-done | bytes 2228256 | tf_op jit(solution)/shard_map/all_to_all | solution.py:487
  69.7 7.3 %all-to-all-start.2 = ((bf16[64,128,128]{2,1,0:T(8,128)(2,1)}), bf16[64,128,128]{2,1,0:T(8,128)(2,1)}, u32[]{:S(2)}, u32[]{:S(2)}) async-start(bf16[64,128,128]{2,1,0:T(8,128)(2,1)} %pack_rows.3), calls=%async_computation.2 | async-start | bytes 4194304 | tf_op jit(solution)/shard_map/all_to_all | solution.py:487
  77.7 0.6 pad_maximum_fusion.2.bands_ref
  78.4 0.4 sqrt_add_fusion
  78.8 1.3 subtract_convert_fusion.change_ref.change_hbm
  80.1 0.0 collective-permute-done
  80.1 0.7 pad_maximum_fusion.7
  80.9 2.9 %collective-permute-start.1 = (f32[2]{0:T(128)S(1)}, f32[2]{0:T(128)S(1)}, u32[]{:S(2)}, u32[]{:S(2)}) collective-permute-start(f32[2]{0:T(128)S(1)} %pad_maximum_fusion.7), channel_id=1, source_target_pairs={{0,2},{1,3},{2,0},{3,1},{4,6},{5,7},{6,4},{7,5},{8,10},{9,11},{10,... | collective-permute-start | bytes 32 | tf_op jit(solution)/shard_map/ppermute | solution.py:460
  83.8 1.4 collective-permute-done.1
  85.2 1.3 broadcast_multiply_fusion
  86.4 1.0 multiply_cosine_fusion
  87.4 0.8 pad_maximum_fusion.base_ref.base_hbm
  88.3 0.9 slice.21
  89.2 0.6 fusion.10.place_ref
  89.8 32.8 %place_and_transform.2 = bf16[4,64,32,128]{3,2,1,0:T(8,128)(2,1)} custom-call(s32[64,64]{1,0:T(8,128)} %fusion.10.place_ref, bf16[64,136,128]{2,1,0:T(8,128)(2,1)} %all-to-all-done.arrived_ref, bf16[128,384]{1,0:T(8,128)(2,1)} %constant.101.clone.first_ref, f32[2,128,128]{2,1,0:T(8,128)} %constant.102.clone.twiddle_ref, ...), custom_call_target="tpu_custom_call" | custom-call | flops 20000000000 | bytes 4194304 | tf_op jit(solution)/shard_map/place_and_transform/pallas_call | solution.py:255
  122.7 4.2 %all-to-all-done.2.arrived_ref = bf16[64,128,128]{2,1,0:T(8,128)(2,1)} async-done(((bf16[64,128,128]{2,1,0:T(8,128)(2,1)}), bf16[64,128,128]{2,1,0:T(8,128)(2,1)}, u32[]{:S(2)}, u32[]{:S(2)}) %all-to-all-start.2) | async-done | bytes 2097184 | tf_op jit(solution)/shard_map/all_to_all | solution.py:487
  126.9 10.9 %all-to-all-start.1 = ((bf16[256,32,128]{2,1,0:T(8,128)(2,1)}), bf16[256,32,128]{2,1,0:T(8,128)(2,1)}, u32[]{:S(2)}, u32[]{:S(2)}) async-start(bf16[256,32,128]{2,1,0:T(8,128)(2,1)} %bitcast.30), calls=%async_computation.1 | async-start | bytes 4194304 | tf_op jit(solution)/shard_map/all_to_all | solution.py:503
  137.8 0.1 fusion.23
  138.0 0.1 pad_maximum_fusion.5
  138.1 0.1 pad_maximum_fusion.3
  138.2 0.6 pad_maximum_fusion.4.bands_ref
  138.8 32.8 %place_and_transform.3 = bf16[4,64,32,128]{3,2,1,0:T(8,128)(2,1)} custom-call(s32[64,64]{1,0:T(8,128)} %fusion.10.place_ref, bf16[64,128,128]{2,1,0:T(8,128)(2,1)} %all-to-all-done.2.arrived_ref, bf16[128,384]{1,0:T(8,128)(2,1)} %constant.101.clone.first_ref, f32[2,128,128]{2,1,0:T(8,128)} %constant.102.clone.twiddle_ref, ...), custom_call_target="tpu_custom_call" | custom-call | flops 20000000000 | bytes 4194304 | tf_op jit(solution)/shard_map/place_and_transform/pallas_call | solution.py:255
  171.7 19.4 %all-to-all-done.1 = bf16[256,32,128]{2,1,0:T(8,128)(2,1)} async-done(((bf16[256,32,128]{2,1,0:T(8,128)(2,1)}), bf16[256,32,128]{2,1,0:T(8,128)(2,1)}, u32[]{:S(2)}, u32[]{:S(2)}) %all-to-all-start.1) | async-done | bytes 2097184 | tf_op jit(solution)/shard_map/all_to_all | solution.py:503
  191.0 0.0 copy-start.2
  191.0 0.0 copy-start.1
  191.0 7.2 %all-to-all-start.3 = ((bf16[256,32,128]{2,1,0:T(8,128)(2,1)}), bf16[256,32,128]{2,1,0:T(8,128)(2,1)}, u32[]{:S(2)}, u32[]{:S(2)}) async-start(bf16[256,32,128]{2,1,0:T(8,128)(2,1)} %bitcast.29), calls=%async_computation.3 | async-start | bytes 4194304 | tf_op jit(solution)/shard_map/all_to_all | solution.py:503
  198.2 0.0 copy-done.2
  198.2 0.7 constant_dynamic-slice_fusion.1
  198.9 0.0 copy-done.1
  198.9 0.7 constant_dynamic-slice_fusion
  199.6 7.4 %early_column_transform.1.early_hbm = f32[16,128,128]{2,1,0:T(8,128)} custom-call(s32[1]{0:T(128)} %bitcast.turn_ref, f32[4]{0:T(128)} %get-tuple-element.21.w_ref, bf16[4,64,32,128]{3,2,1,0:T(8,128)(2,1)} %bitcast.11.early_ref, bf16[256,256]{1,0:T(8,128)(2,1)} %bitcast.34, f32[2,4,128,128]{3,2,1,0:T(8,128)} %pad_maximum_fusion.base_ref.base_hbm, ...), custom_call_target="tpu_custom_call" | custom-call | flops 2200000000 | bytes 5242880 | tf_op jit(solution)/shard_map/early_column_transform/pallas_call | solution.py:338
  207.0 43.5 %all-to-all-done.3 = bf16[256,32,128]{2,1,0:T(8,128)(2,1)} async-done(((bf16[256,32,128]{2,1,0:T(8,128)(2,1)}), bf16[256,32,128]{2,1,0:T(8,128)(2,1)}, u32[]{:S(2)}, u32[]{:S(2)}) %all-to-all-start.3) | async-done | bytes 2097184 | tf_op jit(solution)/shard_map/all_to_all | solution.py:503
  250.5 7.5 %late_column_transform.1 = (f32[16,32,128]{2,1,0:T(8,128)}, bf16[16,32,128]{2,1,0:T(8,128)(2,1)}, bf16[16,32,128]{2,1,0:T(8,128)(2,1)}, bf16[16,32,128]{2,1,0:T(8,128)(2,1)}) custom-call(s32[1]{0:T(128)} %bitcast.turn_ref, f32[4]{0:T(128)} %get-tuple-element.21.w_ref, f32[16,128,128]{2,1,0:T(8,128)} %early_column_transform.1.early_hbm, ...), custom_call_target="tpu_custom_call" | custom-call | flops 2200000000 | bytes 5242880 | tf_op jit(solution)/shard_map/late_column_transform/pallas_call | solution.py:410
  258.0 0.4 collective-permute-start.2
  258.5 1.7 collective-permute-start.3
  260.1 0.8 collective-permute-start.4
  261.0 6.2 %collective-permute-done.2.refs_1_ = bf16[16,32,128]{2,1,0:T(8,128)(2,1)S(1)} collective-permute-done((bf16[16,32,128]{2,1,0:T(8,128)(2,1)}, bf16[16,32,128]{2,1,0:T(8,128)(2,1)S(1)}, u32[]{:S(2)}, u32[]{:S(2)}) %collective-permute-start.2) | collective-permute-done | bytes 131104 | tf_op jit(solution)/shard_map/ppermute | solution.py:460
  267.2 0.0 collective-permute-done.3.refs_2_
  267.2 1.1 collective-permute-done.4.refs_3_
  268.2 0.9 copy-done
  269.2 1.2 place_image_rows.1
  (11 shorter events, 0.1 us)
Async XLA Ops:
  5.0 64.8 %all-to-all-start = ((bf16[64,136,128]{2,1,0:T(8,128)(2,1)}), bf16[64,136,128]{2,1,0:T(8,128)(2,1)}, u32[]{:S(2)}, u32[]{:S(2)}) async-start(bf16[64,136,128]{2,1,0:T(8,128)(2,1)} %pack_rows.2), calls=%async_computation | async-start | bytes 4456448 | tf_op jit(solution)/shard_map/all_to_all | solution.py:487
  17.1 63.0 %collective-permute-start = (f32[1]{0:T(128)}, f32[1]{0:T(128)}, u32[]{:S(2)}, u32[]{:S(2)}) collective-permute-start(f32[1]{0:T(128)} %param.16), channel_id=1, source_target_pairs={{0,1},{1,2},{2,3},{3,0},{4,5},{5,6},{6,7},{7,4},{8,9},{9,10},{10,1... | collective-permute-start | bytes 20 | tf_op jit(solution)/shard_map/ppermute | solution.py:460
  69.7 57.2 %all-to-all-start.2 = ((bf16[64,128,128]{2,1,0:T(8,128)(2,1)}), bf16[64,128,128]{2,1,0:T(8,128)(2,1)}, u32[]{:S(2)}, u32[]{:S(2)}) async-start(bf16[64,128,128]{2,1,0:T(8,128)(2,1)} %pack_rows.3), calls=%async_computation.2 | async-start | bytes 4194304 | tf_op jit(solution)/shard_map/all_to_all | solution.py:487
  80.9 4.3 %collective-permute-start.1 = (f32[2]{0:T(128)S(1)}, f32[2]{0:T(128)S(1)}, u32[]{:S(2)}, u32[]{:S(2)}) collective-permute-start(f32[2]{0:T(128)S(1)} %pad_maximum_fusion.7), channel_id=1, source_target_pairs={{0,2},{1,3},{2,0},{3,1},{4,6},{5,7},{6,4},{7,5},{8,10},{9,11},{10,... | collective-permute-start | bytes 32 | tf_op jit(solution)/shard_map/ppermute | solution.py:460
  126.9 64.1 %all-to-all-start.1 = ((bf16[256,32,128]{2,1,0:T(8,128)(2,1)}), bf16[256,32,128]{2,1,0:T(8,128)(2,1)}, u32[]{:S(2)}, u32[]{:S(2)}) async-start(bf16[256,32,128]{2,1,0:T(8,128)(2,1)} %bitcast.30), calls=%async_computation.1 | async-start | bytes 4194304 | tf_op jit(solution)/shard_map/all_to_all | solution.py:503
  191.0 7.2 %copy-start.2 = (bf16[2,256,256]{2,1,0:T(8,128)(2,1)S(1)}, bf16[2,256,256]{2,1,0:T(8,128)(2,1)}, u32[]{:S(2)}) copy-start(bf16[2,256,256]{2,1,0:T(8,128)(2,1)} %constant.115) | copy-start | bytes 786436
  191.0 7.9 %copy-start.1 = (bf16[2,256,256]{2,1,0:T(8,128)(2,1)S(1)}, bf16[2,256,256]{2,1,0:T(8,128)(2,1)}, u32[]{:S(2)}) copy-start(bf16[2,256,256]{2,1,0:T(8,128)(2,1)} %constant.116) | copy-start | bytes 786436
  191.0 59.5 %all-to-all-start.3 = ((bf16[256,32,128]{2,1,0:T(8,128)(2,1)}), bf16[256,32,128]{2,1,0:T(8,128)(2,1)}, u32[]{:S(2)}, u32[]{:S(2)}) async-start(bf16[256,32,128]{2,1,0:T(8,128)(2,1)} %bitcast.29), calls=%async_computation.3 | async-start | bytes 4194304 | tf_op jit(solution)/shard_map/all_to_all | solution.py:503
  258.0 9.1 %collective-permute-start.2 = (bf16[16,32,128]{2,1,0:T(8,128)(2,1)}, bf16[16,32,128]{2,1,0:T(8,128)(2,1)S(1)}, u32[]{:S(2)}, u32[]{:S(2)}) collective-permute-start(bf16[16,32,128]{2,1,0:T(8,128)(2,1)} %get-tuple-element.17), channel_id=1, source_target_pairs={{0,1},{1,2},{2,3},{3,0},{4,5},{5,6},{6,7},{7,4},{8,9},{9,10},{10,1... | collective-permute-start | bytes 393224 | tf_op jit(solution)/shard_map/ppermute | solution.py:460
  258.5 8.7 %collective-permute-start.3 = (bf16[16,32,128]{2,1,0:T(8,128)(2,1)}, bf16[16,32,128]{2,1,0:T(8,128)(2,1)S(1)}, u32[]{:S(2)}, u32[]{:S(2)}) collective-permute-start(bf16[16,32,128]{2,1,0:T(8,128)(2,1)} %get-tuple-element.18), channel_id=1, source_target_pairs={{0,2},{1,3},{2,0},{3,1},{4,6},{5,7},{6,4},{7,5},{8,10},{9,11},{10,... | collective-permute-start | bytes 393224 | tf_op jit(solution)/shard_map/ppermute | solution.py:460
  260.1 8.1 %collective-permute-start.4 = (bf16[16,32,128]{2,1,0:T(8,128)(2,1)}, bf16[16,32,128]{2,1,0:T(8,128)(2,1)S(1)}, u32[]{:S(2)}, u32[]{:S(2)}) collective-permute-start(bf16[16,32,128]{2,1,0:T(8,128)(2,1)} %get-tuple-element.19), channel_id=1, source_target_pairs={{0,3},{1,0},{2,1},{3,2},{4,7},{5,4},{6,5},{7,6},{8,11},{9,8},{10,9... | collective-permute-start | bytes 393224 | tf_op jit(solution)/shard_map/ppermute | solution.py:460
  268.2 1.0 copy-start

commit v8 on v5

--- a/solution.py
+++ b/solution.py
@@ -302,33 +302,15 @@
     y = (column.astype(F32) - N // 2) / N
     term = jnp.sqrt(1.0 - (x**2 + y**2)) - 1.0
     angle = (2.0 * math.pi) * w[:, None, None] * term[8]
-    return jnp.stack([jnp.cos(angle), jnp.sin(angle)]), term - term[8]
+    return jnp.stack([jnp.cos(angle), jnp.sin(angle)]), (term - term[8]).astype(BF16)
 
 
 def column_kernel(
-    turn_ref, w_ref, early_0, early_1, early_2, early_3, late_ref, table_ref, base_hbm, change_hbm,
-    own_ref, sent_1, sent_2, sent_3, early, late, rows, base_ref, change_ref, sems,
+    turn_ref, w_ref, early_0, early_1, early_2, early_3, late_ref, table_ref, base_ref, change_ref,
+    own_ref, sent_1, sent_2, sent_3, rows,
 ):
-    arrivals = ([], [])
-
-    def fetch(half, source, target):
-        number = len(arrivals[0]) + len(arrivals[1])
-        copy = pltpu.make_async_copy(source, target, sems.at[number])
-        copy.start()
-        arrivals[half].append(copy)
-
-    for half in range(2):
-        k = pl.ds(8 * half, 8)
-        pairs = pl.ds(16 * half, 16)
-        fetch(half, late_ref.at[:, :, pairs], late.at[:, :, pairs])
-        for step, source in enumerate((early_0, early_1, early_2, early_3)):
-            fetch(half, source.at[k], early.at[step, k])
-        fetch(half, change_hbm.at[k], change_ref.at[k])
-        if half == 0:
-            fetch(half, base_hbm, base_ref)
-
     turn = turn_ref[0]
-    table = table_ref[...]
+    early = (early_0, early_1, early_2, early_3)
     targets = (own_ref, sent_1, sent_2, sent_3)
 
     def one(k, carry):
@@ -336,17 +318,21 @@
         for pair in (0, 2):
             cells = jnp.concatenate(
                 [
-                    jnp.concatenate([early[step, k], rows[step, k]], axis=0)
+                    jnp.concatenate([early[step][k], rows[step, k]], axis=0)
                     for step in (pair, pair + 1)
                 ],
                 axis=1,
             )
             sky.append(
-                jnp.dot(table, jnp.concatenate([cells, cells], axis=0), preferred_element_type=F32)
+                jnp.dot(
+                    table_ref[...],
+                    jnp.concatenate([cells, cells], axis=0),
+                    preferred_element_type=F32,
+                )
             )
         for block, target in enumerate(targets):
             where = slice(32 * block, 32 * block + 32)
-            change = change_ref[k, where]
+            change = change_ref[k, where].astype(F32)
             image = jnp.zeros((32, 128), F32)
             for step in range(4):
                 part = sky[step // 2][:, 128 * (step % 2) : 128 * (step % 2) + 128]
@@ -362,10 +348,8 @@
         return carry
 
     for half in range(2):
-        for copy in arrivals[half]:
-            copy.wait()
         for step in range(4):
-            block = late[(turn - step) & 3, :, 16 * half : 16 * half + 16]
+            block = late_ref[(turn - step) & 3, :, 16 * half : 16 * half + 16]
             rows[step, 8 * half : 8 * half + 8] = jnp.swapaxes(block, 0, 1).reshape(8, 128, 128)
         lax.fori_loop(8 * half, 8 * half + 8, one, 0, unroll=4)
 
@@ -373,22 +357,14 @@
 def column_transform(turn, w, early, late, table, base, change):
     smem = pl.BlockSpec(memory_space=pltpu.SMEM)
     vmem = pl.BlockSpec(memory_space=pltpu.VMEM)
-    anywhere = pl.BlockSpec(memory_space=pl.ANY)
     return pl.pallas_call(
         column_kernel,
-        in_specs=[smem] * 2 + [anywhere] * 5 + [vmem] + [anywhere] * 2,
+        in_specs=[smem] * 2 + [vmem] * 8,
         out_specs=[vmem] * 4,
         out_shape=[jax.ShapeDtypeStruct((16, 32, 128), F32)]
         + [jax.ShapeDtypeStruct((16, 32, 128), BF16)] * 3,
-        scratch_shapes=[
-            pltpu.VMEM((4, 16, 128, 128), BF16),
-            pltpu.VMEM((4, 64, 32, 128), BF16),
-            pltpu.VMEM((4, 16, 128, 128), BF16),
-            pltpu.VMEM((2, 4, 128, 128), F32),
-            pltpu.VMEM((16, 128, 128), F32),
-            pltpu.SemaphoreType.DMA((13,)),
-        ],
-        compiler_params=pltpu.CompilerParams(vmem_limit_bytes=62 * MIB),
+        scratch_shapes=[pltpu.VMEM((4, 16, 128, 128), BF16)],
+        compiler_params=pltpu.CompilerParams(vmem_limit_bytes=16 * MIB),
         cost_estimate=pl.CostEstimate(
             flops=4_300_000_000, bytes_accessed=5 << 20, transcendentals=0
         ),

time: 271 us -> 267 us (0.985)
  transfers between devices with their start and end apart: 12 -> 12, of which waited for: 7 -> 7; matrix products, arithmetic and copies ran while one was open for 4% -> 3% of each run, Pallas kernels for 27% -> 27%
where the time goes in v8:
time: 267 us; the launch traced here: 266 us
  waiting for transfers between devices  122 us (46%)
  Pallas kernels  84.7 us (32%)
  starting transfers between devices  48.8 us (18%)
  other arithmetic  5.84 us (2%)
  local copies, waits for them, and re-layouts  3.79 us (1%)
    pallas_call x2, Pallas kernels, grid_and_rows(): pl.pallas_call(grid_kernel, in_specs=[pl.BlockSpec(memory_space=pltpu.SME...  65.7 us
    all_to_all x2, waiting for transfers between devices, local(): lax.all_to_all(packed, 'band', split_axis=0, concat_axis=0, tiled=True)  53 us
    all_to_all x1, waiting for transfers between devices, local(): lax.all_to_all(spectrum.reshape(256, 32, 128), ('wp', 'band'), split_axis...  44.4 us
    all_to_all x2, starting transfers between devices, local(): lax.all_to_all(packed, 'band', split_axis=0, concat_axis=0, tiled=True)  19.4 us
    all_to_all x1, waiting for transfers between devices, local(): lax.all_to_all(spectrum.reshape(64, 128, 128), 'band', split_axis=0, conc...  16 us
    ppermute x8, starting transfers between devices, along_wp(): return lax.ppermute(block, 'wp', pairs)  12.1 us
    all_to_all x1, starting transfers between devices, local(): lax.all_to_all(spectrum.reshape(256, 32, 128), ('wp', 'band'), split_axis...  9.93 us
    pallas_call x2, Pallas kernels, pack(): pl.pallas_call(functools.partial(pack_kernel, half=half), in_specs=[smem,...  8.69 us
  transfers between devices with their start and end apart: 12, of which 7 were waited for; matrix products, arithmetic and copies ran while one was open for 3% of the time, Pallas kernels for 27%

profile of v8, /device:TPU:33, one launch (start us, length us, event | category | flops | bytes accessed | tf_op | source)
XLA Modules:
  0.0 266.4 jit_solution(7557371906378817043)
XLA Ops:
  0.7 4.4 %pack_rows.2 = bf16[64,136,128]{2,1,0:T(8,128)(2,1)} custom-call(s32[1,1]{1,0:T(1,128)S(6)} %copy.19.count_ref, s32[1,64]{1,0:T(1,128)} %bitcast.37, s32[2,64]{1,0:T(2,128)} %bitcast.35, bf16[64,2,128,128]{3,2,1,0:T(8,128)(2,1)} %bitcast.27), custom_call_target="tpu_custom_call" | custom-call | flops 8388608 | bytes 4194304 | tf_op jit(solution)/shard_map/pack_rows/pallas_call | solution.py:135
  5.0 12.1 %all-to-all-start = ((bf16[64,136,128]{2,1,0:T(8,128)(2,1)}), bf16[64,136,128]{2,1,0:T(8,128)(2,1)}, u32[]{:S(2)}, u32[]{:S(2)}) async-start(bf16[64,136,128]{2,1,0:T(8,128)(2,1)} %pack_rows.2), calls=%async_computation | async-start | bytes 4456448 | tf_op jit(solution)/shard_map/all_to_all | solution.py:426
  17.1 1.4 collective-permute-start
  18.5 0.2 fusion.22
  18.7 0.1 maximum_bitcast_fusion
  18.8 0.1 copy.15
  18.8 4.3 %pack_rows.3 = bf16[64,128,128]{2,1,0:T(8,128)(2,1)} custom-call(s32[1,1]{1,0:T(1,128)S(6)} %copy.19.count_ref, s32[1,64]{1,0:T(1,128)} %bitcast.38, s32[2,64]{1,0:T(2,128)} %bitcast.36, bf16[64,2,128,128]{3,2,1,0:T(8,128)(2,1)} %bitcast.28), custom_call_target="tpu_custom_call" | custom-call | flops 8388608 | bytes 4194304 | tf_op jit(solution)/shard_map/pack_rows/pallas_call | solution.py:135
  23.2 46.6 %all-to-all-done.arrived_ref = bf16[64,136,128]{2,1,0:T(8,128)(2,1)} async-done(((bf16[64,136,128]{2,1,0:T(8,128)(2,1)}), bf16[64,136,128]{2,1,0:T(8,128)(2,1)}, u32[]{:S(2)}, u32[]{:S(2)}) %all-to-all-start) | async-done | bytes 2228256 | tf_op jit(solution)/shard_map/all_to_all | solution.py:426
  69.8 7.3 %all-to-all-start.2 = ((bf16[64,128,128]{2,1,0:T(8,128)(2,1)}), bf16[64,128,128]{2,1,0:T(8,128)(2,1)}, u32[]{:S(2)}, u32[]{:S(2)}) async-start(bf16[64,128,128]{2,1,0:T(8,128)(2,1)} %pack_rows.3), calls=%async_computation.2 | async-start | bytes 4194304 | tf_op jit(solution)/shard_map/all_to_all | solution.py:426
  77.8 0.6 pad_maximum_fusion.2.bands_ref
  78.4 0.4 sqrt_add_fusion
  78.9 0.5 subtract_convert_fusion.change_ref
  79.4 0.0 collective-permute-done
  79.4 0.7 pad_maximum_fusion.7
  80.1 2.9 %collective-permute-start.1 = (f32[2]{0:T(128)S(1)}, f32[2]{0:T(128)S(1)}, u32[]{:S(2)}, u32[]{:S(2)}) collective-permute-start(f32[2]{0:T(128)S(1)} %pad_maximum_fusion.7), channel_id=1, source_target_pairs={{0,2},{1,3},{2,0},{3,1},{4,6},{5,7},{6,4},{7,5},{8,10},{9,11},{10,... | collective-permute-start | bytes 32 | tf_op jit(solution)/shard_map/ppermute | solution.py:399
  83.0 1.4 collective-permute-done.1
  84.4 0.7 broadcast_multiply_fusion
  85.1 1.0 multiply_cosine_fusion
  86.1 0.1 pad_maximum_fusion.base_ref
  86.1 0.9 slice.21
  87.1 0.6 fusion.10.place_ref
  87.7 32.9 %place_and_transform.2 = bf16[1,64,128,128]{3,2,1,0:T(8,128)(2,1)} custom-call(s32[64,64]{1,0:T(8,128)} %fusion.10.place_ref, bf16[64,136,128]{2,1,0:T(8,128)(2,1)} %all-to-all-done.arrived_ref, bf16[128,384]{1,0:T(8,128)(2,1)} %constant.98.clone.first_ref, f32[2,128,128]{2,1,0:T(8,128)} %constant.99.clone.twiddle_ref, ...), custom_call_target="tpu_custom_call" | custom-call | flops 20000000000 | bytes 4194304 | tf_op jit(solution)/shard_map/place_and_transform/pallas_call | solution.py:255
  120.6 6.4 %all-to-all-done.2.arrived_ref = bf16[64,128,128]{2,1,0:T(8,128)(2,1)} async-done(((bf16[64,128,128]{2,1,0:T(8,128)(2,1)}), bf16[64,128,128]{2,1,0:T(8,128)(2,1)}, u32[]{:S(2)}, u32[]{:S(2)}) %all-to-all-start.2) | async-done | bytes 2097184 | tf_op jit(solution)/shard_map/all_to_all | solution.py:426
  126.9 7.3 %all-to-all-start.1 = ((bf16[64,128,128]{2,1,0:T(8,128)(2,1)}), bf16[64,128,128]{2,1,0:T(8,128)(2,1)}, u32[]{:S(2)}, u32[]{:S(2)}) async-start(bf16[64,128,128]{2,1,0:T(8,128)(2,1)} %bitcast.30), calls=%async_computation.1 | async-start | bytes 4194304 | tf_op jit(solution)/shard_map/all_to_all | solution.py:442
  134.3 0.1 fusion.23
  134.4 0.1 pad_maximum_fusion.5
  134.5 0.1 pad_maximum_fusion.3
  134.6 0.6 pad_maximum_fusion.4.bands_ref
  135.3 32.8 %place_and_transform.3 = bf16[4,64,32,128]{3,2,1,0:T(8,128)(2,1)} custom-call(s32[64,64]{1,0:T(8,128)} %fusion.10.place_ref, bf16[64,128,128]{2,1,0:T(8,128)(2,1)} %all-to-all-done.2.arrived_ref, bf16[128,384]{1,0:T(8,128)(2,1)} %constant.98.clone.first_ref, f32[2,128,128]{2,1,0:T(8,128)} %constant.99.clone.twiddle_ref, ...), custom_call_target="tpu_custom_call" | custom-call | flops 20000000000 | bytes 4194304 | tf_op jit(solution)/shard_map/place_and_transform/pallas_call | solution.py:255
  168.1 16.0 %all-to-all-done.1.columns_ref = bf16[64,128,128]{2,1,0:T(8,128)(2,1)} async-done(((bf16[64,128,128]{2,1,0:T(8,128)(2,1)}), bf16[64,128,128]{2,1,0:T(8,128)(2,1)}, u32[]{:S(2)}, u32[]{:S(2)}) %all-to-all-start.1) | async-done | bytes 2097184 | tf_op jit(solution)/shard_map/all_to_all | solution.py:442
  184.1 9.9 %all-to-all-start.3 = ((bf16[256,32,128]{2,1,0:T(8,128)(2,1)}), bf16[256,32,128]{2,1,0:T(8,128)(2,1)S(1)}, u32[]{:S(2)}, u32[]{:S(2)}) async-start(bf16[256,32,128]{2,1,0:T(8,128)(2,1)} %bitcast.29), calls=%async_computation.3 | async-start | bytes 4194304 | tf_op jit(solution)/shard_map/all_to_all | solution.py:446
  194.1 3.1 %deal_rows.1 = (bf16[16,128,128]{2,1,0:T(8,128)(2,1)S(1)}, bf16[16,128,128]{2,1,0:T(8,128)(2,1)}, bf16[16,128,128]{2,1,0:T(8,128)(2,1)}, bf16[16,128,128]{2,1,0:T(8,128)(2,1)}) custom-call(s32[1]{0:T(128)} %bitcast.turn_ref, bf16[64,128,128]{2,1,0:T(8,128)(2,1)} %all-to-all-done.1.columns_ref), custom_call_target="tpu_custom_call" | custom-call | flops 1048576 | bytes 4194304 | tf_op jit(solution)/shard_map/deal_rows/pallas_call | solution.py:286
  197.1 0.8 copy-done
  197.9 1.3 collective-permute-start.2
  199.2 2.5 collective-permute-start.3
  201.7 1.1 collective-permute-start.4
  202.8 1.0 constant_dynamic-slice_fusion
  203.8 44.4 %all-to-all-done.3 = bf16[256,32,128]{2,1,0:T(8,128)(2,1)S(1)} async-done(((bf16[256,32,128]{2,1,0:T(8,128)(2,1)}), bf16[256,32,128]{2,1,0:T(8,128)(2,1)S(1)}, u32[]{:S(2)}, u32[]{:S(2)}) %all-to-all-start.3) | async-done | bytes 2097184 | tf_op jit(solution)/shard_map/all_to_all | solution.py:446
  248.2 0.0 collective-permute-done.2.early_1
  248.2 0.0 collective-permute-done.3.early_2
  248.2 1.0 copy-done.1
  249.2 6.0 %column_transform.1 = (f32[16,32,128]{2,1,0:T(8,128)S(1)}, bf16[16,32,128]{2,1,0:T(8,128)(2,1)S(1)}, bf16[16,32,128]{2,1,0:T(8,128)(2,1)S(1)}, bf16[16,32,128]{2,1,0:T(8,128)(2,1)S(1)}) custom-call(s32[1]{0:T(128)} %bitcast.turn_ref, f32[4]{0:T(128)S(1)} %get-tuple-element.28.w_ref, bf16[16,128,128]{2,1,0:T(8,128)(2,1)S(1)} %copy-done.1, ...), custom_call_target="tpu_custom_call" | custom-call | flops 4300000256 | bytes 5242880 | tf_op jit(solution)/shard_map/column_transform/pallas_call | solution.py:360
  255.2 0.4 collective-permute-start.5
  255.7 1.7 collective-permute-start.6
  257.3 0.8 collective-permute-start.7
  258.2 6.0 %collective-permute-done.5.refs_1_ = bf16[16,32,128]{2,1,0:T(8,128)(2,1)S(1)} collective-permute-done((bf16[16,32,128]{2,1,0:T(8,128)(2,1)S(1)}, bf16[16,32,128]{2,1,0:T(8,128)(2,1)S(1)}, u32[]{:S(2)}, u32[]{:S(2)}) %collective-permute-start.5) | collective-permute-done | bytes 131104 | tf_op jit(solution)/shard_map/ppermute | solution.py:399
  264.2 1.1 collective-permute-done.7.refs_3_
  265.2 1.2 place_image_rows.1
  (14 shorter events, 0.1 us)
Async XLA Ops:
  5.0 64.8 %all-to-all-start = ((bf16[64,136,128]{2,1,0:T(8,128)(2,1)}), bf16[64,136,128]{2,1,0:T(8,128)(2,1)}, u32[]{:S(2)}, u32[]{:S(2)}) async-start(bf16[64,136,128]{2,1,0:T(8,128)(2,1)} %pack_rows.2), calls=%async_computation | async-start | bytes 4456448 | tf_op jit(solution)/shard_map/all_to_all | solution.py:426
  17.1 62.2 %collective-permute-start = (f32[1]{0:T(128)}, f32[1]{0:T(128)}, u32[]{:S(2)}, u32[]{:S(2)}) collective-permute-start(f32[1]{0:T(128)} %param.13), channel_id=1, source_target_pairs={{0,1},{1,2},{2,3},{3,0},{4,5},{5,6},{6,7},{7,4},{8,9},{9,10},{10,1... | collective-permute-start | bytes 20 | tf_op jit(solution)/shard_map/ppermute | solution.py:399
  69.8 57.2 %all-to-all-start.2 = ((bf16[64,128,128]{2,1,0:T(8,128)(2,1)}), bf16[64,128,128]{2,1,0:T(8,128)(2,1)}, u32[]{:S(2)}, u32[]{:S(2)}) async-start(bf16[64,128,128]{2,1,0:T(8,128)(2,1)} %pack_rows.3), calls=%async_computation.2 | async-start | bytes 4194304 | tf_op jit(solution)/shard_map/all_to_all | solution.py:426
  80.1 4.3 %collective-permute-start.1 = (f32[2]{0:T(128)S(1)}, f32[2]{0:T(128)S(1)}, u32[]{:S(2)}, u32[]{:S(2)}) collective-permute-start(f32[2]{0:T(128)S(1)} %pad_maximum_fusion.7), channel_id=1, source_target_pairs={{0,2},{1,3},{2,0},{3,1},{4,6},{5,7},{6,4},{7,5},{8,10},{9,11},{10,... | collective-permute-start | bytes 32 | tf_op jit(solution)/shard_map/ppermute | solution.py:399
  126.9 57.2 %all-to-all-start.1 = ((bf16[64,128,128]{2,1,0:T(8,128)(2,1)}), bf16[64,128,128]{2,1,0:T(8,128)(2,1)}, u32[]{:S(2)}, u32[]{:S(2)}) async-start(bf16[64,128,128]{2,1,0:T(8,128)(2,1)} %bitcast.30), calls=%async_computation.1 | async-start | bytes 4194304 | tf_op jit(solution)/shard_map/all_to_all | solution.py:442
  184.1 64.0 %all-to-all-start.3 = ((bf16[256,32,128]{2,1,0:T(8,128)(2,1)}), bf16[256,32,128]{2,1,0:T(8,128)(2,1)S(1)}, u32[]{:S(2)}, u32[]{:S(2)}) async-start(bf16[256,32,128]{2,1,0:T(8,128)(2,1)} %bitcast.29), calls=%async_computation.3 | async-start | bytes 4194304 | tf_op jit(solution)/shard_map/all_to_all | solution.py:446
  197.1 0.8 copy-start
  197.9 50.2 %collective-permute-start.2 = (bf16[16,128,128]{2,1,0:T(8,128)(2,1)}, bf16[16,128,128]{2,1,0:T(8,128)(2,1)}, u32[]{:S(2)}, u32[]{:S(2)}) collective-permute-start(bf16[16,128,128]{2,1,0:T(8,128)(2,1)} %get-tuple-element.18), channel_id=1, source_target_pairs={{0,1},{1,2},{2,3},{3,0},{4,5},{5,6},{6,7},{7,4},{8,9},{9,10},{10,1... | collective-permute-start | bytes 1572872 | tf_op jit(solution)/shard_map/ppermute | solution.py:399
  199.2 49.0 %collective-permute-start.3 = (bf16[16,128,128]{2,1,0:T(8,128)(2,1)}, bf16[16,128,128]{2,1,0:T(8,128)(2,1)}, u32[]{:S(2)}, u32[]{:S(2)}) collective-permute-start(bf16[16,128,128]{2,1,0:T(8,128)(2,1)} %get-tuple-element.19), channel_id=1, source_target_pairs={{0,2},{1,3},{2,0},{3,1},{4,6},{5,7},{6,4},{7,5},{8,10},{9,11},{10,... | collective-permute-start | bytes 1572872 | tf_op jit(solution)/shard_map/ppermute | solution.py:399
  201.7 46.5 %collective-permute-start.4 = (bf16[16,128,128]{2,1,0:T(8,128)(2,1)}, bf16[16,128,128]{2,1,0:T(8,128)(2,1)}, u32[]{:S(2)}, u32[]{:S(2)}) collective-permute-start(bf16[16,128,128]{2,1,0:T(8,128)(2,1)} %get-tuple-element.20), channel_id=1, source_target_pairs={{0,3},{1,0},{2,1},{3,2},{4,7},{5,4},{6,5},{7,6},{8,11},{9,8},{10,9... | collective-permute-start | bytes 1572872 | tf_op jit(solution)/shard_map/ppermute | solution.py:399
  248.2 1.0 copy-start.1
  255.2 8.9 %collective-permute-start.5 = (bf16[16,32,128]{2,1,0:T(8,128)(2,1)S(1)}, bf16[16,32,128]{2,1,0:T(8,128)(2,1)S(1)}, u32[]{:S(2)}, u32[]{:S(2)}) collective-permute-start(bf16[16,32,128]{2,1,0:T(8,128)(2,1)S(1)} %get-tuple-element.24), channel_id=1, source_target_pairs={{0,1},{1,2},{2,3},{3,0},{4,5},{5,6},{6,7},{7,4},{8,9},{9,10},{10,1... | collective-permute-start | bytes 393224 | tf_op jit(solution)/shard_map/ppermute | solution.py:399
  255.7 8.5 %collective-permute-start.6 = (bf16[16,32,128]{2,1,0:T(8,128)(2,1)S(1)}, bf16[16,32,128]{2,1,0:T(8,128)(2,1)S(1)}, u32[]{:S(2)}, u32[]{:S(2)}) collective-permute-start(bf16[16,32,128]{2,1,0:T(8,128)(2,1)S(1)} %get-tuple-element.25), channel_id=1, source_target_pairs={{0,2},{1,3},{2,0},{3,1},{4,6},{5,7},{6,4},{7,5},{8,10},{9,11},{10,... | collective-permute-start | bytes 393224 | tf_op jit(solution)/shard_map/ppermute | solution.py:399
  257.3 7.9 %collective-permute-start.7 = (bf16[16,32,128]{2,1,0:T(8,128)(2,1)S(1)}, bf16[16,32,128]{2,1,0:T(8,128)(2,1)S(1)}, u32[]{:S(2)}, u32[]{:S(2)}) collective-permute-start(bf16[16,32,128]{2,1,0:T(8,128)(2,1)S(1)} %get-tuple-element.26), channel_id=1, source_target_pairs={{0,3},{1,0},{2,1},{3,2},{4,7},{5,4},{6,5},{7,6},{8,11},{9,8},{10,9... | collective-permute-start | bytes 393224 | tf_op jit(solution)/shard_map/ppermute | solution.py:399

commit v9 on v8

--- a/solution.py
+++ b/solution.py
@@ -139,7 +139,7 @@
         out_shape=jax.ShapeDtypeStruct((64, length, 128), BF16),
         scratch_shapes=[
             pltpu.VMEM((SLOTS, 2, 64, 128), BF16),
-            pltpu.VMEM((64 * STRIDE, 128), F32),
+            pltpu.VMEM((65 * STRIDE + 7, 128), F32),
             pltpu.VMEM((64, length, 128), BF16),
             pltpu.SemaphoreType.DMA((8,)),
             pltpu.SemaphoreType.DMA((4,)),
@@ -260,7 +260,7 @@
         scratch_shapes=[
             pltpu.VMEM((ROWS + 8, 128), F32),
             pltpu.VMEM((ROWS + 8, 128), F32),
-            pltpu.VMEM((64 * STRIDE, 128), F32),
+            pltpu.VMEM((65 * STRIDE + 7, 128), F32),
             pltpu.VMEM((64, 128, 128), BF16),
             pltpu.VMEM(shape, BF16),
             pltpu.SemaphoreType.DMA,
@@ -272,23 +272,31 @@
     )(places, arrived, first, twiddle, second, bands)
 
 
-def deal_kernel(turn_ref, columns_ref, *out_refs):
+def deal_kernel(turn_ref, columns_ref, *refs):
+    out_refs = refs[:4]
+    rows_ref, sems = refs[4:]
+    copies = []
     for step, out_ref in enumerate(out_refs):
         begin = ((turn_ref[0] + step) & 3) * 32
         for group in range(2):
             where = pl.ds(pl.multiple_of(begin + 16 * group, 16), 16)
             rows = jnp.swapaxes(columns_ref[:, where, :], 0, 1).reshape(8, 128, 128)
-            out_ref[8 * group : 8 * group + 8] = rows
+            rows_ref[step, 8 * group : 8 * group + 8] = rows
+        copy = pltpu.make_async_copy(rows_ref.at[step], out_ref, sems.at[step])
+        copy.start()
+        copies.append(copy)
+    for copy in copies:
+        copy.wait()
 
 
 def deal_rows(turn, columns):
-    vmem = pl.BlockSpec(memory_space=pltpu.VMEM)
     return pl.pallas_call(
         deal_kernel,
-        in_specs=[pl.BlockSpec(memory_space=pltpu.SMEM), vmem],
-        out_specs=[vmem] * 4,
+        in_specs=[pl.BlockSpec(memory_space=pltpu.SMEM), pl.BlockSpec(memory_space=pltpu.VMEM)],
+        out_specs=[pl.BlockSpec(memory_space=pl.ANY)] * 4,
         out_shape=[jax.ShapeDtypeStruct((16, 128, 128), BF16)] * 4,
-        compiler_params=pltpu.CompilerParams(vmem_limit_bytes=16 * MIB),
+        scratch_shapes=[pltpu.VMEM((4, 16, 128, 128), BF16), pltpu.SemaphoreType.DMA((4,))],
+        compiler_params=pltpu.CompilerParams(vmem_limit_bytes=62 * MIB),
         cost_estimate=pl.CostEstimate(flops=1 << 20, bytes_accessed=4 << 20, transcendentals=0),
         name="deal_rows",
     )(turn, columns)
@@ -307,10 +315,19 @@
 
 def column_kernel(
     turn_ref, w_ref, early_0, early_1, early_2, early_3, late_ref, table_ref, base_ref, change_ref,
-    own_ref, sent_1, sent_2, sent_3, rows,
+    own_ref, sent_1, sent_2, sent_3, rows, early, sems,
 ):
+    incoming = []
+    for half in range(2):
+        where = pl.ds(8 * half, 8)
+        for step, source in enumerate((early_0, early_1, early_2, early_3)):
+            copy = pltpu.make_async_copy(
+                source.at[where], early.at[step, where], sems.at[4 * half + step]
+            )
+            copy.start()
+            incoming.append(copy)
+
     turn = turn_ref[0]
-    early = (early_0, early_1, early_2, early_3)
     targets = (own_ref, sent_1, sent_2, sent_3)
 
     def one(k, carry):
@@ -318,7 +335,7 @@
         for pair in (0, 2):
             cells = jnp.concatenate(
                 [
-                    jnp.concatenate([early[step][k], rows[step, k]], axis=0)
+                    jnp.concatenate([early[step, k], rows[step, k]], axis=0)
                     for step in (pair, pair + 1)
                 ],
                 axis=1,
@@ -351,19 +368,26 @@
         for step in range(4):
             block = late_ref[(turn - step) & 3, :, 16 * half : 16 * half + 16]
             rows[step, 8 * half : 8 * half + 8] = jnp.swapaxes(block, 0, 1).reshape(8, 128, 128)
+        for copy in incoming[4 * half : 4 * half + 4]:
+            copy.wait()
         lax.fori_loop(8 * half, 8 * half + 8, one, 0, unroll=4)
 
 
 def column_transform(turn, w, early, late, table, base, change):
     smem = pl.BlockSpec(memory_space=pltpu.SMEM)
     vmem = pl.BlockSpec(memory_space=pltpu.VMEM)
+    anywhere = pl.BlockSpec(memory_space=pl.ANY)
     return pl.pallas_call(
         column_kernel,
-        in_specs=[smem] * 2 + [vmem] * 8,
+        in_specs=[smem] * 2 + [anywhere] * 4 + [vmem] * 4,
         out_specs=[vmem] * 4,
         out_shape=[jax.ShapeDtypeStruct((16, 32, 128), F32)]
         + [jax.ShapeDtypeStruct((16, 32, 128), BF16)] * 3,
-        scratch_shapes=[pltpu.VMEM((4, 16, 128, 128), BF16)],
+        scratch_shapes=[
+            pltpu.VMEM((4, 16, 128, 128), BF16),
+            pltpu.VMEM((4, 16, 128, 128), BF16),
+            pltpu.SemaphoreType.DMA((8,)),
+        ],
         compiler_params=pltpu.CompilerParams(vmem_limit_bytes=16 * MIB),
         cost_estimate=pl.CostEstimate(
             flops=4_300_000_000, bytes_accessed=5 << 20, transcendentals=0

time: 267 us -> 268 us (level)
  no operation moved by 1% of the time
where the time goes in v9:
time: 268 us; the launch traced here: 267 us
  waiting for transfers between devices  122 us (46%)
  Pallas kernels  85.8 us (32%)
  starting transfers between devices  49.8 us (19%)
  other arithmetic  5.69 us (2%)
  local copies, waits for them, and re-layouts  2.99 us (1%)
    pallas_call x2, Pallas kernels, grid_and_rows(): pl.pallas_call(grid_kernel, in_specs=[pl.BlockSpec(memory_space=pltpu.SME...  65.7 us
    all_to_all x2, waiting for transfers between devices, local(): lax.all_to_all(packed, 'band', split_axis=0, concat_axis=0, tiled=True)  53.2 us
    all_to_all x1, waiting for transfers between devices, local(): lax.all_to_all(spectrum.reshape(256, 32, 128), ('wp', 'band'), split_axis...  43.9 us
    all_to_all x2, starting transfers between devices, local(): lax.all_to_all(packed, 'band', split_axis=0, concat_axis=0, tiled=True)  19.4 us
    all_to_all x1, waiting for transfers between devices, local(): lax.all_to_all(spectrum.reshape(64, 128, 128), 'band', split_axis=0, conc...  16 us
    ppermute x8, starting transfers between devices, along_wp(): return lax.ppermute(block, 'wp', pairs)  12.2 us
    all_to_all x1, starting transfers between devices, local(): lax.all_to_all(spectrum.reshape(256, 32, 128), ('wp', 'band'), split_axis...  10.9 us
    pallas_call x2, Pallas kernels, pack(): pl.pallas_call(functools.partial(pack_kernel, half=half), in_specs=[smem,...  8.68 us
  transfers between devices with their start and end apart: 12, of which 7 were waited for; matrix products, arithmetic and copies ran while one was open for 3% of the time, Pallas kernels for 27%

profile of v9, /device:TPU:33, one launch (start us, length us, event | category | flops | bytes accessed | tf_op | source)
XLA Modules:
  0.0 267.4 jit_solution(15809323511871333822)
XLA Ops:
  0.7 4.4 %pack_rows.2 = bf16[64,136,128]{2,1,0:T(8,128)(2,1)} custom-call(s32[1,1]{1,0:T(1,128)S(6)} %copy.19.count_ref, s32[1,64]{1,0:T(1,128)} %bitcast.36, s32[2,64]{1,0:T(2,128)} %bitcast.34, bf16[64,2,128,128]{3,2,1,0:T(8,128)(2,1)} %bitcast.26), custom_call_target="tpu_custom_call" | custom-call | flops 8388608 | bytes 4194304 | tf_op jit(solution)/shard_map/pack_rows/pallas_call | solution.py:135
  5.0 12.1 %all-to-all-start = ((bf16[64,136,128]{2,1,0:T(8,128)(2,1)}), bf16[64,136,128]{2,1,0:T(8,128)(2,1)}, u32[]{:S(2)}, u32[]{:S(2)}) async-start(bf16[64,136,128]{2,1,0:T(8,128)(2,1)} %pack_rows.2), calls=%async_computation | async-start | bytes 4456448 | tf_op jit(solution)/shard_map/all_to_all | solution.py:450
  17.1 1.4 collective-permute-start
  18.5 0.2 fusion.22
  18.7 0.1 maximum_bitcast_fusion
  18.8 0.1 copy.15
  18.8 4.3 %pack_rows.3 = bf16[64,128,128]{2,1,0:T(8,128)(2,1)} custom-call(s32[1,1]{1,0:T(1,128)S(6)} %copy.19.count_ref, s32[1,64]{1,0:T(1,128)} %bitcast.37, s32[2,64]{1,0:T(2,128)} %bitcast.35, bf16[64,2,128,128]{3,2,1,0:T(8,128)(2,1)} %bitcast.27), custom_call_target="tpu_custom_call" | custom-call | flops 8388608 | bytes 4194304 | tf_op jit(solution)/shard_map/pack_rows/pallas_call | solution.py:135
  23.2 46.6 %all-to-all-done.arrived_ref = bf16[64,136,128]{2,1,0:T(8,128)(2,1)} async-done(((bf16[64,136,128]{2,1,0:T(8,128)(2,1)}), bf16[64,136,128]{2,1,0:T(8,128)(2,1)}, u32[]{:S(2)}, u32[]{:S(2)}) %all-to-all-start) | async-done | bytes 2228256 | tf_op jit(solution)/shard_map/all_to_all | solution.py:450
  69.8 7.3 %all-to-all-start.2 = ((bf16[64,128,128]{2,1,0:T(8,128)(2,1)}), bf16[64,128,128]{2,1,0:T(8,128)(2,1)}, u32[]{:S(2)}, u32[]{:S(2)}) async-start(bf16[64,128,128]{2,1,0:T(8,128)(2,1)} %pack_rows.3), calls=%async_computation.2 | async-start | bytes 4194304 | tf_op jit(solution)/shard_map/all_to_all | solution.py:450
  77.8 0.6 pad_maximum_fusion.2.bands_ref
  78.4 0.4 sqrt_add_fusion
  78.9 0.5 subtract_convert_fusion.change_ref
  79.4 0.0 collective-permute-done
  79.4 0.6 pad_maximum_fusion.7
  80.0 2.9 %collective-permute-start.1 = (f32[2]{0:T(128)S(1)}, f32[2]{0:T(128)S(1)}, u32[]{:S(2)}, u32[]{:S(2)}) collective-permute-start(f32[2]{0:T(128)S(1)} %pad_maximum_fusion.7), channel_id=1, source_target_pairs={{0,2},{1,3},{2,0},{3,1},{4,6},{5,7},{6,4},{7,5},{8,10},{9,11},{10,... | collective-permute-start | bytes 32 | tf_op jit(solution)/shard_map/ppermute | solution.py:423
  82.9 1.4 collective-permute-done.1
  84.3 0.6 broadcast_multiply_fusion
  85.0 1.0 multiply_cosine_fusion
  86.0 0.9 slice.21
  87.0 0.6 fusion.10.place_ref
  87.6 32.9 %place_and_transform.2 = bf16[1,64,128,128]{3,2,1,0:T(8,128)(2,1)} custom-call(s32[64,64]{1,0:T(8,128)} %fusion.10.place_ref, bf16[64,136,128]{2,1,0:T(8,128)(2,1)} %all-to-all-done.arrived_ref, bf16[128,384]{1,0:T(8,128)(2,1)} %constant.98.clone.first_ref, f32[2,128,128]{2,1,0:T(8,128)} %constant.99.clone.twiddle_ref, ...), custom_call_target="tpu_custom_call" | custom-call | flops 20000000000 | bytes 4194304 | tf_op jit(solution)/shard_map/place_and_transform/pallas_call | solution.py:255
  120.4 6.5 %all-to-all-done.2.arrived_ref = bf16[64,128,128]{2,1,0:T(8,128)(2,1)} async-done(((bf16[64,128,128]{2,1,0:T(8,128)(2,1)}), bf16[64,128,128]{2,1,0:T(8,128)(2,1)}, u32[]{:S(2)}, u32[]{:S(2)}) %all-to-all-start.2) | async-done | bytes 2097184 | tf_op jit(solution)/shard_map/all_to_all | solution.py:450
  127.0 7.3 %all-to-all-start.1 = ((bf16[64,128,128]{2,1,0:T(8,128)(2,1)}), bf16[64,128,128]{2,1,0:T(8,128)(2,1)}, u32[]{:S(2)}, u32[]{:S(2)}) async-start(bf16[64,128,128]{2,1,0:T(8,128)(2,1)} %bitcast.29), calls=%async_computation.1 | async-start | bytes 4194304 | tf_op jit(solution)/shard_map/all_to_all | solution.py:466
  134.3 0.1 fusion.23
  134.5 0.1 pad_maximum_fusion.5
  134.5 0.1 pad_maximum_fusion.3
  134.6 0.6 pad_maximum_fusion.4.bands_ref
  135.3 32.8 %place_and_transform.3 = bf16[4,64,32,128]{3,2,1,0:T(8,128)(2,1)} custom-call(s32[64,64]{1,0:T(8,128)} %fusion.10.place_ref, bf16[64,128,128]{2,1,0:T(8,128)(2,1)} %all-to-all-done.2.arrived_ref, bf16[128,384]{1,0:T(8,128)(2,1)} %constant.98.clone.first_ref, f32[2,128,128]{2,1,0:T(8,128)} %constant.99.clone.twiddle_ref, ...), custom_call_target="tpu_custom_call" | custom-call | flops 20000000000 | bytes 4194304 | tf_op jit(solution)/shard_map/place_and_transform/pallas_call | solution.py:255
  168.1 16.0 %all-to-all-done.1.columns_ref = bf16[64,128,128]{2,1,0:T(8,128)(2,1)} async-done(((bf16[64,128,128]{2,1,0:T(8,128)(2,1)}), bf16[64,128,128]{2,1,0:T(8,128)(2,1)}, u32[]{:S(2)}, u32[]{:S(2)}) %all-to-all-start.1) | async-done | bytes 2097184 | tf_op jit(solution)/shard_map/all_to_all | solution.py:466
  184.1 10.9 %all-to-all-start.3 = ((bf16[256,32,128]{2,1,0:T(8,128)(2,1)}), bf16[256,32,128]{2,1,0:T(8,128)(2,1)}, u32[]{:S(2)}, u32[]{:S(2)}) async-start(bf16[256,32,128]{2,1,0:T(8,128)(2,1)} %bitcast.28), calls=%async_computation.3 | async-start | bytes 4194304 | tf_op jit(solution)/shard_map/all_to_all | solution.py:470
  195.1 3.3 %deal_rows.1 = (bf16[16,128,128]{2,1,0:T(8,128)(2,1)}, bf16[16,128,128]{2,1,0:T(8,128)(2,1)}, bf16[16,128,128]{2,1,0:T(8,128)(2,1)}, bf16[16,128,128]{2,1,0:T(8,128)(2,1)}) custom-call(s32[1]{0:T(128)} %bitcast.turn_ref, bf16[64,128,128]{2,1,0:T(8,128)(2,1)} %all-to-all-done.1.columns_ref), custom_call_target="tpu_custom_call" | custom-call | flops 1048576 | bytes 4194304 | tf_op jit(solution)/shard_map/deal_rows/pallas_call | solution.py:293
  198.4 1.3 collective-permute-start.2
  199.7 2.5 collective-permute-start.3
  202.2 1.1 collective-permute-start.4
  203.4 1.0 constant_dynamic-slice_fusion
  204.3 43.9 %all-to-all-done.3 = bf16[256,32,128]{2,1,0:T(8,128)(2,1)} async-done(((bf16[256,32,128]{2,1,0:T(8,128)(2,1)}), bf16[256,32,128]{2,1,0:T(8,128)(2,1)}, u32[]{:S(2)}, u32[]{:S(2)}) %all-to-all-start.3) | async-done | bytes 2097184 | tf_op jit(solution)/shard_map/all_to_all | solution.py:470
  248.3 0.0 collective-permute-done.2.early_1
  248.3 0.0 collective-permute-done.3.early_2
  248.3 0.0 copy-start
  248.3 1.0 copy-done
  249.3 7.0 %column_transform.1 = (f32[16,32,128]{2,1,0:T(8,128)S(1)}, bf16[16,32,128]{2,1,0:T(8,128)(2,1)S(1)}, bf16[16,32,128]{2,1,0:T(8,128)(2,1)S(1)}, bf16[16,32,128]{2,1,0:T(8,128)(2,1)S(1)}) custom-call(s32[1]{0:T(128)} %bitcast.turn_ref, f32[4]{0:T(128)S(1)} %get-tuple-element.28.w_ref, bf16[16,128,128]{2,1,0:T(8,128)(2,1)S(1)} %copy-done, ...), custom_call_target="tpu_custom_call" | custom-call | flops 4300000256 | bytes 5242880 | tf_op jit(solution)/shard_map/column_transform/pallas_call | solution.py:380
  256.3 0.4 collective-permute-start.5
  256.7 1.7 collective-permute-start.6
  258.4 0.8 collective-permute-start.7
  259.2 6.0 %collective-permute-done.5.refs_1_ = bf16[16,32,128]{2,1,0:T(8,128)(2,1)S(1)} collective-permute-done((bf16[16,32,128]{2,1,0:T(8,128)(2,1)S(1)}, bf16[16,32,128]{2,1,0:T(8,128)(2,1)S(1)}, u32[]{:S(2)}, u32[]{:S(2)}) %collective-permute-start.5) | collective-permute-done | bytes 131104 | tf_op jit(solution)/shard_map/ppermute | solution.py:423
  265.2 0.0 collective-permute-done.6.refs_2_
  265.2 1.1 collective-permute-done.7.refs_3_
  266.3 1.2 place_image_rows.1
  (12 shorter events, 0.1 us)
Async XLA Ops:
  5.0 64.8 %all-to-all-start = ((bf16[64,136,128]{2,1,0:T(8,128)(2,1)}), bf16[64,136,128]{2,1,0:T(8,128)(2,1)}, u32[]{:S(2)}, u32[]{:S(2)}) async-start(bf16[64,136,128]{2,1,0:T(8,128)(2,1)} %pack_rows.2), calls=%async_computation | async-start | bytes 4456448 | tf_op jit(solution)/shard_map/all_to_all | solution.py:450
  17.1 62.2 %collective-permute-start = (f32[1]{0:T(128)}, f32[1]{0:T(128)}, u32[]{:S(2)}, u32[]{:S(2)}) collective-permute-start(f32[1]{0:T(128)} %param.13), channel_id=1, source_target_pairs={{0,1},{1,2},{2,3},{3,0},{4,5},{5,6},{6,7},{7,4},{8,9},{9,10},{10,1... | collective-permute-start | bytes 20 | tf_op jit(solution)/shard_map/ppermute | solution.py:423
  69.8 57.2 %all-to-all-start.2 = ((bf16[64,128,128]{2,1,0:T(8,128)(2,1)}), bf16[64,128,128]{2,1,0:T(8,128)(2,1)}, u32[]{:S(2)}, u32[]{:S(2)}) async-start(bf16[64,128,128]{2,1,0:T(8,128)(2,1)} %pack_rows.3), calls=%async_computation.2 | async-start | bytes 4194304 | tf_op jit(solution)/shard_map/all_to_all | solution.py:450
  80.0 4.3 %collective-permute-start.1 = (f32[2]{0:T(128)S(1)}, f32[2]{0:T(128)S(1)}, u32[]{:S(2)}, u32[]{:S(2)}) collective-permute-start(f32[2]{0:T(128)S(1)} %pad_maximum_fusion.7), channel_id=1, source_target_pairs={{0,2},{1,3},{2,0},{3,1},{4,6},{5,7},{6,4},{7,5},{8,10},{9,11},{10,... | collective-permute-start | bytes 32 | tf_op jit(solution)/shard_map/ppermute | solution.py:423
  127.0 57.2 %all-to-all-start.1 = ((bf16[64,128,128]{2,1,0:T(8,128)(2,1)}), bf16[64,128,128]{2,1,0:T(8,128)(2,1)}, u32[]{:S(2)}, u32[]{:S(2)}) async-start(bf16[64,128,128]{2,1,0:T(8,128)(2,1)} %bitcast.29), calls=%async_computation.1 | async-start | bytes 4194304 | tf_op jit(solution)/shard_map/all_to_all | solution.py:466
  184.1 64.1 %all-to-all-start.3 = ((bf16[256,32,128]{2,1,0:T(8,128)(2,1)}), bf16[256,32,128]{2,1,0:T(8,128)(2,1)}, u32[]{:S(2)}, u32[]{:S(2)}) async-start(bf16[256,32,128]{2,1,0:T(8,128)(2,1)} %bitcast.28), calls=%async_computation.3 | async-start | bytes 4194304 | tf_op jit(solution)/shard_map/all_to_all | solution.py:470
  198.4 49.9 %collective-permute-start.2 = (bf16[16,128,128]{2,1,0:T(8,128)(2,1)}, bf16[16,128,128]{2,1,0:T(8,128)(2,1)S(1)}, u32[]{:S(2)}, u32[]{:S(2)}) collective-permute-start(bf16[16,128,128]{2,1,0:T(8,128)(2,1)} %get-tuple-element.18), channel_id=1, source_target_pairs={{0,1},{1,2},{2,3},{3,0},{4,5},{5,6},{6,7},{7,4},{8,9},{9,10},{10,1... | collective-permute-start | bytes 1572872 | tf_op jit(solution)/shard_map/ppermute | solution.py:423
  199.7 48.6 %collective-permute-start.3 = (bf16[16,128,128]{2,1,0:T(8,128)(2,1)}, bf16[16,128,128]{2,1,0:T(8,128)(2,1)S(1)}, u32[]{:S(2)}, u32[]{:S(2)}) collective-permute-start(bf16[16,128,128]{2,1,0:T(8,128)(2,1)} %get-tuple-element.19), channel_id=1, source_target_pairs={{0,2},{1,3},{2,0},{3,1},{4,6},{5,7},{6,4},{7,5},{8,10},{9,11},{10,... | collective-permute-start | bytes 1572872 | tf_op jit(solution)/shard_map/ppermute | solution.py:423
  202.2 46.0 %collective-permute-start.4 = (bf16[16,128,128]{2,1,0:T(8,128)(2,1)}, bf16[16,128,128]{2,1,0:T(8,128)(2,1)S(1)}, u32[]{:S(2)}, u32[]{:S(2)}) collective-permute-start(bf16[16,128,128]{2,1,0:T(8,128)(2,1)} %get-tuple-element.20), channel_id=1, source_target_pairs={{0,3},{1,0},{2,1},{3,2},{4,7},{5,4},{6,5},{7,6},{8,11},{9,8},{10,9... | collective-permute-start | bytes 1572872 | tf_op jit(solution)/shard_map/ppermute | solution.py:423
  248.3 1.0 copy-start
  256.3 8.9 %collective-permute-start.5 = (bf16[16,32,128]{2,1,0:T(8,128)(2,1)S(1)}, bf16[16,32,128]{2,1,0:T(8,128)(2,1)S(1)}, u32[]{:S(2)}, u32[]{:S(2)}) collective-permute-start(bf16[16,32,128]{2,1,0:T(8,128)(2,1)S(1)} %get-tuple-element.24), channel_id=1, source_target_pairs={{0,1},{1,2},{2,3},{3,0},{4,5},{5,6},{6,7},{7,4},{8,9},{9,10},{10,1... | collective-permute-start | bytes 393224 | tf_op jit(solution)/shard_map/ppermute | solution.py:423
  256.7 8.5 %collective-permute-start.6 = (bf16[16,32,128]{2,1,0:T(8,128)(2,1)S(1)}, bf16[16,32,128]{2,1,0:T(8,128)(2,1)S(1)}, u32[]{:S(2)}, u32[]{:S(2)}) collective-permute-start(bf16[16,32,128]{2,1,0:T(8,128)(2,1)S(1)} %get-tuple-element.25), channel_id=1, source_target_pairs={{0,2},{1,3},{2,0},{3,1},{4,6},{5,7},{6,4},{7,5},{8,10},{9,11},{10,... | collective-permute-start | bytes 393224 | tf_op jit(solution)/shard_map/ppermute | solution.py:423
  258.4 7.9 %collective-permute-start.7 = (bf16[16,32,128]{2,1,0:T(8,128)(2,1)S(1)}, bf16[16,32,128]{2,1,0:T(8,128)(2,1)S(1)}, u32[]{:S(2)}, u32[]{:S(2)}) collective-permute-start(bf16[16,32,128]{2,1,0:T(8,128)(2,1)S(1)} %get-tuple-element.26), channel_id=1, source_target_pairs={{0,3},{1,0},{2,1},{3,2},{4,7},{5,4},{6,5},{7,6},{8,11},{9,8},{10,9... | collective-permute-start | bytes 393224 | tf_op jit(solution)/shard_map/ppermute | solution.py:423

commit v10 on v8

--- a/solution.py
+++ b/solution.py
@@ -139,7 +139,7 @@
         out_shape=jax.ShapeDtypeStruct((64, length, 128), BF16),
         scratch_shapes=[
             pltpu.VMEM((SLOTS, 2, 64, 128), BF16),
-            pltpu.VMEM((64 * STRIDE, 128), F32),
+            pltpu.VMEM((65 * STRIDE + 7, 128), F32),
             pltpu.VMEM((64, length, 128), BF16),
             pltpu.SemaphoreType.DMA((8,)),
             pltpu.SemaphoreType.DMA((4,)),
@@ -260,7 +260,7 @@
         scratch_shapes=[
             pltpu.VMEM((ROWS + 8, 128), F32),
             pltpu.VMEM((ROWS + 8, 128), F32),
-            pltpu.VMEM((64 * STRIDE, 128), F32),
+            pltpu.VMEM((65 * STRIDE + 7, 128), F32),
             pltpu.VMEM((64, 128, 128), BF16),
             pltpu.VMEM(shape, BF16),
             pltpu.SemaphoreType.DMA,
@@ -272,23 +272,31 @@
     )(places, arrived, first, twiddle, second, bands)
 
 
-def deal_kernel(turn_ref, columns_ref, *out_refs):
+def deal_kernel(turn_ref, columns_ref, *refs):
+    out_refs = refs[:4]
+    rows_ref, sems = refs[4:]
+    copies = []
     for step, out_ref in enumerate(out_refs):
         begin = ((turn_ref[0] + step) & 3) * 32
         for group in range(2):
             where = pl.ds(pl.multiple_of(begin + 16 * group, 16), 16)
             rows = jnp.swapaxes(columns_ref[:, where, :], 0, 1).reshape(8, 128, 128)
-            out_ref[8 * group : 8 * group + 8] = rows
+            rows_ref[step, 8 * group : 8 * group + 8] = rows
+        copy = pltpu.make_async_copy(rows_ref.at[step], out_ref, sems.at[step])
+        copy.start()
+        copies.append(copy)
+    for copy in copies:
+        copy.wait()
 
 
 def deal_rows(turn, columns):
-    vmem = pl.BlockSpec(memory_space=pltpu.VMEM)
     return pl.pallas_call(
         deal_kernel,
-        in_specs=[pl.BlockSpec(memory_space=pltpu.SMEM), vmem],
-        out_specs=[vmem] * 4,
+        in_specs=[pl.BlockSpec(memory_space=pltpu.SMEM), pl.BlockSpec(memory_space=pltpu.VMEM)],
+        out_specs=[pl.BlockSpec(memory_space=pl.ANY)] * 4,
         out_shape=[jax.ShapeDtypeStruct((16, 128, 128), BF16)] * 4,
-        compiler_params=pltpu.CompilerParams(vmem_limit_bytes=16 * MIB),
+        scratch_shapes=[pltpu.VMEM((4, 16, 128, 128), BF16), pltpu.SemaphoreType.DMA((4,))],
+        compiler_params=pltpu.CompilerParams(vmem_limit_bytes=62 * MIB),
         cost_estimate=pl.CostEstimate(flops=1 << 20, bytes_accessed=4 << 20, transcendentals=0),
         name="deal_rows",
     )(turn, columns)

time: 267 us -> 268 us (level)
  no operation moved by 1% of the time
where the time goes in v10:
time: 268 us; the launch traced here: 267 us
  waiting for transfers between devices  122 us (46%)
  Pallas kernels  85.6 us (32%)
  starting transfers between devices  49.8 us (19%)
  other arithmetic  5.69 us (2%)
  local copies, waits for them, and re-layouts  2.99 us (1%)
    pallas_call x2, Pallas kernels, grid_and_rows(): pl.pallas_call(grid_kernel, in_specs=[pl.BlockSpec(memory_space=pltpu.SME...  65.7 us
    all_to_all x2, waiting for transfers between devices, local(): lax.all_to_all(packed, 'band', split_axis=0, concat_axis=0, tiled=True)  53.2 us
    all_to_all x1, waiting for transfers between devices, local(): lax.all_to_all(spectrum.reshape(256, 32, 128), ('wp', 'band'), split_axis...  43.9 us
    all_to_all x2, starting transfers between devices, local(): lax.all_to_all(packed, 'band', split_axis=0, concat_axis=0, tiled=True)  19.4 us
    all_to_all x1, waiting for transfers between devices, local(): lax.all_to_all(spectrum.reshape(64, 128, 128), 'band', split_axis=0, conc...  16 us
    ppermute x8, starting transfers between devices, along_wp(): return lax.ppermute(block, 'wp', pairs)  12.2 us
    all_to_all x1, starting transfers between devices, local(): lax.all_to_all(spectrum.reshape(256, 32, 128), ('wp', 'band'), split_axis...  10.9 us
    pallas_call x2, Pallas kernels, pack(): pl.pallas_call(functools.partial(pack_kernel, half=half), in_specs=[smem,...  8.68 us
  transfers between devices with their start and end apart: 12, of which 7 were waited for; matrix products, arithmetic and copies ran while one was open for 3% of the time, Pallas kernels for 27%

profile of v10, /device:TPU:33, one launch (start us, length us, event | category | flops | bytes accessed | tf_op | source)
XLA Modules:
  0.0 267.2 jit_solution(551807216442335155)
XLA Ops:
  0.7 4.4 %pack_rows.2 = bf16[64,136,128]{2,1,0:T(8,128)(2,1)} custom-call(s32[1,1]{1,0:T(1,128)S(6)} %copy.19.count_ref, s32[1,64]{1,0:T(1,128)} %bitcast.36, s32[2,64]{1,0:T(2,128)} %bitcast.34, bf16[64,2,128,128]{3,2,1,0:T(8,128)(2,1)} %bitcast.26), custom_call_target="tpu_custom_call" | custom-call | flops 8388608 | bytes 4194304 | tf_op jit(solution)/shard_map/pack_rows/pallas_call | solution.py:135
  5.0 12.1 %all-to-all-start = ((bf16[64,136,128]{2,1,0:T(8,128)(2,1)}), bf16[64,136,128]{2,1,0:T(8,128)(2,1)}, u32[]{:S(2)}, u32[]{:S(2)}) async-start(bf16[64,136,128]{2,1,0:T(8,128)(2,1)} %pack_rows.2), calls=%async_computation | async-start | bytes 4456448 | tf_op jit(solution)/shard_map/all_to_all | solution.py:434
  17.1 1.4 collective-permute-start
  18.5 0.2 fusion.22
  18.7 0.1 maximum_bitcast_fusion
  18.8 0.1 copy.15
  18.8 4.3 %pack_rows.3 = bf16[64,128,128]{2,1,0:T(8,128)(2,1)} custom-call(s32[1,1]{1,0:T(1,128)S(6)} %copy.19.count_ref, s32[1,64]{1,0:T(1,128)} %bitcast.37, s32[2,64]{1,0:T(2,128)} %bitcast.35, bf16[64,2,128,128]{3,2,1,0:T(8,128)(2,1)} %bitcast.27), custom_call_target="tpu_custom_call" | custom-call | flops 8388608 | bytes 4194304 | tf_op jit(solution)/shard_map/pack_rows/pallas_call | solution.py:135
  23.2 46.6 %all-to-all-done.arrived_ref = bf16[64,136,128]{2,1,0:T(8,128)(2,1)} async-done(((bf16[64,136,128]{2,1,0:T(8,128)(2,1)}), bf16[64,136,128]{2,1,0:T(8,128)(2,1)}, u32[]{:S(2)}, u32[]{:S(2)}) %all-to-all-start) | async-done | bytes 2228256 | tf_op jit(solution)/shard_map/all_to_all | solution.py:434
  69.8 7.3 %all-to-all-start.2 = ((bf16[64,128,128]{2,1,0:T(8,128)(2,1)}), bf16[64,128,128]{2,1,0:T(8,128)(2,1)}, u32[]{:S(2)}, u32[]{:S(2)}) async-start(bf16[64,128,128]{2,1,0:T(8,128)(2,1)} %pack_rows.3), calls=%async_computation.2 | async-start | bytes 4194304 | tf_op jit(solution)/shard_map/all_to_all | solution.py:434
  77.8 0.6 pad_maximum_fusion.2.bands_ref
  78.4 0.4 sqrt_add_fusion
  78.9 0.5 subtract_convert_fusion.change_ref
  79.4 0.0 collective-permute-done
  79.4 0.6 pad_maximum_fusion.7
  80.0 2.9 %collective-permute-start.1 = (f32[2]{0:T(128)S(1)}, f32[2]{0:T(128)S(1)}, u32[]{:S(2)}, u32[]{:S(2)}) collective-permute-start(f32[2]{0:T(128)S(1)} %pad_maximum_fusion.7), channel_id=1, source_target_pairs={{0,2},{1,3},{2,0},{3,1},{4,6},{5,7},{6,4},{7,5},{8,10},{9,11},{10,... | collective-permute-start | bytes 32 | tf_op jit(solution)/shard_map/ppermute | solution.py:407
  82.9 1.4 collective-permute-done.1
  84.3 0.6 broadcast_multiply_fusion
  85.0 1.0 multiply_cosine_fusion
  86.0 0.9 slice.21
  87.0 0.6 fusion.10.place_ref
  87.6 32.9 %place_and_transform.2 = bf16[1,64,128,128]{3,2,1,0:T(8,128)(2,1)} custom-call(s32[64,64]{1,0:T(8,128)} %fusion.10.place_ref, bf16[64,136,128]{2,1,0:T(8,128)(2,1)} %all-to-all-done.arrived_ref, bf16[128,384]{1,0:T(8,128)(2,1)} %constant.98.clone.first_ref, f32[2,128,128]{2,1,0:T(8,128)} %constant.99.clone.twiddle_ref, ...), custom_call_target="tpu_custom_call" | custom-call | flops 20000000000 | bytes 4194304 | tf_op jit(solution)/shard_map/place_and_transform/pallas_call | solution.py:255
  120.4 6.5 %all-to-all-done.2.arrived_ref = bf16[64,128,128]{2,1,0:T(8,128)(2,1)} async-done(((bf16[64,128,128]{2,1,0:T(8,128)(2,1)}), bf16[64,128,128]{2,1,0:T(8,128)(2,1)}, u32[]{:S(2)}, u32[]{:S(2)}) %all-to-all-start.2) | async-done | bytes 2097184 | tf_op jit(solution)/shard_map/all_to_all | solution.py:434
  127.0 7.3 %all-to-all-start.1 = ((bf16[64,128,128]{2,1,0:T(8,128)(2,1)}), bf16[64,128,128]{2,1,0:T(8,128)(2,1)}, u32[]{:S(2)}, u32[]{:S(2)}) async-start(bf16[64,128,128]{2,1,0:T(8,128)(2,1)} %bitcast.29), calls=%async_computation.1 | async-start | bytes 4194304 | tf_op jit(solution)/shard_map/all_to_all | solution.py:450
  134.3 0.1 fusion.23
  134.5 0.1 pad_maximum_fusion.5
  134.5 0.1 pad_maximum_fusion.3
  134.6 0.6 pad_maximum_fusion.4.bands_ref
  135.3 32.8 %place_and_transform.3 = bf16[4,64,32,128]{3,2,1,0:T(8,128)(2,1)} custom-call(s32[64,64]{1,0:T(8,128)} %fusion.10.place_ref, bf16[64,128,128]{2,1,0:T(8,128)(2,1)} %all-to-all-done.2.arrived_ref, bf16[128,384]{1,0:T(8,128)(2,1)} %constant.98.clone.first_ref, f32[2,128,128]{2,1,0:T(8,128)} %constant.99.clone.twiddle_ref, ...), custom_call_target="tpu_custom_call" | custom-call | flops 20000000000 | bytes 4194304 | tf_op jit(solution)/shard_map/place_and_transform/pallas_call | solution.py:255
  168.1 16.0 %all-to-all-done.1.columns_ref = bf16[64,128,128]{2,1,0:T(8,128)(2,1)} async-done(((bf16[64,128,128]{2,1,0:T(8,128)(2,1)}), bf16[64,128,128]{2,1,0:T(8,128)(2,1)}, u32[]{:S(2)}, u32[]{:S(2)}) %all-to-all-start.1) | async-done | bytes 2097184 | tf_op jit(solution)/shard_map/all_to_all | solution.py:450
  184.1 10.9 %all-to-all-start.3 = ((bf16[256,32,128]{2,1,0:T(8,128)(2,1)}), bf16[256,32,128]{2,1,0:T(8,128)(2,1)}, u32[]{:S(2)}, u32[]{:S(2)}) async-start(bf16[256,32,128]{2,1,0:T(8,128)(2,1)} %bitcast.28), calls=%async_computation.3 | async-start | bytes 4194304 | tf_op jit(solution)/shard_map/all_to_all | solution.py:454
  195.1 3.3 %deal_rows.1 = (bf16[16,128,128]{2,1,0:T(8,128)(2,1)}, bf16[16,128,128]{2,1,0:T(8,128)(2,1)}, bf16[16,128,128]{2,1,0:T(8,128)(2,1)}, bf16[16,128,128]{2,1,0:T(8,128)(2,1)}) custom-call(s32[1]{0:T(128)} %bitcast.turn_ref, bf16[64,128,128]{2,1,0:T(8,128)(2,1)} %all-to-all-done.1.columns_ref), custom_call_target="tpu_custom_call" | custom-call | flops 1048576 | bytes 4194304 | tf_op jit(solution)/shard_map/deal_rows/pallas_call | solution.py:293
  198.4 1.3 collective-permute-start.2
  199.7 2.5 collective-permute-start.3
  202.2 1.1 collective-permute-start.4
  203.4 1.0 constant_dynamic-slice_fusion
  204.3 43.9 %all-to-all-done.3 = bf16[256,32,128]{2,1,0:T(8,128)(2,1)} async-done(((bf16[256,32,128]{2,1,0:T(8,128)(2,1)}), bf16[256,32,128]{2,1,0:T(8,128)(2,1)}, u32[]{:S(2)}, u32[]{:S(2)}) %all-to-all-start.3) | async-done | bytes 2097184 | tf_op jit(solution)/shard_map/all_to_all | solution.py:454
  248.3 0.0 collective-permute-done.2.early_1
  248.3 0.0 collective-permute-done.3.early_2
  248.3 0.0 collective-permute-done.4.early_3
  248.3 0.0 copy-start
  248.3 1.0 copy-done
  249.3 6.7 %column_transform.1 = (f32[16,32,128]{2,1,0:T(8,128)S(1)}, bf16[16,32,128]{2,1,0:T(8,128)(2,1)S(1)}, bf16[16,32,128]{2,1,0:T(8,128)(2,1)S(1)}, bf16[16,32,128]{2,1,0:T(8,128)(2,1)S(1)}) custom-call(s32[1]{0:T(128)} %bitcast.turn_ref, f32[4]{0:T(128)S(1)} %get-tuple-element.28.w_ref, bf16[16,128,128]{2,1,0:T(8,128)(2,1)S(1)} %copy-done, ...), custom_call_target="tpu_custom_call" | custom-call | flops 4300000256 | bytes 5242880 | tf_op jit(solution)/shard_map/column_transform/pallas_call | solution.py:368
  256.1 0.4 collective-permute-start.5
  256.5 1.7 collective-permute-start.6
  258.1 0.8 collective-permute-start.7
  259.0 6.0 %collective-permute-done.5.refs_1_ = bf16[16,32,128]{2,1,0:T(8,128)(2,1)S(1)} collective-permute-done((bf16[16,32,128]{2,1,0:T(8,128)(2,1)S(1)}, bf16[16,32,128]{2,1,0:T(8,128)(2,1)S(1)}, u32[]{:S(2)}, u32[]{:S(2)}) %collective-permute-start.5) | collective-permute-done | bytes 131104 | tf_op jit(solution)/shard_map/ppermute | solution.py:407
  265.0 1.1 collective-permute-done.7.refs_3_
  266.1 1.2 place_image_rows.1
  (12 shorter events, 0.1 us)
Async XLA Ops:
  5.0 64.8 %all-to-all-start = ((bf16[64,136,128]{2,1,0:T(8,128)(2,1)}), bf16[64,136,128]{2,1,0:T(8,128)(2,1)}, u32[]{:S(2)}, u32[]{:S(2)}) async-start(bf16[64,136,128]{2,1,0:T(8,128)(2,1)} %pack_rows.2), calls=%async_computation | async-start | bytes 4456448 | tf_op jit(solution)/shard_map/all_to_all | solution.py:434
  17.1 62.2 %collective-permute-start = (f32[1]{0:T(128)}, f32[1]{0:T(128)}, u32[]{:S(2)}, u32[]{:S(2)}) collective-permute-start(f32[1]{0:T(128)} %param.13), channel_id=1, source_target_pairs={{0,1},{1,2},{2,3},{3,0},{4,5},{5,6},{6,7},{7,4},{8,9},{9,10},{10,1... | collective-permute-start | bytes 20 | tf_op jit(solution)/shard_map/ppermute | solution.py:407
  69.8 57.2 %all-to-all-start.2 = ((bf16[64,128,128]{2,1,0:T(8,128)(2,1)}), bf16[64,128,128]{2,1,0:T(8,128)(2,1)}, u32[]{:S(2)}, u32[]{:S(2)}) async-start(bf16[64,128,128]{2,1,0:T(8,128)(2,1)} %pack_rows.3), calls=%async_computation.2 | async-start | bytes 4194304 | tf_op jit(solution)/shard_map/all_to_all | solution.py:434
  80.0 4.3 %collective-permute-start.1 = (f32[2]{0:T(128)S(1)}, f32[2]{0:T(128)S(1)}, u32[]{:S(2)}, u32[]{:S(2)}) collective-permute-start(f32[2]{0:T(128)S(1)} %pad_maximum_fusion.7), channel_id=1, source_target_pairs={{0,2},{1,3},{2,0},{3,1},{4,6},{5,7},{6,4},{7,5},{8,10},{9,11},{10,... | collective-permute-start | bytes 32 | tf_op jit(solution)/shard_map/ppermute | solution.py:407
  127.0 57.2 %all-to-all-start.1 = ((bf16[64,128,128]{2,1,0:T(8,128)(2,1)}), bf16[64,128,128]{2,1,0:T(8,128)(2,1)}, u32[]{:S(2)}, u32[]{:S(2)}) async-start(bf16[64,128,128]{2,1,0:T(8,128)(2,1)} %bitcast.29), calls=%async_computation.1 | async-start | bytes 4194304 | tf_op jit(solution)/shard_map/all_to_all | solution.py:450
  184.1 64.1 %all-to-all-start.3 = ((bf16[256,32,128]{2,1,0:T(8,128)(2,1)}), bf16[256,32,128]{2,1,0:T(8,128)(2,1)}, u32[]{:S(2)}, u32[]{:S(2)}) async-start(bf16[256,32,128]{2,1,0:T(8,128)(2,1)} %bitcast.28), calls=%async_computation.3 | async-start | bytes 4194304 | tf_op jit(solution)/shard_map/all_to_all | solution.py:454
  198.4 49.9 %collective-permute-start.2 = (bf16[16,128,128]{2,1,0:T(8,128)(2,1)}, bf16[16,128,128]{2,1,0:T(8,128)(2,1)S(1)}, u32[]{:S(2)}, u32[]{:S(2)}) collective-permute-start(bf16[16,128,128]{2,1,0:T(8,128)(2,1)} %get-tuple-element.18), channel_id=1, source_target_pairs={{0,1},{1,2},{2,3},{3,0},{4,5},{5,6},{6,7},{7,4},{8,9},{9,10},{10,1... | collective-permute-start | bytes 1572872 | tf_op jit(solution)/shard_map/ppermute | solution.py:407
  199.7 48.6 %collective-permute-start.3 = (bf16[16,128,128]{2,1,0:T(8,128)(2,1)}, bf16[16,128,128]{2,1,0:T(8,128)(2,1)S(1)}, u32[]{:S(2)}, u32[]{:S(2)}) collective-permute-start(bf16[16,128,128]{2,1,0:T(8,128)(2,1)} %get-tuple-element.19), channel_id=1, source_target_pairs={{0,2},{1,3},{2,0},{3,1},{4,6},{5,7},{6,4},{7,5},{8,10},{9,11},{10,... | collective-permute-start | bytes 1572872 | tf_op jit(solution)/shard_map/ppermute | solution.py:407
  202.2 46.0 %collective-permute-start.4 = (bf16[16,128,128]{2,1,0:T(8,128)(2,1)}, bf16[16,128,128]{2,1,0:T(8,128)(2,1)S(1)}, u32[]{:S(2)}, u32[]{:S(2)}) collective-permute-start(bf16[16,128,128]{2,1,0:T(8,128)(2,1)} %get-tuple-element.20), channel_id=1, source_target_pairs={{0,3},{1,0},{2,1},{3,2},{4,7},{5,4},{6,5},{7,6},{8,11},{9,8},{10,9... | collective-permute-start | bytes 1572872 | tf_op jit(solution)/shard_map/ppermute | solution.py:407
  248.3 1.0 copy-start
  256.1 8.9 %collective-permute-start.5 = (bf16[16,32,128]{2,1,0:T(8,128)(2,1)S(1)}, bf16[16,32,128]{2,1,0:T(8,128)(2,1)S(1)}, u32[]{:S(2)}, u32[]{:S(2)}) collective-permute-start(bf16[16,32,128]{2,1,0:T(8,128)(2,1)S(1)} %get-tuple-element.24), channel_id=1, source_target_pairs={{0,1},{1,2},{2,3},{3,0},{4,5},{5,6},{6,7},{7,4},{8,9},{9,10},{10,1... | collective-permute-start | bytes 393224 | tf_op jit(solution)/shard_map/ppermute | solution.py:407
  256.5 8.5 %collective-permute-start.6 = (bf16[16,32,128]{2,1,0:T(8,128)(2,1)S(1)}, bf16[16,32,128]{2,1,0:T(8,128)(2,1)S(1)}, u32[]{:S(2)}, u32[]{:S(2)}) collective-permute-start(bf16[16,32,128]{2,1,0:T(8,128)(2,1)S(1)} %get-tuple-element.25), channel_id=1, source_target_pairs={{0,2},{1,3},{2,0},{3,1},{4,6},{5,7},{6,4},{7,5},{8,10},{9,11},{10,... | collective-permute-start | bytes 393224 | tf_op jit(solution)/shard_map/ppermute | solution.py:407
  258.1 7.9 %collective-permute-start.7 = (bf16[16,32,128]{2,1,0:T(8,128)(2,1)S(1)}, bf16[16,32,128]{2,1,0:T(8,128)(2,1)S(1)}, u32[]{:S(2)}, u32[]{:S(2)}) collective-permute-start(bf16[16,32,128]{2,1,0:T(8,128)(2,1)S(1)} %get-tuple-element.26), channel_id=1, source_target_pairs={{0,3},{1,0},{2,1},{3,2},{4,7},{5,4},{6,5},{7,6},{8,11},{9,8},{10,9... | collective-permute-start | bytes 393224 | tf_op jit(solution)/shard_map/ppermute | solution.py:407

commit v11 on v10

--- a/solution.py
+++ b/solution.py
@@ -315,11 +315,12 @@
 
 def column_kernel(
     turn_ref, w_ref, early_0, early_1, early_2, early_3, late_ref, table_ref, base_ref, change_ref,
-    own_ref, sent_1, sent_2, sent_3, rows,
+    *refs, blocks,
 ):
     turn = turn_ref[0]
+    *targets, rows = refs
     early = (early_0, early_1, early_2, early_3)
-    targets = (own_ref, sent_1, sent_2, sent_3)
+    height = 32 * len(blocks)
 
     def one(k, carry):
         sky = []
@@ -338,14 +339,14 @@
                     preferred_element_type=F32,
                 )
             )
-        for block, target in enumerate(targets):
+        for place, (block, target) in enumerate(zip(blocks, targets)):
             where = slice(32 * block, 32 * block + 32)
             change = change_ref[k, where].astype(F32)
             image = jnp.zeros((32, 128), F32)
             for step in range(4):
                 part = sky[step // 2][:, 128 * (step % 2) : 128 * (step % 2) + 128]
-                real = part[:128][where]
-                imag = part[128:][where]
+                real = part[32 * place : 32 * place + 32]
+                imag = part[height + 32 * place : height + 32 * place + 32]
                 angle = (2.0 * math.pi * w_ref[step]) * change
                 square = angle * angle
                 sine = angle * (1.0 - square * (1.0 / 6.0))
@@ -362,19 +363,21 @@
         lax.fori_loop(8 * half, 8 * half + 8, one, 0, unroll=4)
 
 
-def column_transform(turn, w, early, late, table, base, change):
+def column_transform(turn, w, early, late, table, base, change, blocks):
+    table = table[:, 32 * blocks[0] : 32 * blocks[-1] + 32].reshape(64 * len(blocks), 512)
     smem = pl.BlockSpec(memory_space=pltpu.SMEM)
     vmem = pl.BlockSpec(memory_space=pltpu.VMEM)
     return pl.pallas_call(
-        column_kernel,
+        functools.partial(column_kernel, blocks=blocks),
         in_specs=[smem] * 2 + [vmem] * 8,
-        out_specs=[vmem] * 4,
-        out_shape=[jax.ShapeDtypeStruct((16, 32, 128), F32)]
-        + [jax.ShapeDtypeStruct((16, 32, 128), BF16)] * 3,
+        out_specs=[vmem] * len(blocks),
+        out_shape=[
+            jax.ShapeDtypeStruct((16, 32, 128), BF16 if block else F32) for block in blocks
+        ],
         scratch_shapes=[pltpu.VMEM((4, 16, 128, 128), BF16)],
         compiler_params=pltpu.CompilerParams(vmem_limit_bytes=16 * MIB),
         cost_estimate=pl.CostEstimate(
-            flops=4_300_000_000, bytes_accessed=5 << 20, transcendentals=0
+            flops=1_080_000_000 * len(blocks), bytes_accessed=5 << 20, transcendentals=0
         ),
         name="column_transform",
     )(turn, w, *early, late, table, base, change)
@@ -458,10 +461,10 @@
     dealt = deal_rows(turn, early)
     dealt = [dealt[0]] + [along_wp(dealt[step], step) for step in (1, 2, 3)]
     table = jnp.roll(jnp.asarray(column_second_table()).reshape(2, 128, 512), -32 * turn[0], axis=1)
-    own, *sent = column_transform(
-        turn, w, dealt, late, table.reshape(256, 512), base, change
-    )
-    blocks = [own] + [along_wp(block, step + 1) for step, block in enumerate(sent)]
+    operands = (turn, w, dealt, late, table, base, change)
+    sent = column_transform(*operands, (1, 2, 3))
+    blocks = [along_wp(block, step + 1) for step, block in enumerate(sent)]
+    blocks = [*column_transform(*operands, (0,)), *blocks]
     return place_rows(turn, blocks).reshape(2048, 128)
 
 

time: 268 us -> 267 us (level)
  waiting for transfers between devices: 122 us -> 116 us
  Pallas kernels: 85.6 us -> 88.9 us
    ppermute x8, waiting for transfers between devices: 8.47 us -> 3.29 us  [along_wp(): return lax.ppermute(block, 'wp', pairs)]
    pallas_call x1 -> x2, Pallas kernels: 6.72 us -> 10.1 us  [column_transform(): pl.pallas_call(functools.partial(column_kernel, blocks=blocks), in_specs=...]
  transfers between devices with their start and end apart: 12 -> 12, of which waited for: 7 -> 7; matrix products, arithmetic and copies ran while one was open for 3% -> 3% of each run, Pallas kernels for 27% -> 29%
where the time goes in v11:
time: 267 us; the launch traced here: 266 us
  waiting for transfers between devices  116 us (43%)
  Pallas kernels  88.9 us (33%)
  starting transfers between devices  49.8 us (19%)
  other arithmetic  5.69 us (2%)
  local copies, waits for them, and re-layouts  3.81 us (1%)
    pallas_call x2, Pallas kernels, grid_and_rows(): pl.pallas_call(grid_kernel, in_specs=[pl.BlockSpec(memory_space=pltpu.SME...  65.7 us
    all_to_all x2, waiting for transfers between devices, local(): lax.all_to_all(packed, 'band', split_axis=0, concat_axis=0, tiled=True)  53.2 us
    all_to_all x1, waiting for transfers between devices, local(): lax.all_to_all(spectrum.reshape(256, 32, 128), ('wp', 'band'), split_axis...  44 us
    all_to_all x2, starting transfers between devices, local(): lax.all_to_all(packed, 'band', split_axis=0, concat_axis=0, tiled=True)  19.4 us
    all_to_all x1, waiting for transfers between devices, local(): lax.all_to_all(spectrum.reshape(64, 128, 128), 'band', split_axis=0, conc...  16 us
    ppermute x8, starting transfers between devices, along_wp(): return lax.ppermute(block, 'wp', pairs)  12.2 us
    all_to_all x1, starting transfers between devices, local(): lax.all_to_all(spectrum.reshape(256, 32, 128), ('wp', 'band'), split_axis...  10.9 us
    pallas_call x2, Pallas kernels, column_transform(): pl.pallas_call(functools.partial(column_kernel, blocks=blocks), in_specs=...  10.1 us
  transfers between devices with their start and end apart: 12, of which 7 were waited for; matrix products, arithmetic and copies ran while one was open for 3% of the time, Pallas kernels for 29%

profile of v11, /device:TPU:33, one launch (start us, length us, event | category | flops | bytes accessed | tf_op | source)
XLA Modules:
  0.0 266.3 jit_solution(10513337506171199019)
XLA Ops:
  0.7 4.4 %pack_rows.2 = bf16[64,136,128]{2,1,0:T(8,128)(2,1)} custom-call(s32[1,1]{1,0:T(1,128)S(6)} %copy.19.count_ref, s32[1,64]{1,0:T(1,128)} %bitcast.38, s32[2,64]{1,0:T(2,128)} %bitcast.36, bf16[64,2,128,128]{3,2,1,0:T(8,128)(2,1)} %bitcast.28), custom_call_target="tpu_custom_call" | custom-call | flops 8388608 | bytes 4194304 | tf_op jit(solution)/shard_map/pack_rows/pallas_call | solution.py:135
  5.0 12.1 %all-to-all-start = ((bf16[64,136,128]{2,1,0:T(8,128)(2,1)}), bf16[64,136,128]{2,1,0:T(8,128)(2,1)}, u32[]{:S(2)}, u32[]{:S(2)}) async-start(bf16[64,136,128]{2,1,0:T(8,128)(2,1)} %pack_rows.2), calls=%async_computation | async-start | bytes 4456448 | tf_op jit(solution)/shard_map/all_to_all | solution.py:437
  17.1 1.4 collective-permute-start
  18.5 0.2 fusion.22
  18.7 0.1 maximum_bitcast_fusion
  18.8 0.1 copy.15
  18.8 4.3 %pack_rows.3 = bf16[64,128,128]{2,1,0:T(8,128)(2,1)} custom-call(s32[1,1]{1,0:T(1,128)S(6)} %copy.19.count_ref, s32[1,64]{1,0:T(1,128)} %bitcast.39, s32[2,64]{1,0:T(2,128)} %bitcast.37, bf16[64,2,128,128]{3,2,1,0:T(8,128)(2,1)} %bitcast.29), custom_call_target="tpu_custom_call" | custom-call | flops 8388608 | bytes 4194304 | tf_op jit(solution)/shard_map/pack_rows/pallas_call | solution.py:135
  23.2 46.6 %all-to-all-done.arrived_ref = bf16[64,136,128]{2,1,0:T(8,128)(2,1)} async-done(((bf16[64,136,128]{2,1,0:T(8,128)(2,1)}), bf16[64,136,128]{2,1,0:T(8,128)(2,1)}, u32[]{:S(2)}, u32[]{:S(2)}) %all-to-all-start) | async-done | bytes 2228256 | tf_op jit(solution)/shard_map/all_to_all | solution.py:437
  69.8 7.3 %all-to-all-start.2 = ((bf16[64,128,128]{2,1,0:T(8,128)(2,1)}), bf16[64,128,128]{2,1,0:T(8,128)(2,1)}, u32[]{:S(2)}, u32[]{:S(2)}) async-start(bf16[64,128,128]{2,1,0:T(8,128)(2,1)} %pack_rows.3), calls=%async_computation.2 | async-start | bytes 4194304 | tf_op jit(solution)/shard_map/all_to_all | solution.py:437
  77.8 0.6 pad_maximum_fusion.2.bands_ref
  78.4 0.4 sqrt_add_fusion
  78.9 0.5 subtract_convert_fusion.change_ref
  79.4 0.0 collective-permute-done
  79.4 0.6 pad_maximum_fusion.7
  80.0 2.9 %collective-permute-start.1 = (f32[2]{0:T(128)S(1)}, f32[2]{0:T(128)S(1)}, u32[]{:S(2)}, u32[]{:S(2)}) collective-permute-start(f32[2]{0:T(128)S(1)} %pad_maximum_fusion.7), channel_id=1, source_target_pairs={{0,2},{1,3},{2,0},{3,1},{4,6},{5,7},{6,4},{7,5},{8,10},{9,11},{10,... | collective-permute-start | bytes 32 | tf_op jit(solution)/shard_map/ppermute | solution.py:410
  82.9 1.4 collective-permute-done.1
  84.3 0.6 broadcast_multiply_fusion
  85.0 1.0 multiply_cosine_fusion
  86.0 0.9 slice.29
  87.0 0.6 fusion.10.place_ref
  87.6 32.9 %place_and_transform.2 = bf16[1,64,128,128]{3,2,1,0:T(8,128)(2,1)} custom-call(s32[64,64]{1,0:T(8,128)} %fusion.10.place_ref, bf16[64,136,128]{2,1,0:T(8,128)(2,1)} %all-to-all-done.arrived_ref, bf16[128,384]{1,0:T(8,128)(2,1)} %constant.98.clone.first_ref, f32[2,128,128]{2,1,0:T(8,128)} %constant.99.clone.twiddle_ref, ...), custom_call_target="tpu_custom_call" | custom-call | flops 20000000000 | bytes 4194304 | tf_op jit(solution)/shard_map/place_and_transform/pallas_call | solution.py:255
  120.4 6.5 %all-to-all-done.2.arrived_ref = bf16[64,128,128]{2,1,0:T(8,128)(2,1)} async-done(((bf16[64,128,128]{2,1,0:T(8,128)(2,1)}), bf16[64,128,128]{2,1,0:T(8,128)(2,1)}, u32[]{:S(2)}, u32[]{:S(2)}) %all-to-all-start.2) | async-done | bytes 2097184 | tf_op jit(solution)/shard_map/all_to_all | solution.py:437
  127.0 7.3 %all-to-all-start.1 = ((bf16[64,128,128]{2,1,0:T(8,128)(2,1)}), bf16[64,128,128]{2,1,0:T(8,128)(2,1)}, u32[]{:S(2)}, u32[]{:S(2)}) async-start(bf16[64,128,128]{2,1,0:T(8,128)(2,1)} %bitcast.31), calls=%async_computation.1 | async-start | bytes 4194304 | tf_op jit(solution)/shard_map/all_to_all | solution.py:453
  134.3 0.1 fusion.23
  134.5 0.1 pad_maximum_fusion.5
  134.5 0.1 pad_maximum_fusion.3
  134.6 0.6 pad_maximum_fusion.4.bands_ref
  135.3 32.8 %place_and_transform.3 = bf16[4,64,32,128]{3,2,1,0:T(8,128)(2,1)} custom-call(s32[64,64]{1,0:T(8,128)} %fusion.10.place_ref, bf16[64,128,128]{2,1,0:T(8,128)(2,1)} %all-to-all-done.2.arrived_ref, bf16[128,384]{1,0:T(8,128)(2,1)} %constant.98.clone.first_ref, f32[2,128,128]{2,1,0:T(8,128)} %constant.99.clone.twiddle_ref, ...), custom_call_target="tpu_custom_call" | custom-call | flops 20000000000 | bytes 4194304 | tf_op jit(solution)/shard_map/place_and_transform/pallas_call | solution.py:255
  168.1 16.0 %all-to-all-done.1.columns_ref = bf16[64,128,128]{2,1,0:T(8,128)(2,1)} async-done(((bf16[64,128,128]{2,1,0:T(8,128)(2,1)}), bf16[64,128,128]{2,1,0:T(8,128)(2,1)}, u32[]{:S(2)}, u32[]{:S(2)}) %all-to-all-start.1) | async-done | bytes 2097184 | tf_op jit(solution)/shard_map/all_to_all | solution.py:453
  184.1 10.9 %all-to-all-start.3 = ((bf16[256,32,128]{2,1,0:T(8,128)(2,1)}), bf16[256,32,128]{2,1,0:T(8,128)(2,1)}, u32[]{:S(2)}, u32[]{:S(2)}) async-start(bf16[256,32,128]{2,1,0:T(8,128)(2,1)} %bitcast.30), calls=%async_computation.3 | async-start | bytes 4194304 | tf_op jit(solution)/shard_map/all_to_all | solution.py:457
  195.1 3.3 %deal_rows.1 = (bf16[16,128,128]{2,1,0:T(8,128)(2,1)}, bf16[16,128,128]{2,1,0:T(8,128)(2,1)}, bf16[16,128,128]{2,1,0:T(8,128)(2,1)}, bf16[16,128,128]{2,1,0:T(8,128)(2,1)}) custom-call(s32[1]{0:T(128)} %bitcast.turn_ref, bf16[64,128,128]{2,1,0:T(8,128)(2,1)} %all-to-all-done.1.columns_ref), custom_call_target="tpu_custom_call" | custom-call | flops 1048576 | bytes 4194304 | tf_op jit(solution)/shard_map/deal_rows/pallas_call | solution.py:293
  198.4 1.3 collective-permute-start.2
  199.7 2.5 collective-permute-start.3
  202.2 1.1 collective-permute-start.4
  203.4 0.9 constant_dynamic-slice_fusion.1
  204.3 44.0 %all-to-all-done.3 = bf16[256,32,128]{2,1,0:T(8,128)(2,1)} async-done(((bf16[256,32,128]{2,1,0:T(8,128)(2,1)}), bf16[256,32,128]{2,1,0:T(8,128)(2,1)}, u32[]{:S(2)}, u32[]{:S(2)}) %all-to-all-start.3) | async-done | bytes 2097184 | tf_op jit(solution)/shard_map/all_to_all | solution.py:457
  248.3 0.0 collective-permute-done.2.early_1
  248.3 0.0 copy-start
  248.3 1.0 copy-done
  249.3 5.8 %column_transform.3 = (bf16[16,32,128]{2,1,0:T(8,128)(2,1)S(1)}, bf16[16,32,128]{2,1,0:T(8,128)(2,1)S(1)}, bf16[16,32,128]{2,1,0:T(8,128)(2,1)S(1)}) custom-call(s32[1]{0:T(128)} %bitcast.turn_ref, f32[4]{0:T(128)S(1)} %get-tuple-element.26.w_ref, bf16[16,128,128]{2,1,0:T(8,128)(2,1)S(1)} %copy-done, ...), custom_call_target="tpu_custom_call" | custom-call | flops 3240000000 | bytes 5242880 | tf_op jit(solution)/shard_map/column_transform/pallas_call | solution.py:370
  255.1 0.4 collective-permute-start.5
  255.6 1.7 collective-permute-start.6
  257.2 0.8 collective-permute-start.7
  258.1 0.8 constant_dynamic-slice_fusion
  258.9 4.3 %column_transform.2.refs_0_ = f32[16,32,128]{2,1,0:T(8,128)S(1)} custom-call(s32[1]{0:T(128)} %bitcast.turn_ref, f32[4]{0:T(128)S(1)} %get-tuple-element.26.w_ref, bf16[16,128,128]{2,1,0:T(8,128)(2,1)S(1)} %copy-done, bf16[16,128,128]{2,1,0:T(8,128)(2,1)S(1)} %collective-permute-done.2.early_1, bf16[16,128,128]{2,1,0:T(8,128)(2,1)S(1)} %collective-permute-done.3.early_2, ...), custom_call_target="tpu_custom_call" | custom-call | flops 1080000000 | bytes 5242880 | tf_op jit(solution)/shard_map/column_transform/pallas_call | solution.py:370
  263.2 0.8 collective-permute-done.5.refs_1_
  264.1 1.1 collective-permute-done.7.refs_3_
  265.1 1.2 place_image_rows.1
  (14 shorter events, 0.1 us)
Async XLA Ops:
  5.0 64.8 %all-to-all-start = ((bf16[64,136,128]{2,1,0:T(8,128)(2,1)}), bf16[64,136,128]{2,1,0:T(8,128)(2,1)}, u32[]{:S(2)}, u32[]{:S(2)}) async-start(bf16[64,136,128]{2,1,0:T(8,128)(2,1)} %pack_rows.2), calls=%async_computation | async-start | bytes 4456448 | tf_op jit(solution)/shard_map/all_to_all | solution.py:437
  17.1 62.2 %collective-permute-start = (f32[1]{0:T(128)}, f32[1]{0:T(128)}, u32[]{:S(2)}, u32[]{:S(2)}) collective-permute-start(f32[1]{0:T(128)} %param.13), channel_id=1, source_target_pairs={{0,1},{1,2},{2,3},{3,0},{4,5},{5,6},{6,7},{7,4},{8,9},{9,10},{10,1... | collective-permute-start | bytes 20 | tf_op jit(solution)/shard_map/ppermute | solution.py:410
  69.8 57.2 %all-to-all-start.2 = ((bf16[64,128,128]{2,1,0:T(8,128)(2,1)}), bf16[64,128,128]{2,1,0:T(8,128)(2,1)}, u32[]{:S(2)}, u32[]{:S(2)}) async-start(bf16[64,128,128]{2,1,0:T(8,128)(2,1)} %pack_rows.3), calls=%async_computation.2 | async-start | bytes 4194304 | tf_op jit(solution)/shard_map/all_to_all | solution.py:437
  80.0 4.3 %collective-permute-start.1 = (f32[2]{0:T(128)S(1)}, f32[2]{0:T(128)S(1)}, u32[]{:S(2)}, u32[]{:S(2)}) collective-permute-start(f32[2]{0:T(128)S(1)} %pad_maximum_fusion.7), channel_id=1, source_target_pairs={{0,2},{1,3},{2,0},{3,1},{4,6},{5,7},{6,4},{7,5},{8,10},{9,11},{10,... | collective-permute-start | bytes 32 | tf_op jit(solution)/shard_map/ppermute | solution.py:410
  127.0 57.2 %all-to-all-start.1 = ((bf16[64,128,128]{2,1,0:T(8,128)(2,1)}), bf16[64,128,128]{2,1,0:T(8,128)(2,1)}, u32[]{:S(2)}, u32[]{:S(2)}) async-start(bf16[64,128,128]{2,1,0:T(8,128)(2,1)} %bitcast.31), calls=%async_computation.1 | async-start | bytes 4194304 | tf_op jit(solution)/shard_map/all_to_all | solution.py:453
  184.1 64.1 %all-to-all-start.3 = ((bf16[256,32,128]{2,1,0:T(8,128)(2,1)}), bf16[256,32,128]{2,1,0:T(8,128)(2,1)}, u32[]{:S(2)}, u32[]{:S(2)}) async-start(bf16[256,32,128]{2,1,0:T(8,128)(2,1)} %bitcast.30), calls=%async_computation.3 | async-start | bytes 4194304 | tf_op jit(solution)/shard_map/all_to_all | solution.py:457
  198.4 49.9 %collective-permute-start.2 = (bf16[16,128,128]{2,1,0:T(8,128)(2,1)}, bf16[16,128,128]{2,1,0:T(8,128)(2,1)S(1)}, u32[]{:S(2)}, u32[]{:S(2)}) collective-permute-start(bf16[16,128,128]{2,1,0:T(8,128)(2,1)} %get-tuple-element.17), channel_id=1, source_target_pairs={{0,1},{1,2},{2,3},{3,0},{4,5},{5,6},{6,7},{7,4},{8,9},{9,10},{10,1... | collective-permute-start | bytes 1572872 | tf_op jit(solution)/shard_map/ppermute | solution.py:410
  199.7 48.6 %collective-permute-start.3 = (bf16[16,128,128]{2,1,0:T(8,128)(2,1)}, bf16[16,128,128]{2,1,0:T(8,128)(2,1)S(1)}, u32[]{:S(2)}, u32[]{:S(2)}) collective-permute-start(bf16[16,128,128]{2,1,0:T(8,128)(2,1)} %get-tuple-element.18), channel_id=1, source_target_pairs={{0,2},{1,3},{2,0},{3,1},{4,6},{5,7},{6,4},{7,5},{8,10},{9,11},{10,... | collective-permute-start | bytes 1572872 | tf_op jit(solution)/shard_map/ppermute | solution.py:410
  202.2 46.0 %collective-permute-start.4 = (bf16[16,128,128]{2,1,0:T(8,128)(2,1)}, bf16[16,128,128]{2,1,0:T(8,128)(2,1)S(1)}, u32[]{:S(2)}, u32[]{:S(2)}) collective-permute-start(bf16[16,128,128]{2,1,0:T(8,128)(2,1)} %get-tuple-element.19), channel_id=1, source_target_pairs={{0,3},{1,0},{2,1},{3,2},{4,7},{5,4},{6,5},{7,6},{8,11},{9,8},{10,9... | collective-permute-start | bytes 1572872 | tf_op jit(solution)/shard_map/ppermute | solution.py:410
  248.3 1.0 copy-start
  255.1 8.9 %collective-permute-start.5 = (bf16[16,32,128]{2,1,0:T(8,128)(2,1)S(1)}, bf16[16,32,128]{2,1,0:T(8,128)(2,1)S(1)}, u32[]{:S(2)}, u32[]{:S(2)}) collective-permute-start(bf16[16,32,128]{2,1,0:T(8,128)(2,1)S(1)} %get-tuple-element.22), channel_id=1, source_target_pairs={{0,1},{1,2},{2,3},{3,0},{4,5},{5,6},{6,7},{7,4},{8,9},{9,10},{10,1... | collective-permute-start | bytes 393224 | tf_op jit(solution)/shard_map/ppermute | solution.py:410
  255.6 8.5 %collective-permute-start.6 = (bf16[16,32,128]{2,1,0:T(8,128)(2,1)S(1)}, bf16[16,32,128]{2,1,0:T(8,128)(2,1)S(1)}, u32[]{:S(2)}, u32[]{:S(2)}) collective-permute-start(bf16[16,32,128]{2,1,0:T(8,128)(2,1)S(1)} %get-tuple-element.23), channel_id=1, source_target_pairs={{0,2},{1,3},{2,0},{3,1},{4,6},{5,7},{6,4},{7,5},{8,10},{9,11},{10,... | collective-permute-start | bytes 393224 | tf_op jit(solution)/shard_map/ppermute | solution.py:410
  257.2 7.9 %collective-permute-start.7 = (bf16[16,32,128]{2,1,0:T(8,128)(2,1)S(1)}, bf16[16,32,128]{2,1,0:T(8,128)(2,1)S(1)}, u32[]{:S(2)}, u32[]{:S(2)}) collective-permute-start(bf16[16,32,128]{2,1,0:T(8,128)(2,1)S(1)} %get-tuple-element.24), channel_id=1, source_target_pairs={{0,3},{1,0},{2,1},{3,2},{4,7},{5,4},{6,5},{7,6},{8,11},{9,8},{10,9... | collective-permute-start | bytes 393224 | tf_op jit(solution)/shard_map/ppermute | solution.py:410

commit v12 on v11

--- a/solution.py
+++ b/solution.py
@@ -375,7 +375,7 @@
             jax.ShapeDtypeStruct((16, 32, 128), BF16 if block else F32) for block in blocks
         ],
         scratch_shapes=[pltpu.VMEM((4, 16, 128, 128), BF16)],
-        compiler_params=pltpu.CompilerParams(vmem_limit_bytes=16 * MIB),
+        compiler_params=pltpu.CompilerParams(vmem_limit_bytes=58 * MIB),
         cost_estimate=pl.CostEstimate(
             flops=1_080_000_000 * len(blocks), bytes_accessed=5 << 20, transcendentals=0
         ),

time: 267 us -> 270 us (1.011)
  waiting for transfers between devices: 116 us -> 113 us
  Pallas kernels: 88.9 us -> 91.7 us
    pallas_call x2, Pallas kernels: 10.1 us -> 12.9 us  [column_transform(): pl.pallas_call(functools.partial(column_kernel, blocks=blocks), in_specs=...]
  transfers between devices with their start and end apart: 12 -> 12, of which waited for: 7 -> 6; matrix products, arithmetic and copies ran while one was open for 3% -> 4% of each run, Pallas kernels for 29% -> 29%
where the time goes in v12:
time: 270 us; the launch traced here: 269 us
  waiting for transfers between devices  113 us (42%)
  Pallas kernels  91.7 us (34%)
  starting transfers between devices  49.7 us (18%)
  other arithmetic  8 us (3%)
  local copies, waits for them, and re-layouts  4.36 us (2%)
    pallas_call x2, Pallas kernels, grid_and_rows(): pl.pallas_call(grid_kernel, in_specs=[pl.BlockSpec(memory_space=pltpu.SME...  65.7 us
    all_to_all x2, waiting for transfers between devices, local(): lax.all_to_all(packed, 'band', split_axis=0, concat_axis=0, tiled=True)  50.9 us
    all_to_all x1, waiting for transfers between devices, local(): lax.all_to_all(spectrum.reshape(256, 32, 128), ('wp', 'band'), split_axis...  44.2 us
    all_to_all x2, starting transfers between devices, local(): lax.all_to_all(packed, 'band', split_axis=0, concat_axis=0, tiled=True)  19.4 us
    all_to_all x1, waiting for transfers between devices, local(): lax.all_to_all(spectrum.reshape(64, 128, 128), 'band', split_axis=0, conc...  16 us
    pallas_call x2, Pallas kernels, column_transform(): pl.pallas_call(functools.partial(column_kernel, blocks=blocks), in_specs=...  12.9 us
    ppermute x8, starting transfers between devices, along_wp(): return lax.ppermute(block, 'wp', pairs)  12.1 us
    all_to_all x1, starting transfers between devices, local(): lax.all_to_all(spectrum.reshape(256, 32, 128), ('wp', 'band'), split_axis...  10.9 us
  transfers between devices with their start and end apart: 12, of which 6 were waited for; matrix products, arithmetic and copies ran while one was open for 4% of the time, Pallas kernels for 29%

profile of v12, /device:TPU:33, one launch (start us, length us, event | category | flops | bytes accessed | tf_op | source)
XLA Modules:
  0.0 268.6 jit_solution(16172457143983193263)
XLA Ops:
  0.7 4.3 %pack_rows.2 = bf16[64,136,128]{2,1,0:T(8,128)(2,1)} custom-call(s32[1,1]{1,0:T(1,128)S(6)} %copy.19.count_ref, s32[1,64]{1,0:T(1,128)} %bitcast.38, s32[2,64]{1,0:T(2,128)} %bitcast.36, bf16[64,2,128,128]{3,2,1,0:T(8,128)(2,1)} %bitcast.26), custom_call_target="tpu_custom_call" | custom-call | flops 8388608 | bytes 4194304 | tf_op jit(solution)/shard_map/pack_rows/pallas_call | solution.py:135
  5.0 12.1 %all-to-all-start = ((bf16[64,136,128]{2,1,0:T(8,128)(2,1)}), bf16[64,136,128]{2,1,0:T(8,128)(2,1)}, u32[]{:S(2)}, u32[]{:S(2)}) async-start(bf16[64,136,128]{2,1,0:T(8,128)(2,1)} %pack_rows.2), calls=%async_computation | async-start | bytes 4456448 | tf_op jit(solution)/shard_map/all_to_all | solution.py:437
  17.1 1.4 collective-permute-start
  18.4 0.2 fusion.22
  18.6 0.1 maximum_bitcast_fusion
  18.7 0.1 copy.15
  18.8 4.3 %pack_rows.3 = bf16[64,128,128]{2,1,0:T(8,128)(2,1)} custom-call(s32[1,1]{1,0:T(1,128)S(6)} %copy.19.count_ref, s32[1,64]{1,0:T(1,128)} %bitcast.39, s32[2,64]{1,0:T(2,128)} %bitcast.37, bf16[64,2,128,128]{3,2,1,0:T(8,128)(2,1)} %bitcast.27), custom_call_target="tpu_custom_call" | custom-call | flops 8388608 | bytes 4194304 | tf_op jit(solution)/shard_map/pack_rows/pallas_call | solution.py:135
  23.1 46.6 %all-to-all-done.arrived_ref = bf16[64,136,128]{2,1,0:T(8,128)(2,1)} async-done(((bf16[64,136,128]{2,1,0:T(8,128)(2,1)}), bf16[64,136,128]{2,1,0:T(8,128)(2,1)}, u32[]{:S(2)}, u32[]{:S(2)}) %all-to-all-start) | async-done | bytes 2228256 | tf_op jit(solution)/shard_map/all_to_all | solution.py:437
  69.7 7.3 %all-to-all-start.2 = ((bf16[64,128,128]{2,1,0:T(8,128)(2,1)}), bf16[64,128,128]{2,1,0:T(8,128)(2,1)}, u32[]{:S(2)}, u32[]{:S(2)}) async-start(bf16[64,128,128]{2,1,0:T(8,128)(2,1)} %pack_rows.3), calls=%async_computation.2 | async-start | bytes 4194304 | tf_op jit(solution)/shard_map/all_to_all | solution.py:437
  77.7 0.6 pad_maximum_fusion.2.bands_ref
  78.4 0.4 sqrt_add_fusion
  78.8 1.3 subtract_convert_fusion.change_ref
  80.1 0.7 pad_maximum_fusion.7
  80.8 2.9 %collective-permute-start.1 = (f32[2]{0:T(128)S(1)}, f32[2]{0:T(128)S(1)}, u32[]{:S(2)}, u32[]{:S(2)}) collective-permute-start(f32[2]{0:T(128)S(1)} %pad_maximum_fusion.7), channel_id=1, source_target_pairs={{0,2},{1,3},{2,0},{3,1},{4,6},{5,7},{6,4},{7,5},{8,10},{9,11},{10,... | collective-permute-start | bytes 32 | tf_op jit(solution)/shard_map/ppermute | solution.py:410
  83.7 1.4 collective-permute-done.1
  85.1 1.3 broadcast_multiply_fusion
  86.4 1.0 multiply_cosine_fusion
  87.4 0.8 pad_maximum_fusion.base_ref
  88.2 0.9 slice.29
  89.2 0.6 fusion.10.place_ref
  89.8 32.9 %place_and_transform.2 = bf16[1,64,128,128]{3,2,1,0:T(8,128)(2,1)} custom-call(s32[64,64]{1,0:T(8,128)} %fusion.10.place_ref, bf16[64,136,128]{2,1,0:T(8,128)(2,1)} %all-to-all-done.arrived_ref, bf16[128,384]{1,0:T(8,128)(2,1)} %constant.98.clone.first_ref, f32[2,128,128]{2,1,0:T(8,128)} %constant.99.clone.twiddle_ref, ...), custom_call_target="tpu_custom_call" | custom-call | flops 20000000000 | bytes 4194304 | tf_op jit(solution)/shard_map/place_and_transform/pallas_call | solution.py:255
  122.6 4.2 %all-to-all-done.2.arrived_ref = bf16[64,128,128]{2,1,0:T(8,128)(2,1)} async-done(((bf16[64,128,128]{2,1,0:T(8,128)(2,1)}), bf16[64,128,128]{2,1,0:T(8,128)(2,1)}, u32[]{:S(2)}, u32[]{:S(2)}) %all-to-all-start.2) | async-done | bytes 2097184 | tf_op jit(solution)/shard_map/all_to_all | solution.py:437
  126.9 7.3 %all-to-all-start.1 = ((bf16[64,128,128]{2,1,0:T(8,128)(2,1)}), bf16[64,128,128]{2,1,0:T(8,128)(2,1)}, u32[]{:S(2)}, u32[]{:S(2)}) async-start(bf16[64,128,128]{2,1,0:T(8,128)(2,1)} %bitcast.29), calls=%async_computation.1 | async-start | bytes 4194304 | tf_op jit(solution)/shard_map/all_to_all | solution.py:453
  134.2 0.1 fusion.23
  134.4 0.1 pad_maximum_fusion.5
  134.5 0.1 pad_maximum_fusion.3
  134.6 0.6 pad_maximum_fusion.4.bands_ref
  135.2 32.8 %place_and_transform.3 = bf16[4,64,32,128]{3,2,1,0:T(8,128)(2,1)} custom-call(s32[64,64]{1,0:T(8,128)} %fusion.10.place_ref, bf16[64,128,128]{2,1,0:T(8,128)(2,1)} %all-to-all-done.2.arrived_ref, bf16[128,384]{1,0:T(8,128)(2,1)} %constant.98.clone.first_ref, f32[2,128,128]{2,1,0:T(8,128)} %constant.99.clone.twiddle_ref, ...), custom_call_target="tpu_custom_call" | custom-call | flops 20000000000 | bytes 4194304 | tf_op jit(solution)/shard_map/place_and_transform/pallas_call | solution.py:255
  168.0 16.0 %all-to-all-done.1.columns_ref = bf16[64,128,128]{2,1,0:T(8,128)(2,1)} async-done(((bf16[64,128,128]{2,1,0:T(8,128)(2,1)}), bf16[64,128,128]{2,1,0:T(8,128)(2,1)}, u32[]{:S(2)}, u32[]{:S(2)}) %all-to-all-start.1) | async-done | bytes 2097184 | tf_op jit(solution)/shard_map/all_to_all | solution.py:453
  184.1 10.9 %all-to-all-start.3 = ((bf16[256,32,128]{2,1,0:T(8,128)(2,1)}), bf16[256,32,128]{2,1,0:T(8,128)(2,1)}, u32[]{:S(2)}, u32[]{:S(2)}) async-start(bf16[256,32,128]{2,1,0:T(8,128)(2,1)} %bitcast.28), calls=%async_computation.3 | async-start | bytes 4194304 | tf_op jit(solution)/shard_map/all_to_all | solution.py:457
  195.0 3.3 %deal_rows.1 = (bf16[16,128,128]{2,1,0:T(8,128)(2,1)}, bf16[16,128,128]{2,1,0:T(8,128)(2,1)}, bf16[16,128,128]{2,1,0:T(8,128)(2,1)}, bf16[16,128,128]{2,1,0:T(8,128)(2,1)}) custom-call(s32[1]{0:T(128)} %bitcast.turn_ref, bf16[64,128,128]{2,1,0:T(8,128)(2,1)} %all-to-all-done.1.columns_ref), custom_call_target="tpu_custom_call" | custom-call | flops 1048576 | bytes 4194304 | tf_op jit(solution)/shard_map/deal_rows/pallas_call | solution.py:293
  198.4 1.3 collective-permute-start.2
  199.7 2.5 collective-permute-start.3
  202.2 1.1 collective-permute-start.4
  203.3 0.7 constant_dynamic-slice_fusion.1
  204.0 44.2 %all-to-all-done.3 = bf16[256,32,128]{2,1,0:T(8,128)(2,1)} async-done(((bf16[256,32,128]{2,1,0:T(8,128)(2,1)}), bf16[256,32,128]{2,1,0:T(8,128)(2,1)}, u32[]{:S(2)}, u32[]{:S(2)}) %all-to-all-start.3) | async-done | bytes 2097184 | tf_op jit(solution)/shard_map/all_to_all | solution.py:457
  248.2 0.8 copy-done.1
  249.0 0.2 copy-done.2
  249.2 0.2 copy-done.3
  249.3 7.0 %column_transform.3 = (bf16[16,32,128]{2,1,0:T(8,128)(2,1)}, bf16[16,32,128]{2,1,0:T(8,128)(2,1)}, bf16[16,32,128]{2,1,0:T(8,128)(2,1)}) custom-call(s32[1]{0:T(128)} %bitcast.turn_ref, f32[4]{0:T(128)} %get-tuple-element.26.w_ref, bf16[16,128,128]{2,1,0:T(8,128)(2,1)} %get-tuple-element.16.early_0, bf16[16,128,128]{2,1,0:T(8,128)(2,1)} %copy-done.1, ...), custom_call_target="tpu_custom_call" | custom-call | flops 3240000000 | bytes 5242880 | tf_op jit(solution)/shard_map/column_transform/pallas_call | solution.py:370
  256.4 0.3 collective-permute-start.5
  256.7 1.7 collective-permute-start.6
  258.4 0.8 collective-permute-start.7
  259.2 0.6 constant_dynamic-slice_fusion
  259.8 5.8 %column_transform.2.refs_0_ = f32[16,32,128]{2,1,0:T(8,128)} custom-call(s32[1]{0:T(128)} %bitcast.turn_ref, f32[4]{0:T(128)} %get-tuple-element.26.w_ref, bf16[16,128,128]{2,1,0:T(8,128)(2,1)} %get-tuple-element.16.early_0, bf16[16,128,128]{2,1,0:T(8,128)(2,1)} %copy-done.1, bf16[16,128,128]{2,1,0:T(8,128)(2,1)} %copy-done.2, ...), custom_call_target="tpu_custom_call" | custom-call | flops 1080000000 | bytes 5242880 | tf_op jit(solution)/shard_map/column_transform/pallas_call | solution.py:370
  265.6 0.8 collective-permute-done.7.refs_3_
  266.5 0.9 copy-done
  267.4 1.2 place_image_rows.1
  (22 shorter events, 0.1 us)
Async XLA Ops:
  5.0 64.8 %all-to-all-start = ((bf16[64,136,128]{2,1,0:T(8,128)(2,1)}), bf16[64,136,128]{2,1,0:T(8,128)(2,1)}, u32[]{:S(2)}, u32[]{:S(2)}) async-start(bf16[64,136,128]{2,1,0:T(8,128)(2,1)} %pack_rows.2), calls=%async_computation | async-start | bytes 4456448 | tf_op jit(solution)/shard_map/all_to_all | solution.py:437
  17.1 63.0 %collective-permute-start = (f32[1]{0:T(128)}, f32[1]{0:T(128)}, u32[]{:S(2)}, u32[]{:S(2)}) collective-permute-start(f32[1]{0:T(128)} %param.13), channel_id=1, source_target_pairs={{0,1},{1,2},{2,3},{3,0},{4,5},{5,6},{6,7},{7,4},{8,9},{9,10},{10,1... | collective-permute-start | bytes 20 | tf_op jit(solution)/shard_map/ppermute | solution.py:410
  69.7 57.2 %all-to-all-start.2 = ((bf16[64,128,128]{2,1,0:T(8,128)(2,1)}), bf16[64,128,128]{2,1,0:T(8,128)(2,1)}, u32[]{:S(2)}, u32[]{:S(2)}) async-start(bf16[64,128,128]{2,1,0:T(8,128)(2,1)} %pack_rows.3), calls=%async_computation.2 | async-start | bytes 4194304 | tf_op jit(solution)/shard_map/all_to_all | solution.py:437
  80.8 4.3 %collective-permute-start.1 = (f32[2]{0:T(128)S(1)}, f32[2]{0:T(128)S(1)}, u32[]{:S(2)}, u32[]{:S(2)}) collective-permute-start(f32[2]{0:T(128)S(1)} %pad_maximum_fusion.7), channel_id=1, source_target_pairs={{0,2},{1,3},{2,0},{3,1},{4,6},{5,7},{6,4},{7,5},{8,10},{9,11},{10,... | collective-permute-start | bytes 32 | tf_op jit(solution)/shard_map/ppermute | solution.py:410
  126.9 57.2 %all-to-all-start.1 = ((bf16[64,128,128]{2,1,0:T(8,128)(2,1)}), bf16[64,128,128]{2,1,0:T(8,128)(2,1)}, u32[]{:S(2)}, u32[]{:S(2)}) async-start(bf16[64,128,128]{2,1,0:T(8,128)(2,1)} %bitcast.29), calls=%async_computation.1 | async-start | bytes 4194304 | tf_op jit(solution)/shard_map/all_to_all | solution.py:453
  184.1 64.1 %all-to-all-start.3 = ((bf16[256,32,128]{2,1,0:T(8,128)(2,1)}), bf16[256,32,128]{2,1,0:T(8,128)(2,1)}, u32[]{:S(2)}, u32[]{:S(2)}) async-start(bf16[256,32,128]{2,1,0:T(8,128)(2,1)} %bitcast.28), calls=%async_computation.3 | async-start | bytes 4194304 | tf_op jit(solution)/shard_map/all_to_all | solution.py:457
  195.0 8.3 %copy-start.4 = (bf16[2,256,512]{2,1,0:T(8,128)(2,1)S(1)}, bf16[2,256,512]{2,1,0:T(8,128)(2,1)}, u32[]{:S(2)}) copy-start(bf16[2,256,512]{2,1,0:T(8,128)(2,1)} %constant.108) | copy-start | bytes 1572868
  198.4 49.8 %collective-permute-start.2 = (bf16[16,128,128]{2,1,0:T(8,128)(2,1)}, bf16[16,128,128]{2,1,0:T(8,128)(2,1)S(1)}, u32[]{:S(2)}, u32[]{:S(2)}) collective-permute-start(bf16[16,128,128]{2,1,0:T(8,128)(2,1)} %get-tuple-element.17), channel_id=1, source_target_pairs={{0,1},{1,2},{2,3},{3,0},{4,5},{5,6},{6,7},{7,4},{8,9},{9,10},{10,1... | collective-permute-start | bytes 1572872 | tf_op jit(solution)/shard_map/ppermute | solution.py:410
  199.7 48.5 %collective-permute-start.3 = (bf16[16,128,128]{2,1,0:T(8,128)(2,1)}, bf16[16,128,128]{2,1,0:T(8,128)(2,1)S(1)}, u32[]{:S(2)}, u32[]{:S(2)}) collective-permute-start(bf16[16,128,128]{2,1,0:T(8,128)(2,1)} %get-tuple-element.18), channel_id=1, source_target_pairs={{0,2},{1,3},{2,0},{3,1},{4,6},{5,7},{6,4},{7,5},{8,10},{9,11},{10,... | collective-permute-start | bytes 1572872 | tf_op jit(solution)/shard_map/ppermute | solution.py:410
  202.2 46.0 %collective-permute-start.4 = (bf16[16,128,128]{2,1,0:T(8,128)(2,1)}, bf16[16,128,128]{2,1,0:T(8,128)(2,1)S(1)}, u32[]{:S(2)}, u32[]{:S(2)}) collective-permute-start(bf16[16,128,128]{2,1,0:T(8,128)(2,1)} %get-tuple-element.19), channel_id=1, source_target_pairs={{0,3},{1,0},{2,1},{3,2},{4,7},{5,4},{6,5},{7,6},{8,11},{9,8},{10,9... | collective-permute-start | bytes 1572872 | tf_op jit(solution)/shard_map/ppermute | solution.py:410
  248.2 0.8 copy-start.1
  248.2 1.0 copy-start.2
  248.2 1.1 copy-start.3
  256.4 9.3 %collective-permute-start.5 = (bf16[16,32,128]{2,1,0:T(8,128)(2,1)}, bf16[16,32,128]{2,1,0:T(8,128)(2,1)S(1)}, u32[]{:S(2)}, u32[]{:S(2)}) collective-permute-start(bf16[16,32,128]{2,1,0:T(8,128)(2,1)} %get-tuple-element.22), channel_id=1, source_target_pairs={{0,1},{1,2},{2,3},{3,0},{4,5},{5,6},{6,7},{7,4},{8,9},{9,10},{10,1... | collective-permute-start | bytes 393224 | tf_op jit(solution)/shard_map/ppermute | solution.py:410
  256.7 8.9 %collective-permute-start.6 = (bf16[16,32,128]{2,1,0:T(8,128)(2,1)}, bf16[16,32,128]{2,1,0:T(8,128)(2,1)S(1)}, u32[]{:S(2)}, u32[]{:S(2)}) collective-permute-start(bf16[16,32,128]{2,1,0:T(8,128)(2,1)} %get-tuple-element.23), channel_id=1, source_target_pairs={{0,2},{1,3},{2,0},{3,1},{4,6},{5,7},{6,4},{7,5},{8,10},{9,11},{10,... | collective-permute-start | bytes 393224 | tf_op jit(solution)/shard_map/ppermute | solution.py:410
  258.4 8.1 %collective-permute-start.7 = (bf16[16,32,128]{2,1,0:T(8,128)(2,1)}, bf16[16,32,128]{2,1,0:T(8,128)(2,1)S(1)}, u32[]{:S(2)}, u32[]{:S(2)}) collective-permute-start(bf16[16,32,128]{2,1,0:T(8,128)(2,1)} %get-tuple-element.24), channel_id=1, source_target_pairs={{0,3},{1,0},{2,1},{3,2},{4,7},{5,4},{6,5},{7,6},{8,11},{9,8},{10,9... | collective-permute-start | bytes 393224 | tf_op jit(solution)/shard_map/ppermute | solution.py:410
  266.5 1.0 copy-start
